TPU v7x, 32 devices: a whole 2x2x4 slice. The times are simulated.
32 devices in a mesh: fsdp: 8 (over y, x, core), tensor: 4 (over z).
Axes of the slice: x: 2, y: 2, z: 4, core: 2. Of those that a mesh axis runs over, the one named last changes fastest.
Arguments:
- tokens: bfloat16 [2048, 2048], P('fsdp'), may hold values from -6 to 6
- cotangent: bfloat16 [2048, 2048], P('fsdp'), may hold values from -6 to 6
- routes: int32 [2048, 8], P('fsdp'), may hold values from 0 to 63, all different within a row; in each aligned block of 256 rows (0 to 255, 256 to 511, ...) at most 40 rows name the same one
- w_query: bfloat16 [2048, 2048], P('fsdp', 'tensor'), may hold values from -0.125 to 0.125
- w_key: bfloat16 [2048, 2048], P('fsdp', 'tensor'), may hold values from -0.125 to 0.125
- w_value: bfloat16 [2048, 2048], P('fsdp', 'tensor'), may hold values from -0.125 to 0.125
- w_output: bfloat16 [2048, 2048], P('fsdp', 'tensor'), may hold values from -1.25 to 1.25
- w_router: bfloat16 [2048, 64], P('fsdp'), may hold values from -0.0625 to 0.0625
- attn_gain: bfloat16 [2048], P('fsdp'), may hold values from 0.25 to 1.75
- ffn_gain: bfloat16 [2048], P('fsdp'), may hold values from 0.25 to 1.75
- query_gain: bfloat16 [128], P('fsdp'), may hold values from 0.25 to 1.75
- key_gain: bfloat16 [128], P('fsdp'), may hold values from 0.25 to 1.75
- expert_weights: bfloat16 [64, 3, 2048, 1024], P('fsdp', None, None, 'tensor'), may hold values from -4 to 4
Outputs:
- layer_out: bfloat16 [2048, 2048], P('fsdp')
- grad_tokens: bfloat16 [2048, 2048], P('fsdp')
- grad_query: float32 [2048, 2048], P('fsdp', 'tensor')
- grad_key: float32 [2048, 2048], P('fsdp', 'tensor')
- grad_value: float32 [2048, 2048], P('fsdp', 'tensor')
- grad_output: float32 [2048, 2048], P('fsdp', 'tensor')
- grad_router: float32 [2048, 64], P('fsdp')
- grad_attn_gain: float32 [2048], P('fsdp')
- grad_ffn_gain: float32 [2048], P('fsdp')
- grad_query_gain: float32 [128], P('fsdp')
- grad_key_gain: float32 [128], P('fsdp')
- grad_experts: float32 [64, 3, 2048, 1024], P('fsdp', None, None, 'tensor')
Inputs may be any that keep to these rules, and one draw needn't show every extreme that they name: `routes`: each row names 8 different experts. Among the 256 rows of one index of fsdp no expert is named more than 40 times, a bound that some expert reaches in some such block.
All inputs are finite; a program needn't handle non-finite values.
Results may differ from a plain program's by a relative error of at most 0.02.
Values may be sent and summed in bfloat16 or wider, within the bound.
No kernel may reach another device: no remote copies, remote signals or barrier semaphores. Data moves between devices by JAX's collectives and lax.ppermute only.
A program may use at most 320 MiB of HBM per device.

v0:
```python
import jax
import jax.numpy as jnp
from jax import lax
from jax.sharding import PartitionSpec as P

D = 2048
HD = 128
EXPERTS = 64
CAP = 40


EPSILON = 1e-06
ROPE_BASE = 10000.0


def rms_inverse(values):
    return lax.rsqrt(jnp.mean(values * values, axis=-1, keepdims=True) + EPSILON)


def norm_backward(values, inverse, gain, upstream):
    scaled = gain * upstream
    return inverse * scaled - values * inverse**3 * jnp.mean(
        values * scaled, axis=-1, keepdims=True
    )


def rope_tables(length, head_width):
    half_width = head_width // 2
    position = jnp.arange(length, dtype=jnp.float32)[:, None]
    inverse = ROPE_BASE ** (-jnp.arange(half_width, dtype=jnp.float32) / half_width)
    angles = (position * inverse[None, :])[:, None, :]
    return (jnp.cos(angles), jnp.sin(angles))


def rotate(values, cosine, sine_part, direction):
    half_width = values.shape[-1] // 2
    front_half = values[..., :half_width]
    back_half = values[..., half_width:]
    return jnp.concatenate(
        [
            front_half * cosine - direction * back_half * sine_part,
            back_half * cosine + direction * front_half * sine_part,
        ],
        axis=-1,
    )


def slot_tables(route_ids, experts, capacity):
    pair_count = route_ids.shape[0] * route_ids.shape[1]
    chosen = route_ids.reshape(-1)
    onehot = (chosen[:, None] == jnp.arange(experts, dtype=jnp.int32)[None, :]).astype(jnp.int32)
    earlier = jnp.cumsum(onehot, axis=0) - onehot
    places = jnp.sum(earlier * onehot, axis=1)
    slot_ids = chosen * capacity + places
    owners = jnp.full((experts * capacity,), route_ids.shape[0], jnp.int32)
    owners = owners.at[slot_ids].set(jnp.arange(pair_count, dtype=jnp.int32) // route_ids.shape[1])
    return (slot_ids.reshape(route_ids.shape), owners)


def times_transposed(left, right):
    return lax.dot_general(
        left, right, (((1,), (1,)), ((), ())), preferred_element_type=jnp.float32
    )


def transposed_times(left, right):
    return lax.dot_general(
        left, right, (((0,), (0,)), ((), ())), preferred_element_type=jnp.float32
    )


def expert_forward(weights, rows_in):
    gate_pre = jnp.einsum(
        "erd,edf->erf", rows_in, weights[:, 0], preferred_element_type=jnp.float32
    )
    up_pre = jnp.einsum("erd,edf->erf", rows_in, weights[:, 1], preferred_element_type=jnp.float32)
    hidden = (gate_pre * jax.nn.sigmoid(gate_pre) * up_pre).astype(jnp.bfloat16)
    return jnp.einsum("erf,edf->erd", hidden, weights[:, 2], preferred_element_type=jnp.float32)


def expert_backward(weights, rows_in, grad_rows):
    gate_pre = jnp.einsum(
        "erd,edf->erf", rows_in, weights[:, 0], preferred_element_type=jnp.float32
    )
    up_pre = jnp.einsum("erd,edf->erf", rows_in, weights[:, 1], preferred_element_type=jnp.float32)
    sigma_gate = jax.nn.sigmoid(gate_pre)
    swish_gate = gate_pre * sigma_gate
    hidden = (swish_gate * up_pre).astype(jnp.bfloat16)
    grad_hidden = jnp.einsum(
        "erd,edf->erf", grad_rows, weights[:, 2], preferred_element_type=jnp.float32
    )
    grad_gate = (grad_hidden * up_pre * sigma_gate * (1.0 + gate_pre * (1.0 - sigma_gate))).astype(
        jnp.bfloat16
    )
    grad_up = (grad_hidden * swish_gate).astype(jnp.bfloat16)
    grad_input = jnp.einsum(
        "erf,edf->erd", grad_gate, weights[:, 0], preferred_element_type=jnp.float32
    )
    grad_input = grad_input + jnp.einsum(
        "erf,edf->erd", grad_up, weights[:, 1], preferred_element_type=jnp.float32
    )
    return (grad_input, grad_gate, grad_up, hidden)


def expert_weight_grads(rows_in, grad_rows, grad_gate, grad_up, hidden):
    return jnp.stack(
        [
            jnp.einsum("erd,erf->edf", rows_in, grad_gate, preferred_element_type=jnp.float32),
            jnp.einsum("erd,erf->edf", rows_in, grad_up, preferred_element_type=jnp.float32),
            jnp.einsum("erd,erf->edf", grad_rows, hidden, preferred_element_type=jnp.float32),
        ],
        axis=1,
    )


def on_device(
    tokens,
    cotangent,
    routes,
    w_query,
    w_key,
    w_value,
    w_output,
    w_router,
    attn_gain,
    ffn_gain,
    query_gain,
    key_gain,
    expert_weights,
):
    length = tokens.shape[0]
    (
        query_all,
        key_all,
        value_all,
        output_all,
        router_all,
        attn_gain_all,
        ffn_gain_all,
        query_gain_all,
        key_gain_all,
    ) = (
        lax.all_gather(w_query, "fsdp", axis=0, tiled=True),
        lax.all_gather(w_key, "fsdp", axis=0, tiled=True),
        lax.all_gather(w_value, "fsdp", axis=0, tiled=True),
        lax.all_gather(w_output, "fsdp", axis=0, tiled=True),
        lax.all_gather(w_router, "fsdp", axis=0, tiled=True),
        lax.all_gather(attn_gain, "fsdp", axis=0, tiled=True),
        lax.all_gather(ffn_gain, "fsdp", axis=0, tiled=True),
        lax.all_gather(query_gain, "fsdp", axis=0, tiled=True),
        lax.all_gather(key_gain, "fsdp", axis=0, tiled=True),
    )
    attn_gain_f = attn_gain_all.astype(jnp.float32)
    ffn_gain_f = ffn_gain_all.astype(jnp.float32)
    query_gain_f = query_gain_all.astype(jnp.float32)
    key_gain_f = key_gain_all.astype(jnp.float32)
    residual = tokens.astype(jnp.float32)
    inverse_one = rms_inverse(residual)
    normed_one = (residual * inverse_one * attn_gain_f).astype(jnp.bfloat16)
    local_heads = query_all.shape[1] // HD
    query_raw = jnp.dot(normed_one, query_all, preferred_element_type=jnp.float32).reshape(
        length, local_heads, HD
    )
    key_raw = jnp.dot(normed_one, key_all, preferred_element_type=jnp.float32).reshape(
        length, local_heads, HD
    )
    value_low = jnp.dot(normed_one, value_all, preferred_element_type=jnp.float32).astype(
        jnp.bfloat16
    )
    value_low = value_low.reshape(length, local_heads, HD)
    cosine, sine_part = rope_tables(length, HD)
    inverse_query = rms_inverse(query_raw)
    inverse_key = rms_inverse(key_raw)
    query_low = rotate(query_raw * inverse_query * query_gain_f, cosine, sine_part, 1.0).astype(
        jnp.bfloat16
    )
    key_low = rotate(key_raw * inverse_key * key_gain_f, cosine, sine_part, 1.0).astype(
        jnp.bfloat16
    )
    block_rows = min(512, length)
    block_count = length // block_rows
    score_scale = HD ** (-0.5)

    def attend(query_block):
        scores = (
            jnp.einsum("qhd,khd->hqk", query_block, key_low, preferred_element_type=jnp.float32)
            * score_scale
        )
        highest = jnp.max(scores, axis=-1, keepdims=True)
        shifted = jnp.exp(scores - highest)
        row_sums = jnp.sum(shifted, axis=-1, keepdims=True)
        probabilities = (shifted / row_sums).astype(jnp.bfloat16)
        attended = jnp.einsum(
            "hqk,khd->qhd", probabilities, value_low, preferred_element_type=jnp.float32
        )
        return (attended, (highest + jnp.log(row_sums))[..., 0])

    attended, log_totals = lax.map(
        attend, query_low.reshape(block_count, block_rows, local_heads, HD)
    )
    attended_low = attended.reshape(length, local_heads * HD).astype(jnp.bfloat16)
    attn_part = times_transposed(attended_low, output_all)
    after_attn = residual + lax.psum(attn_part, "tensor")
    inverse_two = rms_inverse(after_attn)
    normed_two = (after_attn * inverse_two * ffn_gain_f).astype(jnp.bfloat16)
    logits = jnp.dot(normed_two, router_all, preferred_element_type=jnp.float32)
    chosen = jnp.take_along_axis(logits, routes, axis=1)
    gate_values = jax.nn.softmax(chosen, axis=-1)
    slot_ids, owners = slot_tables(routes, EXPERTS, CAP)
    gate_slots = (
        jnp.zeros((EXPERTS * CAP,), jnp.float32)
        .at[slot_ids.reshape(-1)]
        .set(gate_values.reshape(-1))
    )
    normed_pad = jnp.concatenate([normed_two, jnp.zeros((1, D), jnp.bfloat16)], axis=0)
    cot_pad = jnp.concatenate([cotangent, jnp.zeros((1, D), jnp.bfloat16)], axis=0)
    routed_rows = normed_pad[owners].reshape(EXPERTS, CAP, D)
    owned_rows = lax.all_to_all(routed_rows, "fsdp", split_axis=0, concat_axis=1, tiled=True)
    owned_out = expert_forward(expert_weights, owned_rows)
    returned = lax.all_to_all(owned_out, "fsdp", split_axis=1, concat_axis=0, tiled=True)
    results = returned.reshape(EXPERTS * CAP, D)
    moe_sum = jnp.zeros((length + 1, D), jnp.float32)
    gate_part = gate_slots
    cot_part = cot_pad[owners]
    moe_sum = moe_sum.at[owners].add(results * gate_part[:, None])
    gate_grads = jnp.sum(results * cot_part, axis=-1)
    moe_part, gate_grads = (moe_sum, gate_grads)
    moe_total = lax.psum(moe_part[:length].astype(jnp.bfloat16), "tensor").astype(jnp.float32)
    layer_out = (after_attn + moe_total).astype(jnp.bfloat16)
    grad_routed = (
        (gate_slots[:, None] * cot_pad[owners]).astype(jnp.bfloat16).reshape(EXPERTS, CAP, D)
    )
    owned_grads = lax.all_to_all(grad_routed, "fsdp", split_axis=0, concat_axis=1, tiled=True)
    input_part, gate_part, up_part, hidden_part = expert_backward(
        expert_weights, owned_rows, owned_grads
    )
    grad_experts = expert_weight_grads(owned_rows, owned_grads, gate_part, up_part, hidden_part)
    returned_grads = lax.all_to_all(input_part, "fsdp", split_axis=1, concat_axis=0, tiled=True)
    expert_input = (
        jnp.zeros((length + 1, D), jnp.float32)
        .at[owners]
        .add(returned_grads.reshape(EXPERTS * CAP, D))
    )
    pair_gate_grads = gate_grads[slot_ids]
    expert_input_all, pair_grads = lax.psum((expert_input[:length], pair_gate_grads), "tensor")
    mean_term = jnp.sum(gate_values * pair_grads, axis=-1, keepdims=True)
    chosen_grads = gate_values * (pair_grads - mean_term)
    matches = (routes[:, :, None] == jnp.arange(EXPERTS, dtype=jnp.int32)[None, None, :]).astype(
        jnp.float32
    )
    logit_grads = jnp.sum(matches * chosen_grads[:, :, None], axis=1).astype(jnp.bfloat16)
    grad_router = transposed_times(normed_two, logit_grads)
    grad_normed_two = expert_input_all + times_transposed(logit_grads, router_all)
    grad_ffn_gain = jnp.sum(grad_normed_two * after_attn * inverse_two, axis=0)
    grad_after = cotangent.astype(jnp.float32) + norm_backward(
        after_attn, inverse_two, ffn_gain_f, grad_normed_two
    )
    grad_branch = grad_after.astype(jnp.bfloat16)
    grad_output = transposed_times(grad_branch, attended_low)
    grad_attended = jnp.dot(grad_branch, output_all, preferred_element_type=jnp.float32).astype(
        jnp.bfloat16
    )
    grad_attended = grad_attended.reshape(block_count, block_rows, local_heads, HD)

    def attend_back(running, block_in):
        key_grads, value_grads = running
        query_block, grad_block, log_block = block_in
        scores = (
            jnp.einsum("qhd,khd->hqk", query_block, key_low, preferred_element_type=jnp.float32)
            * score_scale
        )
        probs_exact = jnp.exp(scores - log_block[..., None])
        grad_probs = jnp.einsum(
            "qhd,khd->hqk", grad_block, value_low, preferred_element_type=jnp.float32
        )
        value_grads = value_grads + jnp.einsum(
            "hqk,qhd->khd",
            probs_exact.astype(jnp.bfloat16),
            grad_block,
            preferred_element_type=jnp.float32,
        )
        row_terms = jnp.sum(probs_exact * grad_probs, axis=-1, keepdims=True)
        grad_scores = (probs_exact * (grad_probs - row_terms)).astype(jnp.bfloat16)
        query_grads = (
            jnp.einsum("hqk,khd->qhd", grad_scores, key_low, preferred_element_type=jnp.float32)
            * score_scale
        )
        key_grads = (
            key_grads
            + jnp.einsum(
                "hqk,qhd->khd", grad_scores, query_block, preferred_element_type=jnp.float32
            )
            * score_scale
        )
        return ((key_grads, value_grads), query_grads)

    zero_heads = jnp.zeros((length, local_heads, HD), jnp.float32)
    (key_grads, value_grads), query_grads = lax.scan(
        attend_back,
        (zero_heads, zero_heads),
        (query_low.reshape(block_count, block_rows, local_heads, HD), grad_attended, log_totals),
    )
    query_grads = rotate(query_grads.reshape(length, local_heads, HD), cosine, sine_part, -1.0)
    key_grads = rotate(key_grads, cosine, sine_part, -1.0)
    grad_query_gain = jnp.sum(query_grads * query_raw * inverse_query, axis=(0, 1))
    grad_key_gain = jnp.sum(key_grads * key_raw * inverse_key, axis=(0, 1))
    query_raw_grads = norm_backward(query_raw, inverse_query, query_gain_f, query_grads).astype(
        jnp.bfloat16
    )
    key_raw_grads = norm_backward(key_raw, inverse_key, key_gain_f, key_grads).astype(jnp.bfloat16)
    query_raw_grads = query_raw_grads.reshape(length, local_heads * HD)
    key_raw_grads = key_raw_grads.reshape(length, local_heads * HD)
    value_raw_grads = value_grads.astype(jnp.bfloat16).reshape(length, local_heads * HD)
    grad_query = transposed_times(normed_one, query_raw_grads)
    grad_key = transposed_times(normed_one, key_raw_grads)
    grad_value = transposed_times(normed_one, value_raw_grads)
    grad_normed_part = times_transposed(query_raw_grads, query_all) + times_transposed(
        key_raw_grads, key_all
    )
    grad_normed_part = grad_normed_part + times_transposed(value_raw_grads, value_all)
    grad_normed_one, grad_query_gain, grad_key_gain = lax.psum(
        (grad_normed_part, grad_query_gain, grad_key_gain), "tensor"
    )
    grad_attn_gain = jnp.sum(grad_normed_one * residual * inverse_one, axis=0)
    grad_tokens = (
        grad_after + norm_backward(residual, inverse_one, attn_gain_f, grad_normed_one)
    ).astype(jnp.bfloat16)
    shards = (
        lax.psum_scatter(
            grad_query.astype(jnp.bfloat16), "fsdp", scatter_dimension=0, tiled=True
        ).astype(jnp.float32),
        lax.psum_scatter(
            grad_key.astype(jnp.bfloat16), "fsdp", scatter_dimension=0, tiled=True
        ).astype(jnp.float32),
        lax.psum_scatter(
            grad_value.astype(jnp.bfloat16), "fsdp", scatter_dimension=0, tiled=True
        ).astype(jnp.float32),
        lax.psum_scatter(
            grad_output.astype(jnp.bfloat16), "fsdp", scatter_dimension=0, tiled=True
        ).astype(jnp.float32),
        lax.psum_scatter(
            grad_router.astype(jnp.bfloat16), "fsdp", scatter_dimension=0, tiled=True
        ).astype(jnp.float32),
        lax.psum_scatter(
            grad_attn_gain.astype(jnp.bfloat16), "fsdp", scatter_dimension=0, tiled=True
        ).astype(jnp.float32),
        lax.psum_scatter(
            grad_ffn_gain.astype(jnp.bfloat16), "fsdp", scatter_dimension=0, tiled=True
        ).astype(jnp.float32),
        lax.psum_scatter(
            grad_query_gain.astype(jnp.bfloat16), "fsdp", scatter_dimension=0, tiled=True
        ).astype(jnp.float32),
        lax.psum_scatter(
            grad_key_gain.astype(jnp.bfloat16), "fsdp", scatter_dimension=0, tiled=True
        ).astype(jnp.float32),
    )
    return (
        layer_out,
        grad_tokens,
        shards[0],
        shards[1],
        shards[2],
        shards[3],
        shards[4],
        shards[5],
        shards[6],
        shards[7],
        shards[8],
        grad_experts,
    )


def solution(mesh):
    return jax.shard_map(
        on_device,
        mesh=mesh,
        in_specs=(
            P("fsdp", None),
            P("fsdp", None),
            P("fsdp", None),
            P("fsdp", "tensor"),
            P("fsdp", "tensor"),
            P("fsdp", "tensor"),
            P("fsdp", "tensor"),
            P("fsdp", None),
            P("fsdp"),
            P("fsdp"),
            P("fsdp"),
            P("fsdp"),
            P("fsdp", None, None, "tensor"),
        ),
        out_specs=(
            P("fsdp", None),
            P("fsdp", None),
            P("fsdp", "tensor"),
            P("fsdp", "tensor"),
            P("fsdp", "tensor"),
            P("fsdp", "tensor"),
            P("fsdp", None),
            P("fsdp"),
            P("fsdp"),
            P("fsdp"),
            P("fsdp"),
            P("fsdp", None, None, "tensor"),
        ),
        check_vma=False,
    )
```

profile of v0, /device:TPU:0, one launch (start us, length us, event | category | flops | bytes accessed | tf_op | source)
XLA Modules:
  0.0 1680.4 jit_solution(10987104011820397059)
XLA Ops:
  13.7 15.2 all-reduce.10
  43.9 26.5 %all-gather.9.cloned.1.call-done = bf16[2048,512]{1,0:T(8,128)(2,1)} async-done(((bf16[256,512]{1,0:T(8,128)(2,1)}), bf16[2048,512]{1,0:T(8,128)(2,1)}) %all-gather.9.cloned.1.call-update) | async-done | bytes 2097168 | tf_op jit(solution)/shard_map/all_gather | solution.py:143
  76.9 23.4 %all-gather.7.cloned.1.call-done = bf16[2048,512]{1,0:T(8,128)(2,1)} async-done(((bf16[256,512]{1,0:T(8,128)(2,1)}), bf16[2048,512]{1,0:T(8,128)(2,1)}) %all-gather.7.cloned.1.call-update) | async-done | bytes 2097168 | tf_op jit(solution)/shard_map/all_gather | solution.py:145
  103.7 26.2 %all-gather.13.cloned.1.call-done = bf16[2048,512]{1,0:T(8,128)(2,1)} async-done(((bf16[256,512]{1,0:T(8,128)(2,1)}), bf16[2048,512]{1,0:T(8,128)(2,1)}) %all-gather.13.cloned.1.call-update) | async-done | bytes 2097168 | tf_op jit(solution)/shard_map/all_gather | solution.py:146
  143.6 18.1 %reduce-window.6 = s32[64,16,128]{2,1,0:T(8,128)S(1)} reduce-window(s32[64,16,128]{2,1,0:T(8,128)S(1)} %fusion.59, s32[]{:T(128)} %constant.105.clone.1), window={size=1x1x128 pad=0_0x0_0x127_0}, to_apply=%region_6.7 | reduce-window | flops 16646144 | bytes 1048580 | tf_op jit(solution)/shard_map/reduce-window
  171.6 48.7 %all-reduce.16.cloned.1.call-done = f32[256,2048]{1,0:T(8,128)} async-done(((f32[256,2048]{1,0:T(8,128)}), f32[256,2048]{1,0:T(8,128)}) %all-reduce.16.cloned.1.call-update) | async-done | bytes 2097168 | tf_op jit(solution)/shard_map/psum | solution.py:203
  234.7 122.8 %all_to_all.66 = bf16[64,40,2048]{2,1,0:T(8,128)(2,1)} all-to-all(bf16[64,40,2048]{2,1,0:T(8,128)(2,1)} %bitcast.242), channel_id=1, replica_groups=mesh['fsdp'=8,'tensor'=4] {'fsdp'}, dimensions={0} | all-to-all | bytes 20971520 | tf_op jit(solution)/shard_map/all_to_all | solution.py:218
  388.8 14.3 fusion.3
  403.2 21.6 %copy.252 = f32[8,320,2048]{2,0,1:T(8,128)} copy(f32[8,320,2048]{2,1,0:T(8,128)} %fusion.3) | data formatting | bytes 41943040 | tf_op jit(solution)/shard_map/erf,edf->erd/dot_general | solution.py:78
  456.5 207.6 %all_gather.35 = bf16[2048,64]{0,1:T(8,128)(2,1)S(1)} all-gather(bf16[256,64]{0,1:T(8,128)(2,1)S(1)} %copy-done.62), channel_id=1, replica_groups=mesh['fsdp'=8,'tensor'=4] {'fsdp'}, dimensions={0}, use_global_device_ids=true | all-gather | bytes 294912 | tf_op jit(solution)/shard_map/all_gather | solution.py:147
  664.6 17.0 %gather_fusion.3 = f32[2048]{0:T(1024)S(1)} fusion(f32[256,64]{0,1:T(8,128)S(1)} %fusion.96, s32[2048]{0:T(1024)S(1)} %reshape.331), kind=kCustom, calls=%fused_computation.3 | custom fusion | bytes 32768 | tf_op jit(solution)/shard_map/jit(take_along_axis)/gather | solution.py:207
  681.9 20.6 %fusion = f32[8,8,40]{2,1,0:T(8,128)S(1)} fusion(f32[8,8,40,2048]{3,2,1,0:T(8,128)} %bitcast.234, f32[8,8,40,2048]{3,0,2,1:T(8,128)} %bitcast.17), kind=kLoop, calls=%fused_computation.11 | loop fusion | flops 10483200 | bytes 41953280 | tf_op jit(solution)/shard_map/reduce_sum | solution.py:226
  741.5 120.5 %all_to_all.67 = bf16[64,40,2048]{2,1,0:T(8,128)(2,1)} all-to-all(bf16[64,40,2048]{2,1,0:T(8,128)(2,1)S(1)} %multiply_convert_fusion), channel_id=1, replica_groups=mesh['fsdp'=8,'tensor'=4] {'fsdp'}, dimensions={0} | all-to-all | bytes 20971520 | tf_op jit(solution)/shard_map/all_to_all | solution.py:233
  883.7 14.8 fusion.5
  898.5 18.9 %fusion.13 = f32[8,320,2048]{2,1,0:T(8,128)} fusion(f32[8,320,2048]{2,1,0:T(8,128)} %fusion.5, bf16[8,320,256]{2,1,0:T(8,128)(2,1)S(1)} %get-tuple-element.145, bf16[8,3,2048,256]{3,2,1,0:T(8,128)(2,1)} %param.25), kind=kOutput, calls=%fused_computation.25 | convolution fusion | flops 2689597440 | bytes 51642368 | tf_op jit(solution)/shard_map/erf,edf->erd/dot_general | solution.py:96
  917.4 21.5 %copy.258 = f32[8,320,2048]{2,0,1:T(8,128)} copy(f32[8,320,2048]{2,1,0:T(8,128)} %fusion.13) | data formatting | bytes 41943040 | tf_op jit(solution)/shard_map/add | solution.py:99
  945.7 22.4 %copy.253 = f32[8,8,40,2048]{3,2,0,1:T(8,128)} copy(f32[8,8,40,2048]{3,0,2,1:T(8,128)} %bitcast.17) | data formatting | bytes 41943040 | tf_op jit(solution)/shard_map/all_to_all | solution.py:220
  968.1 205.9 %all-to-all-done.3 = f32[8,320,2048]{2,0,1:T(8,128)} async-done(((f32[8,320,2048]{2,0,1:T(8,128)}), f32[8,320,2048]{2,0,1:T(8,128)}, u32[]{:S(2)}, u32[]{:S(2)}) %all-to-all-start.3) | async-done | bytes 20971552 | tf_op jit(solution)/shard_map/all_to_all | solution.py:238
  1174.0 22.4 %copy.259 = f32[8,8,40,2048]{3,2,0,1:T(8,128)} copy(f32[8,8,40,2048]{3,0,2,1:T(8,128)} %bitcast.25) | data formatting | bytes 41943040 | tf_op jit(solution)/shard_map/all_to_all | solution.py:238
  1196.4 34.1 %scatter_custom_fusion.3 = f32[257,2048]{1,0:T(8,128)S(1)} fusion(s32[2560]{0:T(1024)} %copy-done.57, f32[2560,2048]{1,0:T(8,128)} %bitcast.245, f32[]{:T(128)} %constant.62.clone.1), kind=kCustom, calls=%fused_computation.81 | custom fusion | flops 5242880 | bytes 2105856 | tf_op jit(solution)/shard_map/scatter-add | solution.py:242
  1232.1 16.9 %bitcast_multiply_fusion = f32[2560,2048]{1,0:T(8,128)} fusion(f32[8,8,40,2048]{3,2,0,1:T(8,128)} %copy.253, f32[2560]{0:T(1024)S(1)} %scatter_custom_fusion.1), kind=kLoop, calls=%fused_computation.9 | loop fusion | flops 5242880 | bytes 41953280 | tf_op jit(solution)/shard_map/mul | solution.py:225
  1249.0 34.9 %scatter_custom_fusion.2 = f32[257,2048]{1,0:T(8,128)} fusion(s32[2560]{0:T(1024)} %copy-done.57, f32[2560,2048]{1,0:T(8,128)} %bitcast_multiply_fusion, f32[]{:T(128)} %constant.62.clone.1), kind=kCustom, calls=%fused_computation.83 | custom fusion | flops 5242880 | bytes 2105856 | tf_op jit(solution)/shard_map/scatter-add | solution.py:225
  1295.9 19.2 %all-reduce.20.cloned.1.call-done = f32[256,2048]{1,0:T(8,128)} async-done(((f32[256,2048]{1,0:T(8,128)}), f32[256,2048]{1,0:T(8,128)}) %all-reduce.20.cloned.1.call-update) | async-done | bytes 2097168 | tf_op jit(solution)/shard_map/psum | solution.py:245
  1319.4 49.5 %all-reduce.18.cloned.1.call-done = bf16[256,2048]{1,0:T(8,128)(2,1)} async-done(((bf16[256,2048]{1,0:T(8,128)(2,1)}), bf16[256,2048]{1,0:T(8,128)(2,1)}) %all-reduce.18.cloned.1.call-update) | async-done | bytes 1048592 | tf_op jit(solution)/shard_map/psum | solution.py:228
  1407.8 15.5 convolution_bitcast_fusion
  1423.3 15.1 convolution_bitcast_fusion.1
  1438.4 15.5 convolution_bitcast_fusion.2
  1456.1 35.4 %pad_maximum_fusion = f32[8,3,2048,256]{3,2,0,1:T(8,128)} fusion(f32[8,1,2048,256]{3,2,0,1:T(8,128)} %convolution_bitcast_fusion, f32[8,1,2048,256]{3,2,0,1:T(8,128)} %convolution_bitcast_fusion.1, f32[8,1,2048,256]{3,2,0,1:T(8,128)} %convolution_bitcast_fusion.2), kind=kLoop, calls=%fused_computation.8 | loop fusion | flops 25165824 | bytes 100663296 | tf_op jit(solution)/shard_map/stack | solution.py:106
  1491.5 33.9 %copy.283 = f32[8,3,2048,256]{3,2,1,0:T(8,128)} copy(f32[8,3,2048,256]{3,2,0,1:T(8,128)} %pad_maximum_fusion) | data formatting | bytes 100663296
  1558.0 24.4 %reduce-scatter.8.cloned.1.call-done = bf16[256,512]{1,0:T(8,128)(2,1)} async-done(((bf16[2048,512]{1,0:T(8,128)(2,1)}), bf16[256,512]{1,0:T(8,128)(2,1)}) %reduce-scatter.8.cloned.1.call-update) | async-done | bytes 262160 | tf_op jit(solution)/shard_map/reduce_scatter | solution.py:332
  1584.2 42.9 %reduce-scatter.10.cloned.1.call-done = bf16[256,512]{1,0:T(8,128)(2,1)} async-done(((bf16[2048,512]{1,0:T(8,128)(2,1)}), bf16[256,512]{1,0:T(8,128)(2,1)}) %reduce-scatter.10.cloned.1.call-update) | async-done | bytes 262160 | tf_op jit(solution)/shard_map/reduce_scatter | solution.py:335
  1628.9 42.7 %reduce-scatter.12.cloned.1.call-done = bf16[256,512]{1,0:T(8,128)(2,1)} async-done(((bf16[2048,512]{1,0:T(8,128)(2,1)}), bf16[256,512]{1,0:T(8,128)(2,1)}) %reduce-scatter.12.cloned.1.call-update) | async-done | bytes 262160 | tf_op jit(solution)/shard_map/reduce_scatter | solution.py:338
  (345 shorter events, 294.5 us)
Async XLA Ops:
  7.2 33.7 %copy-start.2 = (bf16[256,2048]{1,0:T(8,128)(2,1)S(1)}, bf16[256,2048]{1,0:T(8,128)(2,1)}, u32[]{:S(2)}) copy-start(bf16[256,2048]{1,0:T(8,128)(2,1)} %param.13) | copy-start | bytes 3145732
  7.2 33.7 %all-gather.11.cloned.1.call-start = ((), (), s32[]{:S(2)}) async-start(), calls=%async_computation.11 | async-start | bytes 2359296 | tf_op jit(solution)/shard_map/all_gather | solution.py:144
  7.9 62.5 %all-gather.9.cloned.1.call-start = ((), (), s32[]{:S(2)}) async-start(), calls=%async_computation.10 | async-start | bytes 2359296 | tf_op jit(solution)/shard_map/all_gather | solution.py:143
  8.7 91.6 %all-gather.7.cloned.1.call-start = ((), (), s32[]{:S(2)}) async-start(), calls=%async_computation.9 | async-start | bytes 2359296 | tf_op jit(solution)/shard_map/all_gather | solution.py:145
  9.4 120.5 %all-gather.13.cloned.1.call-start = ((), (), s32[]{:S(2)}) async-start(), calls=%async_computation.12 | async-start | bytes 2359296 | tf_op jit(solution)/shard_map/all_gather | solution.py:146
  10.0 210.3 %all-reduce.16.cloned.1.call-start = ((), (), s32[]{:S(2)}) async-start(), calls=%async_computation.13 | async-start | bytes 4194304 | tf_op jit(solution)/shard_map/psum | solution.py:203
  29.0 45.7 %copy-start.72 = (f32[128]{0:T(128)}, f32[128]{0:T(128)S(1)}, u32[]{:S(2)}) copy-start(f32[128]{0:T(128)S(1)} %convert_element_type.178) | copy-start | bytes 1540
  37.6 62.7 %copy-start.50 = (f32[8,1,256]{2,1,0:T(1,128)}, f32[8,1,256]{2,1,0:T(1,128)S(1)}, u32[]{:S(2)}) copy-start(f32[8,1,256]{2,1,0:T(1,128)S(1)} %convert_element_type.228) | copy-start | bytes 24580
  37.6 37.0 %copy-start.75 = (f32[128]{0:T(128)}, f32[128]{0:T(128)S(1)}, u32[]{:S(2)}) copy-start(f32[128]{0:T(128)S(1)} %convert_element_type.177) | copy-start | bytes 1540
  39.7 60.5 %copy-start.63 = (f32[256]{0:T(256)}, f32[256]{0:T(256)S(1)}, u32[]{:S(2)}) copy-start(f32[256]{0:T(256)S(1)} %get-tuple-element.176) | copy-start | bytes 3076
  40.9 34.1 %copy-start.36 = (f32[256,64]{1,0:T(8,128)}, f32[256,64]{1,0:T(8,128)S(1)}, u32[]{:S(2)}) copy-start(f32[256,64]{1,0:T(8,128)S(1)} %get-tuple-element.183) | copy-start | bytes 196612
  43.3 31.4 %copy-start.12 = (f32[256,512]{1,0:T(8,128)}, f32[256,512]{1,0:T(8,128)S(1)}, u32[]{:S(2)}) copy-start(f32[256,512]{1,0:T(8,128)S(1)} %fusion.87) | copy-start | bytes 1572868
  103.7 29.9 %copy-start.38 = (bf16[4,128,256]{2,1,0:T(8,128)(2,1)}, bf16[4,128,256]{2,1,0:T(8,128)(2,1)S(1)}, u32[]{:S(2)}) copy-start(bf16[4,128,256]{2,1,0:T(8,128)(2,1)S(1)} %convolution_convert_fusion.7) | copy-start | bytes 786436
  143.5 79.3 %copy-start.52 = (f32[8,1,256]{2,1,0:T(1,128)}, f32[8,1,256]{2,1,0:T(1,128)S(1)}, u32[]{:S(2)}) copy-start(f32[8,1,256]{2,1,0:T(1,128)S(1)} %convert_element_type.229) | copy-start | bytes 24580
  163.5 58.7 %copy-start.69 = (s32[2048,1]{0,1:T(1,128)}, s32[2048,1]{0,1:T(1,128)S(1)}, u32[]{:S(2)}) copy-start(s32[2048,1]{0,1:T(1,128)S(1)} %compare_select_fusion) | copy-start | bytes 24580
  171.6 50.6 %copy-start.57 = (s32[2560]{0:T(1024)}, s32[2560]{0:T(1024)S(1)}, u32[]{:S(2)}) copy-start(s32[2560]{0:T(1024)S(1)} %compare_select_fusion.1) | copy-start | bytes 30724
  223.9 440.3 %copy-start.6 = (bf16[256,2048]{1,0:T(8,128)(2,1)}, bf16[256,2048]{1,0:T(8,128)(2,1)S(1)}, u32[]{:S(2)}) copy-start(bf16[256,2048]{1,0:T(8,128)(2,1)S(1)} %multiply_convert_fusion.4) | copy-start | bytes 3145732
  424.7 257.1 %all-to-all-start.1 = ((f32[8,320,2048]{2,0,1:T(8,128)}), f32[8,320,2048]{2,0,1:T(8,128)}, u32[]{:S(2)}, u32[]{:S(2)}) async-start(f32[8,320,2048]{2,0,1:T(8,128)} %copy.252), calls=%async_computation.1 | async-start | bytes 41943040 | tf_op jit(solution)/shard_map/all_to_all | solution.py:220
  938.9 235.1 %all-to-all-start.3 = ((f32[8,320,2048]{2,0,1:T(8,128)}), f32[8,320,2048]{2,0,1:T(8,128)}, u32[]{:S(2)}, u32[]{:S(2)}) async-start(f32[8,320,2048]{2,0,1:T(8,128)} %copy.258), calls=%async_computation.3 | async-start | bytes 41943040 | tf_op jit(solution)/shard_map/all_to_all | solution.py:238
  945.1 370.0 %all-reduce.20.cloned.1.call-start = ((), (), s32[]{:S(2)}) async-start(), calls=%async_computation.15 | async-start | bytes 4194304 | tf_op jit(solution)/shard_map/psum | solution.py:245
  1232.0 136.8 %all-reduce.18.cloned.1.call-start = ((), (), s32[]{:S(2)}) async-start(), calls=%async_computation.14 | async-start | bytes 2097152 | tf_op jit(solution)/shard_map/psum | solution.py:228
  1286.7 28.5 %copy-start.30 = (bf16[2048,64]{0,1:T(8,128)(2,1)S(1)}, bf16[2048,64]{0,1:T(8,128)(2,1)}, u32[]{:S(2)}) copy-start(bf16[2048,64]{0,1:T(8,128)(2,1)} %copy-done.29) | copy-start | bytes 786436
  1286.7 28.5 %copy-start.53 = (f32[8,1,256]{2,1,0:T(1,128)S(1)}, f32[8,1,256]{2,1,0:T(1,128)}, u32[]{:S(2)}) copy-start(f32[8,1,256]{2,1,0:T(1,128)} %copy-done.52) | copy-start | bytes 24580
  1286.7 119.7 %reduce-scatter.14.cloned.1.call-start = ((), (), s32[]{:S(2)}) async-start(), calls=%async_computation.21 | async-start | bytes 294912 | tf_op jit(solution)/shard_map/reduce_scatter | solution.py:341
  1295.6 73.2 %copy-start.18 = (bf16[256,2048]{1,0:T(8,128)(2,1)S(1)}, bf16[256,2048]{1,0:T(8,128)(2,1)}, u32[]{:S(2)}) copy-start(bf16[256,2048]{1,0:T(8,128)(2,1)} %param.14) | copy-start | bytes 3145732
  1295.6 73.2 %copy-start.68 = (f32[256]{0:T(256)S(1)}, f32[256]{0:T(256)}, u32[]{:S(2)}) copy-start(f32[256]{0:T(256)} %copy-done.67) | copy-start | bytes 3076
  1295.6 73.2 %copy-start.79 = (f32[256]{0:T(256)S(1)}, f32[256]{0:T(256)}, u32[]{:S(2)}) copy-start(f32[256]{0:T(256)} %get-tuple-element.177) | copy-start | bytes 3076
  1295.6 240.3 %all-reduce.22.cloned.1.call-start = ((), (), s32[]{:S(2)}) async-start(), calls=%async_computation.16 | async-start | bytes 4194304 | tf_op jit(solution)/shard_map/psum | solution.py:321
  1394.9 161.3 %reduce-scatter.6.cloned.1.call-start = ((), (), s32[]{:S(2)}) async-start(), calls=%async_computation.17 | async-start | bytes 2359296 | tf_op jit(solution)/shard_map/reduce_scatter | solution.py:329
  1399.3 183.1 %reduce-scatter.8.cloned.1.call-start = ((), (), s32[]{:S(2)}) async-start(), calls=%async_computation.18 | async-start | bytes 2359296 | tf_op jit(solution)/shard_map/reduce_scatter | solution.py:332
  1402.5 224.7 %reduce-scatter.10.cloned.1.call-start = ((), (), s32[]{:S(2)}) async-start(), calls=%async_computation.19 | async-start | bytes 2359296 | tf_op jit(solution)/shard_map/reduce_scatter | solution.py:335
  1404.8 266.9 %reduce-scatter.12.cloned.1.call-start = ((), (), s32[]{:S(2)}) async-start(), calls=%async_computation.20 | async-start | bytes 2359296 | tf_op jit(solution)/shard_map/reduce_scatter | solution.py:338
  (65 other events, 390.0 us)
Sparse Core Ops, SparseCore 0:
  9.9 30.6 all-gather.10
  42.5 27.8 all-gather.8
  72.3 27.8 all-gather.6
  102.0 27.8 all-gather.12
  133.8 86.4 all-reduce.15
  1232.1 82.9 all-reduce.19
  1318.0 50.7 all-reduce.17
  1372.1 32.9 reduce-scatter.13
  1407.5 86.5 all-reduce.21
  1497.5 40.1 reduce-scatter.5
  1541.0 41.3 reduce-scatter.7
  1585.9 41.2 reduce-scatter.9
  1630.4 41.1 reduce-scatter.11
where the time goes:
time: 1690 us; the launch traced here: 1680 us
  blocking collectives  516 us (31%)
  waiting for transfers between devices  512 us (30%)
  local copies, waits for them, and re-layouts  238 us (14%)
  other arithmetic  221 us (13%)
  matrix products  163 us (10%)
  between operations  17.5 us (1%)
    all_gather x1, blocking collectives, on_device(): lax.all_gather(w_router, 'fsdp', axis=0, tiled=True)  208 us
    all_to_all x1, waiting for transfers between devices, on_device(): lax.all_to_all(input_part, 'fsdp', split_axis=1, concat_axis=0, tiled=True)  206 us
    all_to_all x1, blocking collectives, on_device(): lax.all_to_all(routed_rows, 'fsdp', split_axis=0, concat_axis=1, tiled=True)  123 us
    all_to_all x1, blocking collectives, on_device(): lax.all_to_all(grad_routed, 'fsdp', split_axis=0, concat_axis=1, tiled=True)  121 us
    psum x1, waiting for transfers between devices, on_device(): lax.psum(moe_part[:length].astype(jnp.bfloat16), 'tensor')  49.5 us
    psum x1, waiting for transfers between devices, on_device(): after_attn = residual + lax.psum(attn_part, 'tensor')  48.7 us
    unnamed x175, local copies, waits for them, and re-layouts  46.6 us
    reduce_scatter x1, waiting for transfers between devices, on_device(): lax.psum_scatter(grad_value.astype(jnp.bfloat16), 'fsdp', scatter_dimensi...  42.9 us
  transfers between devices with their start and end apart: 15, of which 10 were waited for; matrix products, arithmetic and copies ran while one was open for 20% of the time, Pallas kernels for 0%

commit v1 on v0

v1 whole, which is shorter than its diff:
```python
import functools

import jax
import jax.numpy as jnp
from jax import lax
from jax.experimental import pallas as pl
from jax.experimental.pallas import tpu as pltpu
from jax.sharding import PartitionSpec as P

D = 2048
HD = 128
EXPERTS = 64
CAP = 40
SIDE = 128
EPSILON = 1e-06
ROPE_BASE = 10000.0

F32 = jnp.float32
BF16 = jnp.bfloat16
VMEM = pl.BlockSpec(memory_space=pltpu.VMEM)
SMEM = pl.BlockSpec(memory_space=pltpu.SMEM)
HBM = pl.BlockSpec(memory_space=pl.ANY)
VMEM_BYTES = 60 * 1024 * 1024


def shape(dims, dtype):
    return jax.ShapeDtypeStruct(tuple(dims), dtype)


def params(**more):
    return pltpu.CompilerParams(vmem_limit_bytes=VMEM_BYTES, **more)


def cost(flops, moved):
    return pl.CostEstimate(flops=int(flops), bytes_accessed=int(moved), transcendentals=0)


def dot(left, right):
    return jnp.dot(left, right, preferred_element_type=F32)


def dot_nt(left, right):
    return lax.dot_general(left, right, (((1,), (1,)), ((), ())), preferred_element_type=F32)


def dot_tn(left, right):
    return lax.dot_general(left, right, (((0,), (0,)), ((), ())), preferred_element_type=F32)


def rms_inverse(values):
    return lax.rsqrt(jnp.mean(values * values, axis=-1, keepdims=True) + EPSILON)


def norm_backward(values, inverse, gain, upstream):
    scaled = gain * upstream
    return inverse * scaled - values * (inverse * inverse * inverse) * jnp.mean(
        values * scaled, axis=-1, keepdims=True
    )


def half_turn(values):
    return pltpu.roll(values, HD // 2, 1)


def lanes(dims):
    return lax.broadcasted_iota(jnp.int32, dims, len(dims) - 1)


def swap(block, axis, size, step):
    return lax.ppermute(block, axis, [(i, i ^ step) for i in range(size)])


def plane_gather(block, size):
    if size != 8:
        return [(0, 0, block)] + [(p, 0, swap(block, "fsdp", size, p)) for p in range(1, size)]
    half = block.shape[0] // 2
    along_x = swap(block, "fsdp", size, 2)
    along_y = swap(block, "fsdp", size, 4)
    front = swap(along_y[:half], "fsdp", size, 2)
    back = swap(along_x[half:], "fsdp", size, 4)
    mine = [(0, 0, block), (2, 0, along_x), (4, 0, along_y), (6, 0, front), (6, half, back)]
    return mine + [(p + 1, row, swap(part, "fsdp", size, 1)) for p, row, part in mine]


def plane_reduce(keep, send, size):
    if size != 8:
        total = keep[0].astype(F32)
        for p in range(1, size):
            block = keep[p // 2] if p % 2 == 0 else send[p // 2]
            total = total + swap(block, "fsdp", size, p).astype(F32)
        return total
    got = swap(send, "fsdp", size, 1)
    half = keep.shape[1] // 2

    def both(q, rows):
        return keep[q, rows].astype(F32) + got[q, rows].astype(F32)

    front, back = slice(0, half), slice(half, None)
    front_got = swap(
        jnp.stack([both(1, front), both(3, front)]).astype(BF16), "fsdp", size, 2
    )
    back_got = swap(jnp.stack([both(2, back), both(3, back)]).astype(BF16), "fsdp", size, 4)
    front_last = swap((both(2, front) + front_got[1].astype(F32)).astype(BF16), "fsdp", size, 4)
    back_last = swap((both(1, back) + back_got[1].astype(F32)).astype(BF16), "fsdp", size, 2)
    front_sum = both(0, front) + front_got[0].astype(F32) + front_last.astype(F32)
    back_sum = both(0, back) + back_got[0].astype(F32) + back_last.astype(F32)
    return jnp.concatenate([front_sum, back_sum], axis=0)


def start_fetch(pieces, refs, place, sems):
    copies = []
    for k, (index, row, part) in enumerate(pieces):
        copy = pltpu.make_async_copy(refs[k], place(index, row, part.shape[0]), sems.at[k])
        copy.start()
        copies.append(copy)
    return copies


def attend_forward(pos, tokens, cosine, sine, pieces, nf, nt):
    length = tokens.shape[0]
    block = D // nf
    rows = length // nt
    columns = pieces[0][2].shape[1]
    width = (columns - SIDE) // 4
    heads = width // HD
    count = len(pieces)

    def kernel(pos_ref, x_ref, cos_ref, sin_ref, *refs):
        piece_refs, refs = refs[:count], refs[count:]
        n1_ref, qk_ref, rot_ref, v_ref, prob_ref, att_ref, side_ref, gain_ref, head_gain_ref = refs[:9]
        part_refs, (w, out, sems) = refs[9 : 9 + nt], refs[9 + nt :]
        f, t = pos_ref[0], pos_ref[1]

        def place(index, row, number):
            start = pl.multiple_of((f ^ index) * block + row, 16)
            return w.at[pl.ds(start, number), :]

        copies = start_fetch(pieces, piece_refs, place, sems)
        x = x_ref[...].astype(F32)
        normed = x * rms_inverse(x)
        for copy in copies:
            copy.wait()
        side_ref[...] = w[:, 4 * width :]
        turned = jnp.transpose(w[:, 4 * width :].astype(F32))
        gain_ref[...] = turned[EXPERTS : EXPERTS + 8]
        head_rows = turned[EXPERTS : EXPERTS + 8, :block]
        for p in range(1, nf):
            head_rows = head_rows + turned[EXPERTS : EXPERTS + 8, p * block : (p + 1) * block]
        head_gains = head_rows[:, :HD]
        head_gain_ref[...] = head_gains
        n1 = (normed * turned[EXPERTS : EXPERTS + 1]).astype(BF16)
        n1_ref[...] = n1
        raw = dot(n1, w[:, : 3 * width])
        qk_ref[...] = raw[:, : 2 * width]
        v_ref[...] = raw[:, 2 * width :].astype(BF16)
        cos, sin = cos_ref[...], sin_ref[...]
        for h in range(heads):
            span = slice(h * HD, (h + 1) * HD)
            turned_rows = []
            for which in range(2):
                values = raw[:, which * width + h * HD : which * width + (h + 1) * HD]
                scaled = values * rms_inverse(values) * head_gains[2 + which : 3 + which]
                low = (scaled * cos + half_turn(scaled) * sin).astype(BF16)
                rot_ref[:, which * width + h * HD : which * width + (h + 1) * HD] = low
                turned_rows.append(low)
            scores = dot_nt(turned_rows[0], turned_rows[1]) * (HD**-0.5)
            shifted = jnp.exp(scores - jnp.max(scores, axis=-1, keepdims=True))
            probs = shifted / jnp.sum(shifted, axis=-1, keepdims=True)
            prob_ref[h] = probs
            att_ref[:, span] = dot(probs.astype(BF16), v_ref[:, span]).astype(BF16)
        out[...] = dot_nt(att_ref[...], w[:, 3 * width : 4 * width]).astype(BF16)
        for d in range(nt):
            start = pl.multiple_of((t ^ d) * rows, 16)
            part_refs[d][...] = out[pl.ds(start, rows), :]

    results = pl.pallas_call(
        kernel,
        out_shape=[
            shape((length, D), BF16),
            shape((length, 2 * width), F32),
            shape((length, 2 * width), BF16),
            shape((length, width), BF16),
            shape((heads, length, length), F32),
            shape((length, width), BF16),
            shape((D, SIDE), BF16),
            shape((8, D), F32),
            shape((8, HD), F32),
        ]
        + [shape((rows, D), BF16)] * nt,
        in_specs=[SMEM, VMEM, VMEM, VMEM] + [HBM] * count,
        out_specs=[VMEM] * (9 + nt),
        scratch_shapes=[
            pltpu.VMEM((D, columns), BF16),
            pltpu.VMEM((length, D), BF16),
            pltpu.SemaphoreType.DMA((count,)),
        ],
        compiler_params=params(),
        cost_estimate=cost(2 * length * D * 4 * width, 2 * D * columns),
        name="attend_forward",
    )(pos, tokens, cosine, sine, *[part for _, _, part in pieces])
    return results[:9], results[9:]


def attend_backward(pos, grad_rows, pieces, saved, tokens, cosine, sine, nf, nt):
    _, qk, rot, values, probs, _, _, gains, head_gains = saved
    length = tokens.shape[0]
    block = D // nf
    rows = length // nt
    columns = pieces[0][2].shape[1]
    width = (columns - SIDE) // 4
    heads = width // HD
    count = len(pieces)

    def kernel(pos_ref, x_ref, cos_ref, sin_ref, qk_ref, rot_ref, v_ref, prob_ref, gain_ref, head_gain_ref, *refs):
        grad_refs, refs = refs[:nt], refs[nt:]
        piece_refs, refs = refs[:count], refs[count:]
        dqkv_ref, db_ref, row_ref, head_row_ref = refs[:4]
        part_refs, (w, out, sems) = refs[4 : 4 + nt], refs[4 + nt :]
        f, t = pos_ref[0], pos_ref[1]

        def place(index, row, number):
            start = pl.multiple_of((f ^ index) * block + row, 16)
            return w.at[pl.ds(start, number), :]

        copies = start_fetch(pieces, piece_refs, place, sems)
        for d in range(nt):
            start = pl.multiple_of((t ^ d) * rows, 16)
            db_ref[pl.ds(start, rows), :] = grad_refs[d][...]
        for copy in copies:
            copy.wait()
        cos, sin = cos_ref[...], sin_ref[...]
        head_gains = head_gain_ref[...]
        grad_att = dot(db_ref[...], w[:, 3 * width : 4 * width]).astype(BF16)
        gain_rows = [jnp.zeros((1, HD), F32), jnp.zeros((1, HD), F32)]
        for h in range(heads):
            span = slice(h * HD, (h + 1) * HD)
            query_low = rot_ref[:, span]
            key_low = rot_ref[:, width + h * HD : width + (h + 1) * HD]
            grad_out = grad_att[:, span]
            exact = prob_ref[h]
            grad_probs = dot_nt(grad_out, v_ref[:, span])
            row_terms = jnp.sum(exact * grad_probs, axis=-1, keepdims=True)
            grad_scores = (exact * (grad_probs - row_terms)).astype(BF16)
            dqkv_ref[:, 2 * width + h * HD : 2 * width + (h + 1) * HD] = dot_tn(
                exact.astype(BF16), grad_out
            ).astype(BF16)
            both = (dot(grad_scores, key_low), dot_tn(grad_scores, query_low))
            for which in range(2):
                span_w = slice(which * width + h * HD, which * width + (h + 1) * HD)
                grads = both[which] * (HD**-0.5)
                grads = grads * cos - half_turn(grads) * sin
                raw = qk_ref[:, span_w]
                inverse = rms_inverse(raw)
                gain_rows[which] = gain_rows[which] + jnp.sum(
                    grads * raw * inverse, axis=0, keepdims=True
                )
                dqkv_ref[:, span_w] = norm_backward(
                    raw, inverse, head_gains[2 + which : 3 + which], grads
                ).astype(BF16)
        head_row_ref[...] = jnp.concatenate(gain_rows + [jnp.zeros((6, HD), F32)], axis=0)
        grad_normed = dot_nt(dqkv_ref[...], w[:, : 3 * width])
        out[...] = grad_normed.astype(BF16)
        x = x_ref[...].astype(F32)
        row = jnp.sum(grad_normed * (x * rms_inverse(x)), axis=0, keepdims=True)
        row_ref[...] = jnp.broadcast_to(row, (8, D))
        for d in range(nt):
            start = pl.multiple_of((t ^ d) * rows, 16)
            part_refs[d][...] = out[pl.ds(start, rows), :]

    results = pl.pallas_call(
        kernel,
        out_shape=[
            shape((length, 3 * width), BF16),
            shape((length, D), BF16),
            shape((8, D), F32),
            shape((8, HD), F32),
        ]
        + [shape((rows, D), BF16)] * nt,
        in_specs=[SMEM] + [VMEM] * (9 + nt) + [HBM] * count,
        out_specs=[VMEM] * (4 + nt),
        scratch_shapes=[
            pltpu.VMEM((D, columns), BF16),
            pltpu.VMEM((length, D), BF16),
            pltpu.SemaphoreType.DMA((count,)),
        ],
        compiler_params=params(),
        cost_estimate=cost(2 * length * D * 4 * width, 2 * D * columns),
        name="attend_backward",
    )(
        pos, tokens, cosine, sine, qk, rot, values, probs, gains, head_gains,
        *grad_rows, *[part for _, _, part in pieces],
    )
    return results[:4], results[4:]


def projection_gradients(pos, normed, dqkv, grad_branch, attended, side_grads, attn_row, head_rows, group, nf):
    length = normed.shape[0]
    block = D // nf
    width = attended.shape[1]
    columns = 4 * width + SIDE

    def kernel(pos_ref, n1_ref, dqkv_ref, db_ref, att_ref, side_ref, row_ref, head_ref, keep_ref, send_ref):
        f = pos_ref[0]
        lane = lanes((block, SIDE))
        sub = lax.broadcasted_iota(jnp.int32, (block, SIDE), 0)
        for p in range(nf):
            owner = f ^ p
            start = pl.multiple_of(owner * block, 128)
            to = (keep_ref if p % 2 == 0 else send_ref).at[p // 2]
            to[:, : 3 * width] = dot_tn(n1_ref[:, pl.ds(start, block)], dqkv_ref[...]).astype(BF16)
            to[:, 3 * width : 4 * width] = dot_tn(
                db_ref[:, pl.ds(start, block)], att_ref[...]
            ).astype(BF16)
            side = side_ref[pl.ds(start, block), :]
            gain = jnp.transpose(jnp.broadcast_to(row_ref[0:1, pl.ds(start, block)], (SIDE, block)))
            side = jnp.where(lane == EXPERTS + 1, gain, side)
            mine = (lane == owner * group + sub) & (sub < group)
            for which in range(2):
                spread = jnp.where(mine, head_ref[which : which + 1, :], 0.0)
                side = jnp.where(
                    lane == EXPERTS + 2 + which, jnp.sum(spread, axis=1, keepdims=True), side
                )
            to[:, 4 * width :] = side.astype(BF16)

    return pl.pallas_call(
        kernel,
        out_shape=[shape((nf // 2, block, columns), BF16)] * 2,
        in_specs=[SMEM] + [VMEM] * 7,
        out_specs=[VMEM] * 2,
        compiler_params=params(),
        cost_estimate=cost(2 * length * D * 4 * width, 2 * D * columns),
        name="projection_gradients",
    )(pos, normed, dqkv, grad_branch, attended, side_grads, attn_row, head_rows)


def norm_and_route(pos, tokens, routes, parts, gains, side, nt):
    rows = tokens.shape[0] // nt
    top = routes.shape[1]

    def kernel(pos_ref, x_ref, route_ref, gain_ref, side_ref, *refs):
        part_refs, (h_ref, next_ref, gate_ref) = refs[:nt], refs[nt:]
        h = x_ref[...].astype(F32)
        for ref in part_refs:
            h = h + ref[...].astype(F32)
        h_ref[...] = h
        n2 = (h * rms_inverse(h) * gain_ref[1:2]).astype(BF16)
        next_ref[:, :D] = n2
        logits = dot(n2, side_ref[...])
        lane = lanes((rows, SIDE))
        chosen = route_ref[:, 0:1] == lane
        for j in range(1, top):
            chosen = chosen | (route_ref[:, j : j + 1] == lane)
        highest = jnp.max(jnp.where(chosen, logits, -jnp.inf), axis=-1, keepdims=True)
        shifted = jnp.where(chosen, jnp.exp(jnp.where(chosen, logits - highest, 0.0)), 0.0)
        gates = shifted / jnp.sum(shifted, axis=-1, keepdims=True)
        gate_ref[...] = gates
        first = gates.astype(BF16).astype(F32)
        rest = (gates - first).astype(BF16).astype(F32)
        next_ref[:, D:] = (first + pltpu.roll(rest, EXPERTS, 1)).astype(BF16)

    whole = lambda i, pos: (0, 0)
    mine = lambda i, pos: (pos[1], 0)
    return pl.pallas_call(
        kernel,
        out_shape=[shape((rows, D), F32), shape((rows, D + SIDE), BF16), shape((rows, SIDE), F32)],
        grid_spec=pltpu.PrefetchScalarGridSpec(
            num_scalar_prefetch=1,
            grid=(1,),
            in_specs=[
                pl.BlockSpec((rows, D), mine),
                pl.BlockSpec((rows, top), mine),
                pl.BlockSpec((8, D), whole),
                pl.BlockSpec((D, SIDE), whole),
            ]
            + [pl.BlockSpec((rows, D), whole)] * nt,
            out_specs=[
                pl.BlockSpec((rows, D), whole),
                pl.BlockSpec((rows, D + SIDE), whole),
                pl.BlockSpec((rows, SIDE), whole),
            ],
        ),
        compiler_params=params(),
        cost_estimate=cost(2 * rows * D * SIDE, 8 * rows * D),
        name="norm_and_route",
    )(pos, tokens, routes, gains, side, *parts)


def norm_back(pos, cotangent, parts, h, gates, normed, gains, side, nt):
    rows = h.shape[0]

    def kernel(pos_ref, cot_ref, h_ref, gate_ref, n2_ref, gain_ref, side_ref, *refs):
        part_refs, (dh_ref, db_ref, small_ref) = refs[:nt], refs[nt:]
        total = part_refs[0][...].astype(F32)
        for ref in part_refs[1:]:
            total = total + ref[...].astype(F32)
        pair = total[:, D:]
        pair = pair + pltpu.roll(pair, EXPERTS, 1)
        gates = gate_ref[...]
        grads = gates * (pair - jnp.sum(gates * pair, axis=-1, keepdims=True))
        low = grads.astype(BF16)
        dn2 = total[:, :D] + dot_nt(low, side_ref[...])
        h = h_ref[...]
        inverse = rms_inverse(h)
        gain_row = jnp.sum(dn2 * h * inverse, axis=0, keepdims=True)
        small = dot_tn(n2_ref[:, :D], low)
        column = jnp.transpose(jnp.broadcast_to(gain_row, (SIDE, D)))
        small_ref[...] = jnp.where(lanes((D, SIDE)) == EXPERTS, column, small)
        dh = cot_ref[...].astype(F32) + norm_backward(h, inverse, gain_ref[1:2], dn2)
        dh_ref[...] = dh
        db_ref[...] = dh.astype(BF16)

    whole = lambda i, pos: (0, 0)
    mine = lambda i, pos: (pos[1], 0)
    return pl.pallas_call(
        kernel,
        out_shape=[shape((rows, D), F32), shape((rows, D), BF16), shape((D, SIDE), F32)],
        grid_spec=pltpu.PrefetchScalarGridSpec(
            num_scalar_prefetch=1,
            grid=(1,),
            in_specs=[
                pl.BlockSpec((rows, D), mine),
                pl.BlockSpec((rows, D), whole),
                pl.BlockSpec((rows, SIDE), whole),
                pl.BlockSpec((rows, D + SIDE), whole),
                pl.BlockSpec((8, D), whole),
                pl.BlockSpec((D, SIDE), whole),
            ]
            + [pl.BlockSpec((rows, D + SIDE), whole)] * nt,
            out_specs=[
                pl.BlockSpec((rows, D), whole),
                pl.BlockSpec((rows, D), whole),
                pl.BlockSpec((D, SIDE), whole),
            ],
        ),
        compiler_params=params(),
        cost_estimate=cost(4 * rows * D * SIDE, 8 * rows * D),
        name="norm_back",
    )(pos, cotangent, h, gates, normed, gains, side, *parts)


def input_gradient(pos, tokens, parts, dh, gains, nt):
    rows = dh.shape[0]

    def kernel(pos_ref, x_ref, dh_ref, gain_ref, *refs):
        part_refs, out_ref = refs[:nt], refs[nt]
        total = part_refs[0][...].astype(F32)
        for ref in part_refs[1:]:
            total = total + ref[...].astype(F32)
        x = x_ref[...].astype(F32)
        out_ref[...] = (
            dh_ref[...] + norm_backward(x, rms_inverse(x), gain_ref[0:1], total)
        ).astype(BF16)

    whole = lambda i, pos: (0, 0)
    return pl.pallas_call(
        kernel,
        out_shape=shape((rows, D), BF16),
        grid_spec=pltpu.PrefetchScalarGridSpec(
            num_scalar_prefetch=1,
            grid=(1,),
            in_specs=[
                pl.BlockSpec((rows, D), lambda i, pos: (pos[1], 0)),
                pl.BlockSpec((rows, D), whole),
                pl.BlockSpec((8, D), whole),
            ]
            + [pl.BlockSpec((rows, D), whole)] * nt,
            out_specs=pl.BlockSpec((rows, D), whole),
        ),
        compiler_params=params(),
        name="input_gradient",
    )(pos, tokens, dh, gains, *parts)


def place_rows(pos, parts):
    rows, features = parts[0].shape
    nt = len(parts)

    def kernel(pos_ref, *refs):
        for d in range(nt):
            start = pl.multiple_of((pos_ref[1] ^ d) * rows, 16)
            refs[nt][pl.ds(start, rows), :] = refs[d][...]

    return pl.pallas_call(
        kernel,
        out_shape=shape((rows * nt, features), parts[0].dtype),
        in_specs=[SMEM] + [VMEM] * nt,
        out_specs=VMEM,
        compiler_params=params(),
        name="place_rows",
    )(pos, *parts)


def spread_rows(slots, source, target, pair, number, cut):
    for begin in range(0, source.shape[2], cut):
        span = slice(begin, min(begin + cut, source.shape[2]))
        two = [dot_tn(slots[2 * pair + k], source[2 * pair + k, :, span]) for k in range(2)]
        for e in range(number):
            joined = jnp.concatenate([rows[e * CAP : (e + 1) * CAP] for rows in two], axis=0)
            target(e, span, joined)


def sum_rows(slots, results, target, pair, number, total, cut):
    at = slice(pair * 2 * CAP, (pair + 1) * 2 * CAP)
    for begin in range(0, total, cut):
        span = slice(begin, min(begin + cut, total))
        blocks = [results[e, at, span].astype(F32) for e in range(number)]
        for k in range(2):
            rows = jnp.concatenate([b[k * CAP : (k + 1) * CAP] for b in blocks], axis=0)
            target[2 * pair + k, :, span] = dot(slots[2 * pair + k], rows.astype(BF16)).astype(BF16)


def route_cotangent(pos, pieces, weights, nf, top):
    number, _, _, width = weights.shape
    length = sum(part.shape[0] for index, _, part in pieces if index == 0)
    slots = number * CAP
    count = len(pieces)

    def kernel(pos_ref, w_ref, *refs):
        piece_refs, (slot_ref, rows_ref, down_ref, cot, spread, sems) = refs[:count], refs[count:]
        e = pl.program_id(0)
        f = pos_ref[0]

        @pl.when(e == 0)
        def _():
            copies = start_fetch(
                pieces, piece_refs, lambda i, row, n: cot.at[i, pl.ds(row, n), :], sems
            )
            column = lanes((length, slots))
            expert = jnp.zeros((length, slots), jnp.int32)
            for k in range(1, number):
                expert = expert + (column >= k * CAP).astype(jnp.int32)
            rank = (column - expert * CAP + 1).astype(F32)
            expert = (expert + f * number).astype(F32)
            lower = (
                lax.broadcasted_iota(jnp.int32, (length, length), 0) >= lanes((length, length))
            ).astype(F32).astype(BF16)
            for copy in copies:
                copy.wait()
            for s in range(nf):
                named = cot[s, :, D:].astype(F32)
                hit = named[:, 0:1] == expert
                for j in range(1, top):
                    hit = hit | (named[:, j : j + 1] == expert)
                hit = jnp.where(hit, 1.0, 0.0)
                so_far = dot(lower, hit.astype(BF16))
                slot_ref[s] = jnp.where((so_far == rank) & (hit > 0.0), 1.0, 0.0).astype(BF16)
            for pair in range(nf // 2):
                at = slice(pair * 2 * CAP, (pair + 1) * 2 * CAP)

                def put(k, span, rows):
                    spread[k, at, span] = rows.astype(BF16)

                spread_rows(slot_ref, cot.at[:, :, :D], put, pair, number, 512)

        rows = spread[e]
        rows_ref[0] = rows
        down_ref[0] = dot(rows, w_ref[0, 0])

    return pl.pallas_call(
        kernel,
        out_shape=[
            shape((nf, length, slots), BF16),
            shape((number, nf * CAP, D), BF16),
            shape((number, nf * CAP, width), F32),
        ],
        grid_spec=pltpu.PrefetchScalarGridSpec(
            num_scalar_prefetch=1,
            grid=(number,),
            in_specs=[pl.BlockSpec((1, 1, D, width), lambda e, pos: (e, 2, 0, 0))] + [HBM] * count,
            out_specs=[
                pl.BlockSpec((nf, length, slots), lambda e, pos: (0, 0, 0)),
                pl.BlockSpec((1, nf * CAP, D), lambda e, pos: (e, 0, 0)),
                pl.BlockSpec((1, nf * CAP, width), lambda e, pos: (e, 0, 0)),
            ],
            scratch_shapes=[
                pltpu.VMEM((nf, length, D + SIDE), BF16),
                pltpu.VMEM((number, nf * CAP, D), BF16),
                pltpu.SemaphoreType.DMA((count,)),
            ],
        ),
        compiler_params=params(),
        cost_estimate=cost(4 * slots * nf * D * 256, 8 * slots * nf * D),
        name="route_cotangent",
    )(pos, weights, *[part for _, _, part in pieces])


def run_experts(pos, pieces, slot_table, down, weights, nf):
    number, _, _, width = weights.shape
    length, slots = slot_table.shape[1:]
    filled = nf * CAP
    count = len(pieces)

    def kernel(pos_ref, slot_ref, down_ref, gate_w, up_w, *refs):
        piece_refs, refs = refs[:count], refs[count:]
        rows_ref, dg_ref, du_ref, hidden_ref, keep_ref, send_ref = refs[:6]
        wide, spread, gates, results, sems, out_sems = refs[6:]
        e = pl.program_id(0)
        f = pos_ref[0]

        @pl.when(e == 0)
        def _():
            copies = start_fetch(
                pieces, piece_refs, lambda i, row, n: wide.at[i, pl.ds(row, n), :], sems
            )
            for copy in copies:
                copy.wait()
            for pair in range(nf // 2):
                at = slice(pair * 2 * CAP, (pair + 1) * 2 * CAP)

                def put(k, span, rows):
                    if span.start < D:
                        spread[k, at, span] = rows.astype(BF16)
                    else:
                        lane = lanes((2 * CAP, SIDE))
                        own = f * number + k
                        gate = jnp.where((lane == own) | (lane == own + EXPERTS), rows, 0.0)
                        gates[k, at, :] = jnp.broadcast_to(
                            jnp.sum(gate, axis=-1, keepdims=True), (2 * CAP, SIDE)
                        )

                spread_rows(slot_ref, wide, put, pair, number, 512)

        rows = spread[e]
        rows_ref[0] = rows
        first, second = gate_w[0, 0], up_w[0, 0]
        gate_pre = dot(rows, first)
        up_pre = dot(rows, second)
        gate = gates[e][:, 0:1]
        sigma = jax.nn.sigmoid(gate_pre)
        swish = gate_pre * sigma
        hidden = (swish * up_pre).astype(BF16).astype(F32)
        hidden_ref[0] = (gate * hidden).astype(BF16)
        unscaled = down_ref[0]
        grad_hidden = gate * unscaled
        dg = (grad_hidden * up_pre * sigma * (1.0 + gate_pre * (1.0 - sigma))).astype(BF16)
        du = (grad_hidden * swish).astype(BF16)
        dg_ref[0] = dg
        du_ref[0] = du
        results[e, :, :D] = (dot_nt(dg, first) + dot_nt(du, second)).astype(BF16)
        pair_grad = jnp.sum(unscaled * hidden, axis=-1, keepdims=True)
        high = pair_grad.astype(BF16).astype(F32)
        lane = lanes((filled, SIDE))
        own = f * number + e
        results[e, :, D:] = jnp.where(
            lane == own, high, jnp.where(lane == own + EXPERTS, pair_grad - high, 0.0)
        ).astype(BF16)

        @pl.when(e == number - 1)
        def _():
            copies = []
            for pair in range(nf // 2):
                sum_rows(slot_ref, results, wide, pair, number, D + SIDE, 512)
                for k, to in enumerate((keep_ref, send_ref)):
                    index = 2 * pair + k
                    copy = pltpu.make_async_copy(wide.at[index], to.at[pair], out_sems.at[index])
                    copy.start()
                    copies.append(copy)
            for copy in copies:
                copy.wait()

    return pl.pallas_call(
        kernel,
        out_shape=[
            shape((number, filled, D), BF16),
            shape((number, filled, width), BF16),
            shape((number, filled, width), BF16),
            shape((number, filled, width), BF16),
            shape((nf // 2, length, D + SIDE), BF16),
            shape((nf // 2, length, D + SIDE), BF16),
        ],
        grid_spec=pltpu.PrefetchScalarGridSpec(
            num_scalar_prefetch=1,
            grid=(number,),
            in_specs=[
                pl.BlockSpec((nf, length, slots), lambda e, pos: (0, 0, 0)),
                pl.BlockSpec((1, filled, width), lambda e, pos: (e, 0, 0)),
                pl.BlockSpec((1, 1, D, width), lambda e, pos: (e, 0, 0, 0)),
                pl.BlockSpec((1, 1, D, width), lambda e, pos: (e, 1, 0, 0)),
            ]
            + [HBM] * count,
            out_specs=[
                pl.BlockSpec((1, filled, D), lambda e, pos: (e, 0, 0)),
                pl.BlockSpec((1, filled, width), lambda e, pos: (e, 0, 0)),
                pl.BlockSpec((1, filled, width), lambda e, pos: (e, 0, 0)),
                pl.BlockSpec((1, filled, width), lambda e, pos: (e, 0, 0)),
                HBM,
                HBM,
            ],
            scratch_shapes=[
                pltpu.VMEM((nf, length, D + SIDE), BF16),
                pltpu.VMEM((number, filled, D), BF16),
                pltpu.VMEM((number, filled, SIDE), F32),
                pltpu.VMEM((number, filled, D + SIDE), BF16),
                pltpu.SemaphoreType.DMA((count,)),
                pltpu.SemaphoreType.DMA((nf,)),
            ],
        ),
        compiler_params=params(),
        cost_estimate=cost(12 * slots * nf * D * 256, 8 * slots * nf * D),
        name="run_experts",
    )(pos, slot_table, down, weights, weights, *[part for _, _, part in pieces])


def expert_outputs(slot_table, hidden, weights):
    number, filled, width = hidden.shape
    nf, length, slots = slot_table.shape

    def kernel(slot_ref, hidden_ref, w_ref, keep_ref, send_ref, results, out, sems):
        e = pl.program_id(0)
        results[e] = dot_nt(hidden_ref[0], w_ref[0, 0]).astype(BF16)

        @pl.when(e == number - 1)
        def _():
            copies = []
            for pair in range(nf // 2):
                sum_rows(slot_ref, results, out, pair, number, D, 512)
                for k, to in enumerate((keep_ref, send_ref)):
                    index = 2 * pair + k
                    copy = pltpu.make_async_copy(out.at[index], to.at[pair], sems.at[index])
                    copy.start()
                    copies.append(copy)
            for copy in copies:
                copy.wait()

    return pl.pallas_call(
        kernel,
        out_shape=[shape((nf // 2, length, D), BF16)] * 2,
        grid=(number,),
        in_specs=[
            pl.BlockSpec((nf, length, slots), lambda e: (0, 0, 0)),
            pl.BlockSpec((1, filled, width), lambda e: (e, 0, 0)),
            pl.BlockSpec((1, 1, D, width), lambda e: (e, 2, 0, 0)),
        ],
        out_specs=[HBM, HBM],
        scratch_shapes=[
            pltpu.VMEM((number, filled, D), BF16),
            pltpu.VMEM((nf, length, D), BF16),
            pltpu.SemaphoreType.DMA((nf,)),
        ],
        compiler_params=params(),
        cost_estimate=cost(4 * slots * nf * D * 256, 8 * slots * nf * D),
        name="expert_outputs",
    )(slot_table, hidden, weights)


def expert_gradients(rows, grad_rows, dg, du, hidden):
    number, filled, width = dg.shape

    def kernel(rows_ref, grad_ref, dg_ref, du_ref, hidden_ref, out_ref):
        rows = rows_ref[0]
        out_ref[0, 0] = dot_tn(rows, dg_ref[0])
        out_ref[0, 1] = dot_tn(rows, du_ref[0])
        out_ref[0, 2] = dot_tn(grad_ref[0], hidden_ref[0])

    tall = pl.BlockSpec((1, filled, D), lambda e: (e, 0, 0))
    thin = pl.BlockSpec((1, filled, width), lambda e: (e, 0, 0))
    return pl.pallas_call(
        kernel,
        out_shape=shape((number, 3, D, width), F32),
        grid=(number,),
        in_specs=[tall, tall, thin, thin, thin],
        out_specs=pl.BlockSpec((1, 3, D, width), lambda e: (e, 0, 0, 0)),
        compiler_params=params(),
        cost_estimate=cost(6 * number * filled * D * width, 12 * number * D * width),
        name="expert_gradients",
    )(rows, grad_rows, dg, du, hidden)


def on_device(
    nf,
    nt,
    tokens,
    cotangent,
    routes,
    w_query,
    w_key,
    w_value,
    w_output,
    w_router,
    attn_gain,
    ffn_gain,
    query_gain,
    key_gain,
    expert_weights,
):
    length = tokens.shape[0]
    rows = length // nt
    block = D // nf
    group = query_gain.shape[0]
    top = routes.shape[1]
    f = lax.axis_index("fsdp").astype(jnp.int32)
    t = lax.axis_index("tensor").astype(jnp.int32)
    pos = jnp.stack([f, t])

    def placed(gain):
        return lax.dynamic_update_slice(jnp.zeros((block,), BF16), gain, (f * group,))[:, None]

    packed = jnp.concatenate(
        [
            w_query,
            w_key,
            w_value,
            w_output,
            w_router,
            attn_gain[:, None],
            ffn_gain[:, None],
            placed(query_gain),
            placed(key_gain),
            jnp.zeros((block, SIDE - EXPERTS - 4), BF16),
        ],
        axis=1,
    )
    weight_pieces = plane_gather(packed, nf)

    wide_cot = jnp.concatenate(
        [cotangent, routes.astype(BF16), jnp.zeros((length, SIDE - top), BF16)], axis=1
    )
    wide_cot = jnp.concatenate(
        [lax.dynamic_slice_in_dim(wide_cot, (t ^ d) * rows, rows, 0) for d in range(nt)], axis=0
    )
    cot_pieces = plane_gather(wide_cot, nf)

    position = jnp.arange(length, dtype=F32)[:, None]
    inverse = ROPE_BASE ** (-jnp.arange(HD // 2, dtype=F32) / (HD // 2))
    angles = position * inverse[None, :]
    cosine = jnp.concatenate([jnp.cos(angles)] * 2, axis=1)
    sine = jnp.concatenate([-jnp.sin(angles), jnp.sin(angles)], axis=1)

    saved, parts = attend_forward(pos, tokens, cosine, sine, weight_pieces, nf, nt)
    normed_one, _, _, _, _, attended, side, gains, _ = saved
    parts = [parts[0]] + [swap(parts[d], "tensor", nt, d) for d in range(1, nt)]
    h, normed_two, gates = norm_and_route(pos, tokens, routes, parts, gains, side, nt)

    others = [swap(normed_two, "tensor", nt, d) for d in range(1, nt)]
    n2_pieces = plane_gather(normed_two, nf) + [
        (index, row + rows, part)
        for index, row, part in plane_gather(jnp.concatenate(others, axis=0), nf)
    ]
    slot_table, cot_rows, down = route_cotangent(pos, cot_pieces, expert_weights, nf, top)
    n2_rows, dg, du, hidden, keep, send = run_experts(
        pos, n2_pieces, slot_table, down, expert_weights, nf
    )

    def over_tensor(total):
        low = total.astype(BF16)
        return [low[:rows]] + [
            swap(low[d * rows : (d + 1) * rows], "tensor", nt, d) for d in range(1, nt)
        ]

    grad_parts = over_tensor(plane_reduce(keep, send, nf))
    grad_experts = expert_gradients(n2_rows, cot_rows, dg, du, hidden)
    out_keep, out_send = expert_outputs(slot_table, hidden, expert_weights)
    dh, db, side_grads = norm_back(
        pos, cotangent, grad_parts, h, gates, normed_two, gains, side, nt
    )
    db_parts = [db] + [swap(db, "tensor", nt, d) for d in range(1, nt)]

    moe_parts = over_tensor(plane_reduce(out_keep, out_send, nf))
    layer_rows = h
    for part in moe_parts:
        layer_rows = layer_rows + part.astype(F32)
    layer_out = lax.all_gather(layer_rows.astype(BF16), "tensor", axis=0, tiled=True)

    (dqkv, grad_branch, attn_row, head_rows), parts = attend_backward(
        pos, db_parts, weight_pieces, saved, tokens, cosine, sine, nf, nt
    )
    parts = [parts[0]] + [swap(parts[d], "tensor", nt, d) for d in range(1, nt)]
    keep, send = projection_gradients(
        pos, normed_one, dqkv, grad_branch, attended, side_grads, attn_row, head_rows, group, nf
    )
    weight_grads = plane_reduce(keep, send, nf)
    token_rows = input_gradient(pos, tokens, parts, dh, gains, nt)
    grad_tokens = place_rows(
        pos, [token_rows] + [swap(token_rows, "tensor", nt, d) for d in range(1, nt)]
    )
    width = attended.shape[1]
    small = lax.psum(weight_grads[:, 4 * width :], "tensor")
    return (
        layer_out,
        grad_tokens,
        weight_grads[:, :width],
        weight_grads[:, width : 2 * width],
        weight_grads[:, 2 * width : 3 * width],
        weight_grads[:, 3 * width : 4 * width],
        small[:, :EXPERTS],
        small[:, EXPERTS + 1],
        small[:, EXPERTS],
        small[:group, EXPERTS + 2],
        small[:group, EXPERTS + 3],
        grad_experts,
    )


def solution(mesh):
    nf, nt = mesh.shape["fsdp"], mesh.shape["tensor"]
    rows, both, line = P("fsdp", None), P("fsdp", "tensor"), P("fsdp")
    experts = P("fsdp", None, None, "tensor")
    return jax.shard_map(
        functools.partial(on_device, nf, nt),
        mesh=mesh,
        in_specs=(rows, rows, rows, both, both, both, both, rows, line, line, line, line, experts),
        out_specs=(rows, rows, both, both, both, both, rows, line, line, line, line, experts),
        check_vma=False,
    )
```

time: 1690 us -> 591 us (0.35)
  blocking collectives: 516 us -> 0 us
  waiting for transfers between devices: 512 us -> 292 us
  local copies, waits for them, and re-layouts: 238 us -> 27.6 us
  other arithmetic: 221 us -> 27.5 us
  matrix products: 163 us -> 0 us
  Pallas kernels: 0 us -> 144 us
  starting transfers between devices: 13.4 us -> 75.3 us
    ppermute x0 -> x72, waiting for transfers between devices: none -> 260 us  [swap(): return lax.ppermute(block, axis, [(i, i ^ step) for i in range(size)])]
    all_to_all x2 -> x0, blocking collectives: 243 us -> none  [the longest x1 123 us: on_device(): lax.all_to_all(routed_rows, 'fsdp', split_axis=0, concat_axis=1, tiled=True)]
    all_gather x3 -> x0, blocking collectives: 224 us -> none  [the longest x1 208 us: on_device(): lax.all_gather(w_router, 'fsdp', axis=0, tiled=True)]
    all_to_all x2 -> x0, waiting for transfers between devices: 206 us -> none  [the longest x1 206 us: on_device(): lax.all_to_all(input_part, 'fsdp', split_axis=1, concat_axis=0, tiled=True)]
    dot_general x30 -> x0, matrix products: 163 us -> none  [the longest x1 18.9 us: expert_backward(): jnp.einsum('erf,edf->erd', grad_gate, weights[:, 0], preferred_element_ty...]
    pallas_call x0 -> x11, Pallas kernels: none -> 144 us  [the longest x1 34 us: run_experts(): pl.pallas_call(kernel, out_shape=[shape((number, filled, D), BF16), shape...]
    reduce_scatter x5 -> x0, waiting for transfers between devices: 110 us -> none  [the longest x1 42.9 us: on_device(): lax.psum_scatter(grad_value.astype(jnp.bfloat16), 'fsdp', scatter_dimensi...]
    psum x4 -> x1, waiting for transfers between devices: 117 us -> 32.3 us  [on_device(): small = lax.psum(weight_grads[:, 4 * width:], 'tensor')]
  transfers between devices with their start and end apart: 15 -> 74, of which waited for: 10 -> 29; matrix products, arithmetic and copies ran while one was open for 20% -> 4% of each run, Pallas kernels for 0% -> 19%
where the time goes in v1:
time: 591 us; the launch traced here: 582 us
  waiting for transfers between devices  292 us (49%)
  Pallas kernels  144 us (24%)
  starting transfers between devices  75.3 us (13%)
  local copies, waits for them, and re-layouts  27.6 us (5%)
  other arithmetic  27.5 us (5%)
  between operations  15.1 us (3%)
    ppermute x72, waiting for transfers between devices, swap(): return lax.ppermute(block, axis, [(i, i ^ step) for i in range(size)])  260 us
    ppermute x72, starting transfers between devices, swap(): return lax.ppermute(block, axis, [(i, i ^ step) for i in range(size)])  75.3 us
    pallas_call x1, Pallas kernels, run_experts(): pl.pallas_call(kernel, out_shape=[shape((number, filled, D), BF16), shape...  34 us
    psum x1, waiting for transfers between devices, on_device(): small = lax.psum(weight_grads[:, 4 * width:], 'tensor')  32.3 us
    pallas_call x1, Pallas kernels, expert_gradients(): pl.pallas_call(kernel, out_shape=shape((number, 3, D, width), F32), grid=...  28.6 us
    pallas_call x1, Pallas kernels, route_cotangent(): pl.pallas_call(kernel, out_shape=[shape((nf, length, slots), BF16), shape...  22.6 us
    pallas_call x1, Pallas kernels, expert_outputs(): pl.pallas_call(kernel, out_shape=[shape((nf // 2, length, D), BF16)] * 2,...  14.7 us
    unnamed x112, local copies, waits for them, and re-layouts  12.5 us
  transfers between devices with their start and end apart: 74, of which 29 were waited for; matrix products, arithmetic and copies ran while one was open for 4% of the time, Pallas kernels for 19%

profile of v1, /device:TPU:0, one launch (start us, length us, event | category | flops | bytes accessed | tf_op | source)
XLA Modules:
  0.0 581.6 jit_solution(12699641553716287920)
XLA Ops:
  18.2 23.1 %collective-permute-done.1.refs_2_.refs_6_ = bf16[256,2176]{1,0:T(8,128)(2,1)S(1)} collective-permute-done((bf16[256,2176]{1,0:T(8,128)(2,1)S(1)}, bf16[256,2176]{1,0:T(8,128)(2,1)S(1)}, u32[]{:S(2)}, u32[]{:S(2)}) %collective-permute-start.1) | collective-permute-done | bytes 1114144 | tf_op jit(solution)/shard_map/ppermute | solution.py:70
  49.3 7.1 %collective-permute-done.2.refs_3_.refs_7_ = bf16[128,2176]{1,0:T(8,128)(2,1)} collective-permute-done((bf16[128,2176]{1,0:T(8,128)(2,1)}, bf16[128,2176]{1,0:T(8,128)(2,1)}, u32[]{:S(2)}, u32[]{:S(2)}) %collective-permute-start.2) | collective-permute-done | bytes 557088 | tf_op jit(solution)/shard_map/ppermute | solution.py:70
  58.9 3.7 collective-permute-done.3.refs_4_.refs_8_
  67.1 10.3 %attend_forward.1 = (bf16[256,2048]{1,0:T(8,128)(2,1)}, f32[256,1024]{1,0:T(8,128)}, bf16[256,1024]{1,0:T(8,128)(2,1)}, bf16[256,512]{1,0:T(8,128)(2,1)}, f32[4,...) custom-call(s32[2]{0:T(128)} %pad_add_fusion.pos_ref, ...), custom_call_target="tpu_custom_call" | custom-call | flops 2147483648 | bytes 8912896 | tf_op jit(solution)/shard_map/attend_forward/pallas_call | solution.py:176
  82.7 8.6 %collective-permute-done.9.refs_1_ = bf16[64,2048]{1,0:T(8,128)(2,1)S(1)} collective-permute-done((bf16[64,2048]{1,0:T(8,128)(2,1)}, bf16[64,2048]{1,0:T(8,128)(2,1)S(1)}, u32[]{:S(2)}, u32[]{:S(2)}) %collective-permute-start.9) | collective-permute-done | bytes 262176 | tf_op jit(solution)/shard_map/ppermute | solution.py:70
  91.3 9.5 %collective-permute-done.10.refs_2_ = bf16[64,2048]{1,0:T(8,128)(2,1)S(1)} collective-permute-done((bf16[64,2048]{1,0:T(8,128)(2,1)}, bf16[64,2048]{1,0:T(8,128)(2,1)S(1)}, u32[]{:S(2)}, u32[]{:S(2)}) %collective-permute-start.10) | collective-permute-done | bytes 262176 | tf_op jit(solution)/shard_map/ppermute | solution.py:70
  105.2 5.1 collective-permute-start.30
  119.8 4.0 collective-permute-done.14.refs_3_
  125.3 14.2 %collective-permute-done.31 = bf16[64,2176]{1,0:T(8,128)(2,1)S(1)} collective-permute-done((bf16[64,2176]{1,0:T(8,128)(2,1)S(1)}, bf16[64,2176]{1,0:T(8,128)(2,1)S(1)}, u32[]{:S(2)}, u32[]{:S(2)}) %collective-permute-start.31) | collective-permute-done | bytes 278560 | tf_op jit(solution)/shard_map/ppermute | solution.py:70
  142.3 24.3 %collective-permute-done.22.refs_2_ = bf16[64,2176]{1,0:T(8,128)(2,1)S(1)} collective-permute-done((bf16[64,2176]{1,0:T(8,128)(2,1)S(1)}, bf16[64,2176]{1,0:T(8,128)(2,1)S(1)}, u32[]{:S(2)}, u32[]{:S(2)}) %collective-permute-start.22) | collective-permute-done | bytes 278560 | tf_op jit(solution)/shard_map/ppermute | solution.py:70
  167.2 7.7 %collective-permute-done.21.refs_1_ = bf16[64,2176]{1,0:T(8,128)(2,1)S(1)} collective-permute-done((bf16[64,2176]{1,0:T(8,128)(2,1)S(1)}, bf16[64,2176]{1,0:T(8,128)(2,1)S(1)}, u32[]{:S(2)}, u32[]{:S(2)}) %collective-permute-start.21) | collective-permute-done | bytes 278560 | tf_op jit(solution)/shard_map/ppermute | solution.py:70
  185.2 8.2 %collective-permute-done.35.refs_13_ = bf16[96,2176]{1,0:T(8,128)(2,1)S(1)} collective-permute-done((bf16[96,2176]{1,0:T(8,128)(2,1)S(1)}, bf16[96,2176]{1,0:T(8,128)(2,1)S(1)}, u32[]{:S(2)}, u32[]{:S(2)}) %collective-permute-start.35) | collective-permute-done | bytes 417824 | tf_op jit(solution)/shard_map/ppermute | solution.py:70
  194.9 22.6 %route_cotangent.1 = (bf16[8,256,320]{2,1,0:T(8,128)(2,1)}, bf16[8,320,2048]{2,1,0:T(8,128)(2,1)}, f32[8,320,256]{2,1,0:T(8,128)}) custom-call(s32[2]{0:T(128)} %pad_add_fusion.pos_ref, bf16[8,3,2048,256]{3,2,1,0:T(8,128)(2,1)} %w_ref.3, bf16[256,2176]{1,0:T(8,128)(2,1)} %pad_maximum_fusion.refs_0_, bf16[256,2176]{1,0:T(8,128)(2,1)} %collective-permute-done.12.refs_1_, ...), custom_call_target="tpu_custom_call" | custom-call | flops 5368709120 | bytes 41943040 | tf_op jit(solution)/shard_map/route_cotangent/pallas_call | solution.py:559
  218.4 34.0 %run_experts.1 = (bf16[8,320,2048]{2,1,0:T(8,128)(2,1)}, bf16[8,320,256]{2,1,0:T(8,128)(2,1)}, bf16[8,320,256]{2,1,0:T(8,128)(2,1)}, bf16[8,320,256]{2,1,0:T(8,1...) custom-call(s32[2]{0:T(128)} %pad_add_fusion.pos_ref, ...), custom_call_target="tpu_custom_call" | custom-call | flops 16106127360 | bytes 41943040 | tf_op jit(solution)/shard_map/run_experts/pallas_call | solution.py:661
  253.0 7.4 %collective-permute-done.50 = bf16[4,256,2176]{2,1,0:T(8,128)(2,1)S(1)} collective-permute-done((bf16[4,256,2176]{2,1,0:T(8,128)(2,1)}, bf16[4,256,2176]{2,1,0:T(8,128)(2,1)S(1)}, u32[]{:S(2)}, u32[]{:S(2)}) %collective-permute-start.50) | collective-permute-done | bytes 4456480 | tf_op jit(solution)/shard_map/ppermute | solution.py:70
  260.4 3.7 add_convert_fusion.8
  267.0 24.2 %collective-permute-done.51 = bf16[2,128,2176]{2,1,0:T(8,128)(2,1)S(1)} collective-permute-done((bf16[2,128,2176]{2,1,0:T(8,128)(2,1)S(1)}, bf16[2,128,2176]{2,1,0:T(8,128)(2,1)S(1)}, u32[]{:S(2)}, u32[]{:S(2)}) %collective-permute-start.51) | collective-permute-done | bytes 1114144 | tf_op jit(solution)/shard_map/ppermute | solution.py:70
  296.3 14.7 %expert_outputs.1 = (bf16[4,256,2048]{2,1,0:T(8,128)(2,1)}, bf16[4,256,2048]{2,1,0:T(8,128)(2,1)}) custom-call(bf16[8,256,320]{2,1,0:T(8,128)(2,1)} %get-tuple-element.59.slot_ref, bf16[8,320,256]{2,1,0:T(8,128)(2,1)} %get-tuple-element.62.hidden_ref, bf16[8,3,2048,256]{3,2,1,0:T(8,128)(2,1)} %w_ref.3), custom_call_target="tpu_custom_call" | custom-call | flops 5368709120 | bytes 41943040 | tf_op jit(solution)/shard_map/expert_outputs/pallas_call | solution.py:725
  318.7 6.3 %collective-permute-done.57.refs_3_ = bf16[64,2176]{1,0:T(8,128)(2,1)S(1)} collective-permute-done((bf16[64,2176]{1,0:T(8,128)(2,1)S(1)}, bf16[64,2176]{1,0:T(8,128)(2,1)S(1)}, u32[]{:S(2)}, u32[]{:S(2)}) %collective-permute-start.57) | collective-permute-done | bytes 278560 | tf_op jit(solution)/shard_map/ppermute | solution.py:70
  324.9 14.6 %collective-permute-done.56.refs_2_ = bf16[64,2176]{1,0:T(8,128)(2,1)S(1)} collective-permute-done((bf16[64,2176]{1,0:T(8,128)(2,1)S(1)}, bf16[64,2176]{1,0:T(8,128)(2,1)S(1)}, u32[]{:S(2)}, u32[]{:S(2)}) %collective-permute-start.56) | collective-permute-done | bytes 278560 | tf_op jit(solution)/shard_map/ppermute | solution.py:70
  340.4 4.4 norm_back.1
  349.2 6.9 %collective-permute-done.60.refs_3_ = bf16[64,2048]{1,0:T(8,128)(2,1)S(1)} collective-permute-done((bf16[64,2048]{1,0:T(8,128)(2,1)}, bf16[64,2048]{1,0:T(8,128)(2,1)S(1)}, u32[]{:S(2)}, u32[]{:S(2)}) %collective-permute-start.60) | collective-permute-done | bytes 262176 | tf_op jit(solution)/shard_map/ppermute | solution.py:70
  356.1 11.6 %collective-permute-done.59.refs_2_ = bf16[64,2048]{1,0:T(8,128)(2,1)S(1)} collective-permute-done((bf16[64,2048]{1,0:T(8,128)(2,1)}, bf16[64,2048]{1,0:T(8,128)(2,1)S(1)}, u32[]{:S(2)}, u32[]{:S(2)}) %collective-permute-start.59) | collective-permute-done | bytes 262176 | tf_op jit(solution)/shard_map/ppermute | solution.py:70
  368.5 12.2 %attend_backward.1 = (bf16[256,1536]{1,0:T(8,128)(2,1)}, bf16[256,2048]{1,0:T(8,128)(2,1)}, f32[8,2048]{1,0:T(8,128)}, f32[8,128]{1,0:T(8,128)}, bf16[64,2048]{1...) custom-call(s32[2]{0:T(128)} %pad_add_fusion.pos_ref, ...), custom_call_target="tpu_custom_call" | custom-call | flops 2147483648 | bytes 8912896 | tf_op jit(solution)/shard_map/attend_backward/pallas_call | solution.py:270
  380.8 7.9 %projection_gradients.1 = (bf16[4,256,2176]{2,1,0:T(8,128)(2,1)}, bf16[4,256,2176]{2,1,0:T(8,128)(2,1)}) custom-call(s32[2]{0:T(128)} %pad_add_fusion.pos_ref, bf16[256,2048]{1,0:T(8,128)(2,1)} %get-tuple-element.79.n1_ref, bf16[256,1536]{1,0:T(8,128)(2,1)} %get-tuple-element.80.dqkv_ref, bf16[256,2048]{1,0:T(8,128)(2,1)} %get-tuple-element.81.db_ref, ...), custom_call_target="tpu_custom_call" | custom-call | flops 2147483648 | bytes 8912896 | tf_op jit(solution)/shard_map/projection_gradients/pallas_call | solution.py:325
  393.5 23.9 %collective-permute-done.46 = bf16[2,128,2048]{2,1,0:T(8,128)(2,1)S(1)} collective-permute-done((bf16[2,128,2048]{2,1,0:T(8,128)(2,1)S(1)}, bf16[2,128,2048]{2,1,0:T(8,128)(2,1)S(1)}, u32[]{:S(2)}, u32[]{:S(2)}) %collective-permute-start.46) | collective-permute-done | bytes 1048608 | tf_op jit(solution)/shard_map/ppermute | solution.py:70
  422.1 10.7 %collective-permute-done.44 = bf16[128,2048]{1,0:T(8,128)(2,1)S(1)} collective-permute-done((bf16[128,2048]{1,0:T(8,128)(2,1)S(1)}, bf16[128,2048]{1,0:T(8,128)(2,1)S(1)}, u32[]{:S(2)}, u32[]{:S(2)}) %collective-permute-start.44) | collective-permute-done | bytes 524320 | tf_op jit(solution)/shard_map/ppermute | solution.py:70
  445.4 15.0 %collective-permute-done.48 = bf16[64,2048]{1,0:T(8,128)(2,1)S(1)} collective-permute-done((bf16[64,2048]{1,0:T(8,128)(2,1)S(1)}, bf16[64,2048]{1,0:T(8,128)(2,1)S(1)}, u32[]{:S(2)}, u32[]{:S(2)}) %collective-permute-start.48) | collective-permute-done | bytes 262176 | tf_op jit(solution)/shard_map/ppermute | solution.py:70
  463.8 19.1 %collective-permute-done.62.refs_2_ = bf16[64,2048]{1,0:T(8,128)(2,1)} collective-permute-done((bf16[64,2048]{1,0:T(8,128)(2,1)}, bf16[64,2048]{1,0:T(8,128)(2,1)}, u32[]{:S(2)}, u32[]{:S(2)}) %collective-permute-start.62) | collective-permute-done | bytes 262176 | tf_op jit(solution)/shard_map/ppermute | solution.py:70
  488.7 4.0 collective-permute-start.65
  497.6 28.6 %expert_gradients.1 = f32[8,3,2048,256]{3,2,1,0:T(8,128)} custom-call(bf16[8,320,2048]{2,1,0:T(8,128)(2,1)} %get-tuple-element.88.rows_ref, bf16[8,320,2048]{2,1,0:T(8,128)(2,1)} %get-tuple-element.89.grad_ref, bf16[8,320,256]{2,1,0:T(8,128)(2,1)} %get-tuple-element.90.dg_ref, bf16[8,320,256]{2,1,0:T(8,128)(2,1)} %get-tuple-element.91.du_ref, ...), custom_call_target="tpu_custom_call" | custom-call | flops 8053063680 | bytes 50331648 | tf_op jit(solution)/shard_map/expert_gradients/pallas_call | solution.py:757
  536.4 32.3 %all-reduce.2.cloned.1.call-done = f32[256,128]{1,0:T(8,128)} async-done(((f32[256,128]{1,0:T(8,128)}), f32[256,128]{1,0:T(8,128)}) %all-reduce.2.cloned.1.call-update) | async-done | bytes 131088 | tf_op jit(solution)/shard_map/psum | solution.py:877
  (295 shorter events, 136.4 us)
Async XLA Ops:
  7.2 523.7 %all-gather.2.cloned.1.call-start = ((), (), s32[]{:S(2)}) async-start(), calls=%async_computation | async-start | bytes 1310720 | tf_op jit(solution)/shard_map/all_gather | solution.py:862
  13.7 27.6 %collective-permute-start.1 = (bf16[256,2176]{1,0:T(8,128)(2,1)S(1)}, bf16[256,2176]{1,0:T(8,128)(2,1)S(1)}, u32[]{:S(2)}, u32[]{:S(2)}) collective-permute-start(bf16[256,2176]{1,0:T(8,128)(2,1)S(1)} %concatenate.27.refs_0_.refs_4_), channel_id=1, source_target_pairs={{0,16},{4,20},{8,24},{12,28},{16,0},{20,4},{24,8},{28,12},{1,17},{... | collective-permute-start | bytes 3342344 | tf_op jit(solution)/shard_map/ppermute | solution.py:70
  16.7 30.4 %collective-permute-start = (bf16[256,2176]{1,0:T(8,128)(2,1)S(1)}, bf16[256,2176]{1,0:T(8,128)(2,1)S(1)}, u32[]{:S(2)}, u32[]{:S(2)}) collective-permute-start(bf16[256,2176]{1,0:T(8,128)(2,1)S(1)} %concatenate.27.refs_0_.refs_4_), channel_id=1, source_target_pairs={{0,8},{4,12},{8,0},{12,4},{16,24},{20,28},{24,16},{28,20},{1,9},{5... | collective-permute-start | bytes 3342344 | tf_op jit(solution)/shard_map/ppermute | solution.py:70
  57.5 52.8 %collective-permute-start.13 = (bf16[256,2176]{1,0:T(8,128)(2,1)}, bf16[256,2176]{1,0:T(8,128)(2,1)S(1)}, u32[]{:S(2)}, u32[]{:S(2)}) collective-permute-start(bf16[256,2176]{1,0:T(8,128)(2,1)} %pad_maximum_fusion.refs_0_), channel_id=1, source_target_pairs={{0,16},{4,20},{8,24},{12,28},{16,0},{20,4},{24,8},{28,12},{1,17},{... | collective-permute-start | bytes 3342344 | tf_op jit(solution)/shard_map/ppermute | solution.py:70
  62.7 49.7 %collective-permute-start.12 = (bf16[256,2176]{1,0:T(8,128)(2,1)}, bf16[256,2176]{1,0:T(8,128)(2,1)}, u32[]{:S(2)}, u32[]{:S(2)}) collective-permute-start(bf16[256,2176]{1,0:T(8,128)(2,1)} %pad_maximum_fusion.refs_0_), channel_id=1, source_target_pairs={{0,8},{4,12},{8,0},{12,4},{16,24},{20,28},{24,16},{28,20},{1,9},{5... | collective-permute-start | bytes 3342344 | tf_op jit(solution)/shard_map/ppermute | solution.py:70
  111.9 27.7 %collective-permute-start.16 = (bf16[256,2176]{1,0:T(8,128)(2,1)}, bf16[256,2176]{1,0:T(8,128)(2,1)S(1)}, u32[]{:S(2)}, u32[]{:S(2)}) collective-permute-start(bf16[256,2176]{1,0:T(8,128)(2,1)} %pad_maximum_fusion.refs_0_), channel_id=1, source_target_pairs={{0,4},{4,0},{8,12},{12,8},{16,20},{20,16},{24,28},{28,24},{1,5},{5... | collective-permute-start | bytes 3342344 | tf_op jit(solution)/shard_map/ppermute | solution.py:70
  111.9 30.4 %collective-permute-start.18 = (bf16[256,2176]{1,0:T(8,128)(2,1)S(1)}, bf16[256,2176]{1,0:T(8,128)(2,1)S(1)}, u32[]{:S(2)}, u32[]{:S(2)}) collective-permute-start(bf16[256,2176]{1,0:T(8,128)(2,1)S(1)} %collective-permute-done.13.refs_2_), channel_id=1, source_target_pairs={{0,4},{4,0},{8,12},{12,8},{16,20},{20,16},{24,28},{28,24},{1,5},{5... | collective-permute-start | bytes 3342344 | tf_op jit(solution)/shard_map/ppermute | solution.py:70
  116.5 23.0 %collective-permute-start.31 = (bf16[64,2176]{1,0:T(8,128)(2,1)S(1)}, bf16[64,2176]{1,0:T(8,128)(2,1)S(1)}, u32[]{:S(2)}, u32[]{:S(2)}) collective-permute-start(bf16[64,2176]{1,0:T(8,128)(2,1)S(1)} %copy-done.17), channel_id=1, source_target_pairs={{0,2},{1,3},{2,0},{3,1},{4,6},{5,7},{6,4},{7,5},{8,10},{9,11},{10,... | collective-permute-start | bytes 835592 | tf_op jit(solution)/shard_map/ppermute | solution.py:70
  125.3 51.8 %collective-permute-start.17 = (bf16[256,2176]{1,0:T(8,128)(2,1)}, bf16[256,2176]{1,0:T(8,128)(2,1)S(1)}, u32[]{:S(2)}, u32[]{:S(2)}) collective-permute-start(bf16[256,2176]{1,0:T(8,128)(2,1)} %collective-permute-done.12.refs_1_), channel_id=1, source_target_pairs={{0,4},{4,0},{8,12},{12,8},{16,20},{20,16},{24,28},{28,24},{1,5},{5... | collective-permute-start | bytes 3342344 | tf_op jit(solution)/shard_map/ppermute | solution.py:70
  139.6 41.0 %collective-permute-start.34 = (bf16[192,2176]{1,0:T(8,128)(2,1)S(1)}, bf16[192,2176]{1,0:T(8,128)(2,1)S(1)}, u32[]{:S(2)}, u32[]{:S(2)}) collective-permute-start(bf16[192,2176]{1,0:T(8,128)(2,1)S(1)} %constant_dynamic-update-slice_fusion.refs_10_), channel_id=1, source_target_pairs={{0,16},{4,20},{8,24},{12,28},{16,0},{20,4},{24,8},{28,12},{1,17},{... | collective-permute-start | bytes 2506760 | tf_op jit(solution)/shard_map/ppermute | solution.py:70
  141.2 25.4 %collective-permute-start.22 = (bf16[64,2176]{1,0:T(8,128)(2,1)S(1)}, bf16[64,2176]{1,0:T(8,128)(2,1)S(1)}, u32[]{:S(2)}, u32[]{:S(2)}) collective-permute-start(bf16[64,2176]{1,0:T(8,128)(2,1)S(1)} %copy-done.17), channel_id=1, source_target_pairs={{0,16},{4,20},{8,24},{12,28},{16,0},{20,4},{24,8},{28,12},{1,17},{... | collective-permute-start | bytes 835592 | tf_op jit(solution)/shard_map/ppermute | solution.py:70
  141.7 39.4 %collective-permute-start.33 = (bf16[192,2176]{1,0:T(8,128)(2,1)S(1)}, bf16[192,2176]{1,0:T(8,128)(2,1)S(1)}, u32[]{:S(2)}, u32[]{:S(2)}) collective-permute-start(bf16[192,2176]{1,0:T(8,128)(2,1)S(1)} %constant_dynamic-update-slice_fusion.refs_10_), channel_id=1, source_target_pairs={{0,8},{4,12},{8,0},{12,4},{16,24},{20,28},{24,16},{28,20},{1,9},{5... | collective-permute-start | bytes 2506760 | tf_op jit(solution)/shard_map/ppermute | solution.py:70
  142.3 33.2 %collective-permute-start.20 = (bf16[128,2176]{1,0:T(8,128)(2,1)S(1)}, bf16[128,2176]{1,0:T(8,128)(2,1)S(1)}, u32[]{:S(2)}, u32[]{:S(2)}) collective-permute-start(bf16[128,2176]{1,0:T(8,128)(2,1)S(1)} %collective-permute-done.15.refs_4_), channel_id=1, source_target_pairs={{0,4},{4,0},{8,12},{12,8},{16,20},{20,16},{24,28},{28,24},{1,5},{5... | collective-permute-start | bytes 1671176 | tf_op jit(solution)/shard_map/ppermute | solution.py:70
  184.5 33.0 %collective-permute-start.37 = (bf16[192,2176]{1,0:T(8,128)(2,1)S(1)}, bf16[192,2176]{1,0:T(8,128)(2,1)S(1)}, u32[]{:S(2)}, u32[]{:S(2)}) collective-permute-start(bf16[192,2176]{1,0:T(8,128)(2,1)S(1)} %constant_dynamic-update-slice_fusion.refs_10_), channel_id=1, source_target_pairs={{0,4},{4,0},{8,12},{12,8},{16,20},{20,16},{24,28},{28,24},{1,5},{5... | collective-permute-start | bytes 2506760 | tf_op jit(solution)/shard_map/ppermute | solution.py:70
  184.6 33.0 %collective-permute-start.39 = (bf16[192,2176]{1,0:T(8,128)(2,1)S(1)}, bf16[192,2176]{1,0:T(8,128)(2,1)}, u32[]{:S(2)}, u32[]{:S(2)}) collective-permute-start(bf16[192,2176]{1,0:T(8,128)(2,1)S(1)} %collective-permute-done.34.refs_12_), channel_id=1, source_target_pairs={{0,4},{4,0},{8,12},{12,8},{16,20},{20,16},{24,28},{28,24},{1,5},{5... | collective-permute-start | bytes 2506760 | tf_op jit(solution)/shard_map/ppermute | solution.py:70
  185.1 32.5 %collective-permute-start.38 = (bf16[192,2176]{1,0:T(8,128)(2,1)S(1)}, bf16[192,2176]{1,0:T(8,128)(2,1)}, u32[]{:S(2)}, u32[]{:S(2)}) collective-permute-start(bf16[192,2176]{1,0:T(8,128)(2,1)S(1)} %collective-permute-done.33.refs_11_), channel_id=1, source_target_pairs={{0,4},{4,0},{8,12},{12,8},{16,20},{20,16},{24,28},{28,24},{1,5},{5... | collective-permute-start | bytes 2506760 | tf_op jit(solution)/shard_map/ppermute | solution.py:70
  193.4 24.1 %collective-permute-start.40 = (bf16[96,2176]{1,0:T(8,128)(2,1)S(1)}, bf16[96,2176]{1,0:T(8,128)(2,1)}, u32[]{:S(2)}, u32[]{:S(2)}) collective-permute-start(bf16[96,2176]{1,0:T(8,128)(2,1)S(1)} %collective-permute-done.35.refs_13_), channel_id=1, source_target_pairs={{0,4},{4,0},{8,12},{12,8},{16,20},{20,16},{24,28},{28,24},{1,5},{5... | collective-permute-start | bytes 1253384 | tf_op jit(solution)/shard_map/ppermute | solution.py:70
  264.3 26.9 %collective-permute-start.51 = (bf16[2,128,2176]{2,1,0:T(8,128)(2,1)S(1)}, bf16[2,128,2176]{2,1,0:T(8,128)(2,1)S(1)}, u32[]{:S(2)}, u32[]{:S(2)}) collective-permute-start(bf16[2,128,2176]{2,1,0:T(8,128)(2,1)S(1)} %pad_maximum_fusion.1), channel_id=1, source_target_pairs={{0,8},{4,12},{8,0},{12,4},{16,24},{20,28},{24,16},{28,20},{1,9},{5... | collective-permute-start | bytes 3342344 | tf_op jit(solution)/shard_map/ppermute | solution.py:70
  265.4 26.6 %collective-permute-start.54 = (bf16[2,128,2176]{2,1,0:T(8,128)(2,1)S(1)}, bf16[2,128,2176]{2,1,0:T(8,128)(2,1)S(1)}, u32[]{:S(2)}, u32[]{:S(2)}) collective-permute-start(bf16[2,128,2176]{2,1,0:T(8,128)(2,1)S(1)} %pad_maximum_fusion.2), channel_id=1, source_target_pairs={{0,16},{4,20},{8,24},{12,28},{16,0},{20,4},{24,8},{28,12},{1,17},{... | collective-permute-start | bytes 3342344 | tf_op jit(solution)/shard_map/ppermute | solution.py:70
  311.0 77.7 %collective-permute-start.42 = (bf16[4,256,2048]{2,1,0:T(8,128)(2,1)}, bf16[4,256,2048]{2,1,0:T(8,128)(2,1)}, u32[]{:S(2)}, u32[]{:S(2)}) collective-permute-start(bf16[4,256,2048]{2,1,0:T(8,128)(2,1)} %get-tuple-element.64), channel_id=1, source_target_pairs={{0,4},{4,0},{8,12},{12,8},{16,20},{20,16},{24,28},{28,24},{1,5},{5... | collective-permute-start | bytes 12582920 | tf_op jit(solution)/shard_map/ppermute | solution.py:70
  316.0 23.6 %collective-permute-start.56 = (bf16[64,2176]{1,0:T(8,128)(2,1)S(1)}, bf16[64,2176]{1,0:T(8,128)(2,1)S(1)}, u32[]{:S(2)}, u32[]{:S(2)}) collective-permute-start(bf16[64,2176]{1,0:T(8,128)(2,1)S(1)} %get-tuple-element.153), channel_id=1, source_target_pairs={{0,2},{1,3},{2,0},{3,1},{4,6},{5,7},{6,4},{7,5},{8,10},{9,11},{10,... | collective-permute-start | bytes 835592 | tf_op jit(solution)/shard_map/ppermute | solution.py:70
  388.7 47.4 %collective-permute-start.67 = (bf16[4,256,2176]{2,1,0:T(8,128)(2,1)}, bf16[4,256,2176]{2,1,0:T(8,128)(2,1)S(1)}, u32[]{:S(2)}, u32[]{:S(2)}) collective-permute-start(bf16[4,256,2176]{2,1,0:T(8,128)(2,1)} %get-tuple-element.87), channel_id=1, source_target_pairs={{0,4},{4,0},{8,12},{12,8},{16,20},{20,16},{24,28},{28,24},{1,5},{5... | collective-permute-start | bytes 13369352 | tf_op jit(solution)/shard_map/ppermute | solution.py:70
  391.8 25.6 %collective-permute-start.46 = (bf16[2,128,2048]{2,1,0:T(8,128)(2,1)S(1)}, bf16[2,128,2048]{2,1,0:T(8,128)(2,1)S(1)}, u32[]{:S(2)}, u32[]{:S(2)}) collective-permute-start(bf16[2,128,2048]{2,1,0:T(8,128)(2,1)S(1)} %pad_maximum_fusion.6), channel_id=1, source_target_pairs={{0,16},{4,20},{8,24},{12,28},{16,0},{20,4},{24,8},{28,12},{1,17},{... | collective-permute-start | bytes 3145736 | tf_op jit(solution)/shard_map/ppermute | solution.py:70
  392.5 25.4 %collective-permute-start.43 = (bf16[2,128,2048]{2,1,0:T(8,128)(2,1)S(1)}, bf16[2,128,2048]{2,1,0:T(8,128)(2,1)S(1)}, u32[]{:S(2)}, u32[]{:S(2)}) collective-permute-start(bf16[2,128,2048]{2,1,0:T(8,128)(2,1)S(1)} %pad_maximum_fusion.5), channel_id=1, source_target_pairs={{0,8},{4,12},{8,0},{12,4},{16,24},{20,28},{24,16},{28,20},{1,9},{5... | collective-permute-start | bytes 3145736 | tf_op jit(solution)/shard_map/ppermute | solution.py:70
  438.3 54.4 %collective-permute-start.68 = (bf16[2,128,2176]{2,1,0:T(8,128)(2,1)S(1)}, bf16[2,128,2176]{2,1,0:T(8,128)(2,1)S(1)}, u32[]{:S(2)}, u32[]{:S(2)}) collective-permute-start(bf16[2,128,2176]{2,1,0:T(8,128)(2,1)S(1)} %pad_maximum_fusion.3), channel_id=1, source_target_pairs={{0,8},{4,12},{8,0},{12,4},{16,24},{20,28},{24,16},{28,20},{1,9},{5... | collective-permute-start | bytes 3342344 | tf_op jit(solution)/shard_map/ppermute | solution.py:70
  440.4 52.3 %collective-permute-start.70 = (bf16[2,128,2176]{2,1,0:T(8,128)(2,1)}, bf16[2,128,2176]{2,1,0:T(8,128)(2,1)S(1)}, u32[]{:S(2)}, u32[]{:S(2)}) collective-permute-start(bf16[2,128,2176]{2,1,0:T(8,128)(2,1)} %pad_maximum_fusion.4), channel_id=1, source_target_pairs={{0,16},{4,20},{8,24},{12,28},{16,0},{20,4},{24,8},{28,12},{1,17},{... | collective-permute-start | bytes 3342344 | tf_op jit(solution)/shard_map/ppermute | solution.py:70
  463.8 104.9 %all-reduce.2.cloned.1.call-start = ((), (), s32[]{:S(2)}) async-start(), calls=%async_computation.1 | async-start | bytes 262144 | tf_op jit(solution)/shard_map/psum | solution.py:877
  486.3 39.9 %collective-permute-start.66 = (bf16[64,2048]{1,0:T(8,128)(2,1)}, bf16[64,2048]{1,0:T(8,128)(2,1)S(1)}, u32[]{:S(2)}, u32[]{:S(2)}) collective-permute-start(bf16[64,2048]{1,0:T(8,128)(2,1)} %input_gradient.1.refs_0_), channel_id=1, source_target_pairs={{0,3},{1,2},{2,1},{3,0},{4,7},{5,6},{6,5},{7,4},{8,11},{9,10},{10,... | collective-permute-start | bytes 786440 | tf_op jit(solution)/shard_map/ppermute | solution.py:70
  488.7 39.2 %collective-permute-start.65 = (bf16[64,2048]{1,0:T(8,128)(2,1)}, bf16[64,2048]{1,0:T(8,128)(2,1)S(1)}, u32[]{:S(2)}, u32[]{:S(2)}) collective-permute-start(bf16[64,2048]{1,0:T(8,128)(2,1)} %input_gradient.1.refs_0_), channel_id=1, source_target_pairs={{0,2},{1,3},{2,0},{3,1},{4,6},{5,7},{6,4},{7,5},{8,10},{9,11},{10,... | collective-permute-start | bytes 786440 | tf_op jit(solution)/shard_map/ppermute | solution.py:70
  492.7 35.3 %collective-permute-start.64 = (bf16[64,2048]{1,0:T(8,128)(2,1)}, bf16[64,2048]{1,0:T(8,128)(2,1)}, u32[]{:S(2)}, u32[]{:S(2)}) collective-permute-start(bf16[64,2048]{1,0:T(8,128)(2,1)} %input_gradient.1.refs_0_), channel_id=1, source_target_pairs={{0,1},{1,0},{2,3},{3,2},{4,5},{5,4},{6,7},{7,6},{8,9},{9,8},{10,11... | collective-permute-start | bytes 786440 | tf_op jit(solution)/shard_map/ppermute | solution.py:70
  495.1 35.8 %collective-permute-start.71 = (bf16[128,2176]{1,0:T(8,128)(2,1)S(1)}, bf16[128,2176]{1,0:T(8,128)(2,1)S(1)}, u32[]{:S(2)}, u32[]{:S(2)}) collective-permute-start(bf16[128,2176]{1,0:T(8,128)(2,1)S(1)} %get-tuple-element.122), channel_id=1, source_target_pairs={{0,8},{4,12},{8,0},{12,4},{16,24},{20,28},{24,16},{28,20},{1,9},{5... | collective-permute-start | bytes 1671176 | tf_op jit(solution)/shard_map/ppermute | solution.py:70
  496.2 35.5 %collective-permute-start.69 = (bf16[128,2176]{1,0:T(8,128)(2,1)S(1)}, bf16[128,2176]{1,0:T(8,128)(2,1)}, u32[]{:S(2)}, u32[]{:S(2)}) collective-permute-start(bf16[128,2176]{1,0:T(8,128)(2,1)S(1)} %get-tuple-element.123), channel_id=1, source_target_pairs={{0,16},{4,20},{8,24},{12,28},{16,0},{20,4},{24,8},{28,12},{1,17},{... | collective-permute-start | bytes 1671176 | tf_op jit(solution)/shard_map/ppermute | solution.py:70
  (95 other events, 1417.1 us)
Sparse Core Ops, SparseCore 0:
  463.9 60.6 all-gather.1
  535.1 33.5 all-reduce.1

commit v2 on v1

v2 whole, which is shorter than its diff:
```python
import functools

import jax
import jax.numpy as jnp
from jax import lax
from jax.experimental import pallas as pl
from jax.experimental.pallas import tpu as pltpu
from jax.sharding import PartitionSpec as P

D = 2048
HD = 128
EXPERTS = 64
CAP = 40
SIDE = 128
EPSILON = 1e-06
ROPE_BASE = 10000.0

F32 = jnp.float32
BF16 = jnp.bfloat16
VMEM = pl.BlockSpec(memory_space=pltpu.VMEM)
SMEM = pl.BlockSpec(memory_space=pltpu.SMEM)
HBM = pl.BlockSpec(memory_space=pl.ANY)
VMEM_BYTES = 60 * 1024 * 1024


def shape(dims, dtype):
    return jax.ShapeDtypeStruct(tuple(dims), dtype)


def params(**more):
    return pltpu.CompilerParams(vmem_limit_bytes=VMEM_BYTES, **more)


def cost(micros):
    return pl.CostEstimate(
        flops=int(micros * 1e9), bytes_accessed=int(micros * 3e6), transcendentals=0
    )


def dot(left, right):
    return jnp.dot(left, right, preferred_element_type=F32)


def dot_nt(left, right):
    return lax.dot_general(left, right, (((1,), (1,)), ((), ())), preferred_element_type=F32)


def dot_tn(left, right):
    return lax.dot_general(left, right, (((0,), (0,)), ((), ())), preferred_element_type=F32)


def rms_inverse(values):
    return lax.rsqrt(jnp.mean(values * values, axis=-1, keepdims=True) + EPSILON)


def norm_backward(values, inverse, gain, upstream):
    scaled = gain * upstream
    return inverse * scaled - values * (inverse * inverse * inverse) * jnp.mean(
        values * scaled, axis=-1, keepdims=True
    )


def half_turn(values):
    return pltpu.roll(values, HD // 2, 1)


def lanes(dims):
    return lax.broadcasted_iota(jnp.int32, dims, len(dims) - 1)


def swap(block, axis, size, step):
    return lax.ppermute(block, axis, [(i, i ^ step) for i in range(size)])


def without(kernel, at, number):
    def body(*refs):
        kernel(*refs[:at], *refs[at + number :])

    return body


def through(moves, buffer, sems):
    arriving, leaving, row = [], [], 0
    for k, (source, target) in enumerate(moves):
        here = buffer.at[pl.ds(row, source.shape[0]), :]
        arriving.append(pltpu.make_async_copy(source, here, sems.at[2 * k]))
        leaving.append(pltpu.make_async_copy(here, target, sems.at[2 * k + 1]))
        arriving[-1].start()
        row += source.shape[0]
    for arrives, leaves in zip(arriving, leaving):
        arrives.wait()
        leaves.start()
    for leaves in leaving:
        leaves.wait()


def joins(groups, deps=()):
    parts = [part for group in groups for part in group]
    count = len(parts)
    features, dtype = parts[0].shape[1], parts[0].dtype
    totals = [sum(part.shape[0] for part in group) for group in groups]

    def kernel(*refs):
        out_refs, (buffer, sems) = refs[count:-2], refs[-2:]
        moves, k = [], 0
        for out_ref, group in zip(out_refs, groups):
            row = 0
            for part in group:
                moves.append((refs[k], out_ref.at[pl.ds(row, part.shape[0]), :]))
                row, k = row + part.shape[0], k + 1
        through(moves, buffer, sems)

    return pl.pallas_call(
        without(kernel, count, len(deps)),
        out_shape=[shape((total, features), dtype) for total in totals],
        in_specs=[HBM] * (count + len(deps)),
        out_specs=[HBM] * len(groups),
        scratch_shapes=[
            pltpu.VMEM((sum(totals), features), dtype),
            pltpu.SemaphoreType.DMA((2 * count,)),
        ],
        compiler_params=params(),
        cost_estimate=cost(0.1),
        name="joins",
    )(*parts, *deps)


def join(parts, deps=()):
    return joins([parts], deps)[0]


def relay(parts, deps):
    return joins([[part] for part in parts], deps)


def halves(upper_of, lower_of, deps=()):
    rows, features = upper_of.shape
    half = rows // 2

    def kernel(upper_ref, lower_ref, upper_out, lower_out, buffer, sems):
        through(
            [
                (upper_ref.at[pl.ds(0, half), :], upper_out),
                (lower_ref.at[pl.ds(half, half), :], lower_out),
            ],
            buffer,
            sems,
        )

    return pl.pallas_call(
        without(kernel, 2, len(deps)),
        out_shape=[shape((half, features), upper_of.dtype)] * 2,
        in_specs=[HBM] * (2 + len(deps)),
        out_specs=[HBM] * 2,
        scratch_shapes=[
            pltpu.VMEM((rows, features), upper_of.dtype),
            pltpu.SemaphoreType.DMA((4,)),
        ],
        compiler_params=params(),
        cost_estimate=cost(0.1),
        name="halves",
    )(upper_of, lower_of, *deps)


def gather_near(block, size):
    if size != 8:
        return [swap(block, "fsdp", size, p) for p in range(1, size)]
    return [swap(block, "fsdp", size, 2), swap(block, "fsdp", size, 4)]


def gather_rest(block, near, size, deps=()):
    rows = block.shape[0]
    if size != 8:
        return [(p, 0, part, 0, rows) for p, part in enumerate([block] + near)]
    half = rows // 2
    upper, lower = halves(near[1], near[0], deps)
    front = swap(upper, "fsdp", size, 2)
    back = swap(lower, "fsdp", size, 4)
    pieces = []
    for k, part in enumerate([block] + near):
        pieces.append((2 * k, 0, part, 0, rows))
        pieces.append((2 * k + 1, 0, swap(part, "fsdp", size, 1), 0, rows))
    for row, part in ((0, front), (half, back)):
        pieces.append((6, row, part, 0, half))
        pieces.append((7, row, swap(part, "fsdp", size, 1), 0, half))
    return pieces


def gather_two(blocks, near, size, sources=None):
    pieces = []
    start = 0
    sources = sources or [near[0][1], near[1][0]]
    for block, (along_x, along_y), source, step in zip(blocks, near, sources, (2, 4)):
        rows = block.shape[0]
        last = swap(source, "fsdp", size, step)
        for index, part in ((0, block), (2, along_x), (4, along_y), (6, last)):
            pieces.append((index, start, part, 0, rows))
            pieces.append((index + 1, start, swap(part, "fsdp", size, 1), 0, rows))
        start += rows
    return pieces


def arrays_of(pieces):
    found = []
    for _, _, part, _, _ in pieces:
        if not any(part is other for other in found):
            found.append(part)
    return found


def start_fetch(pieces, refs, place, sems, own=None):
    arrays = arrays_of(pieces)
    copies = []
    for k, (index, row, part, at, rows) in enumerate(pieces):
        ref = next(ref for other, ref in zip(arrays, refs) if other is part)
        if at is None:
            at = pl.multiple_of((own ^ index) * rows, 16)
        copy = pltpu.make_async_copy(
            ref.at[pl.ds(at, rows), :], place(index, row, rows), sems.at[k]
        )
        copy.start()
        copies.append(copy)
    return copies


def pair_sums(keep, got, deps=()):
    _, rows, columns = keep.shape
    half = rows // 2

    def kernel(keep_x, got_x, keep_y, got_y, out_x, out_y):
        out_x[...] = (keep_x[...].astype(F32) + got_x[...].astype(F32)).astype(BF16)
        out_y[...] = (keep_y[...].astype(F32) + got_y[...].astype(F32)).astype(BF16)

    block = (1, half, columns)
    along_x = pl.BlockSpec(block, lambda j: (2 * j + 1, 0, 0))
    along_y = pl.BlockSpec(block, lambda j: (2 + j, 1, 0))
    return pl.pallas_call(
        without(kernel, 4, len(deps)),
        out_shape=[shape((2, half, columns), BF16)] * 2,
        grid=(2,),
        in_specs=[along_x, along_x, along_y, along_y] + [HBM] * len(deps),
        out_specs=[pl.BlockSpec(block, lambda j: (j, 0, 0))] * 2,
        compiler_params=params(),
        cost_estimate=cost(0.1),
        name="pair_sums",
    )(keep, got, keep, got, *deps)


def next_sums(keep, got, from_x, from_y, deps, micros):
    _, rows, columns = keep.shape
    half = rows // 2
    part = half // 2

    def kernel(keep_x, got_x, new_x, keep_y, got_y, new_y, out_x, out_y):
        out_x[...] = (
            keep_x[0].astype(F32) + got_x[0].astype(F32) + new_x[0].astype(F32)
        ).astype(BF16)
        out_y[...] = (
            keep_y[0].astype(F32) + got_y[0].astype(F32) + new_y[0].astype(F32)
        ).astype(BF16)

    block = (1, part, columns)
    upper = pl.BlockSpec(block, lambda j: (2, j, 0))
    lower = pl.BlockSpec(block, lambda j: (1, j + 2, 0))
    new = pl.BlockSpec(block, lambda j: (1, j, 0))
    return pl.pallas_call(
        without(kernel, 6, len(deps)),
        out_shape=[shape((half, columns), BF16)] * 2,
        grid=(2,),
        in_specs=[upper, upper, new, lower, lower, new] + [HBM] * len(deps),
        out_specs=[pl.BlockSpec((part, columns), lambda j: (j, 0))] * 2,
        compiler_params=params(),
        cost_estimate=cost(micros),
        name="next_sums",
    )(keep, got, from_x, keep, got, from_y, *deps)


def last_sums(keep, got, from_x, from_y, last_x, last_y, count, deps=()):
    _, rows, columns = keep.shape
    half = rows // 2
    part = rows // count
    each = half // part

    def kernel(keep_x, got_x, new_x, end_x, keep_y, got_y, new_y, end_y, *out_refs):
        for k in range(count):
            refs = (keep_x, got_x, new_x, end_x) if k < each else (keep_y, got_y, new_y, end_y)
            span = slice((k % each) * part, (k % each + 1) * part)
            total = refs[0][0, span].astype(F32)
            for ref in refs[1:3]:
                total = total + ref[0, span].astype(F32)
            out_refs[k][...] = (total + refs[3][span].astype(F32)).astype(BF16)

    block = (1, half, columns)
    first = pl.BlockSpec(block, lambda j: (0, 0, 0))
    second = pl.BlockSpec(block, lambda j: (0, 1, 0))
    end = pl.BlockSpec((half, columns), lambda j: (0, 0))
    return pl.pallas_call(
        without(kernel, 8, len(deps)),
        out_shape=[shape((part, columns), BF16)] * count,
        grid=(1,),
        in_specs=[first, first, first, end, second, second, first, end] + [HBM] * len(deps),
        out_specs=[pl.BlockSpec((part, columns), lambda j: (0, 0))] * count,
        compiler_params=params(),
        cost_estimate=cost(20),
        name="last_sums",
    )(keep, got, from_x, last_x, keep, got, from_y, last_y, *deps)


class Reduce:
    def __init__(self, keep, send, size):
        self.keep, self.send, self.size = keep, send, size
        if size == 8:
            self.got = swap(send, "fsdp", size, 1)

    def first(self, deps=()):
        if self.size != 8:
            return []
        self.pair = pair_sums(self.keep, self.got, deps)
        self.from_x = swap(self.pair[0], "fsdp", self.size, 2)
        self.from_y = swap(self.pair[1], "fsdp", self.size, 4)
        return list(self.pair[:1])

    def second(self, deps=(), micros=0.1):
        if self.size != 8:
            return []
        sums = next_sums(self.keep, self.got, self.from_x, self.from_y, deps, micros)
        self.last_x = swap(sums[0], "fsdp", self.size, 4)
        self.last_y = swap(sums[1], "fsdp", self.size, 2)
        return list(sums[:1])

    def total(self):
        if self.size != 8:
            total = self.keep[0].astype(F32)
            for p in range(1, self.size):
                block = self.keep[p // 2] if p % 2 == 0 else self.send[p // 2]
                total = total + swap(block, "fsdp", self.size, p).astype(F32)
            return total
        half = self.keep.shape[1] // 2
        sums = []
        for rows, new, last in (
            (slice(0, half), self.from_x, self.last_x),
            (slice(half, None), self.from_y, self.last_y),
        ):
            sums.append(
                self.keep[0, rows].astype(F32)
                + self.got[0, rows].astype(F32)
                + new[0].astype(F32)
                + last.astype(F32)
            )
        return jnp.concatenate(sums, axis=0)

    def rows(self, count, deps=()):
        if self.size != 8:
            return jnp.split(self.total().astype(BF16), count, axis=0)
        return last_sums(
            self.keep, self.got, self.from_x, self.from_y, self.last_x, self.last_y, count, deps
        )


def attend_forward(pos, tokens, cosine, sine, pieces, nf, nt, deps=()):
    length = tokens.shape[0]
    block = D // nf
    rows = length // nt
    columns = pieces[0][2].shape[1]
    width = (columns - SIDE) // 4
    heads = width // HD
    arrays = arrays_of(pieces)
    count = len(arrays)

    def kernel(pos_ref, x_ref, cos_ref, sin_ref, *refs):
        piece_refs, refs = refs[:count], refs[count:]
        n1_ref, qk_ref, rot_ref, v_ref, prob_ref, att_ref, side_ref, gain_ref, head_gain_ref = refs[:9]
        part_refs, (w, out, sems) = refs[9 : 9 + nt], refs[9 + nt :]
        f, t = pos_ref[0], pos_ref[1]

        def place(index, row, number):
            start = pl.multiple_of((f ^ index) * block + row, 16)
            return w.at[pl.ds(start, number), :]

        copies = start_fetch(pieces, piece_refs, place, sems)
        x = x_ref[...].astype(F32)
        normed = x * rms_inverse(x)
        for copy in copies:
            copy.wait()
        side_ref[...] = w[:, 4 * width :]
        turned = jnp.transpose(w[:, 4 * width :].astype(F32))
        gain_ref[...] = turned[EXPERTS : EXPERTS + 8]
        head_rows = turned[EXPERTS : EXPERTS + 8, :block]
        for p in range(1, nf):
            head_rows = head_rows + turned[EXPERTS : EXPERTS + 8, p * block : (p + 1) * block]
        head_gains = head_rows[:, :HD]
        head_gain_ref[...] = head_gains
        n1 = (normed * turned[EXPERTS : EXPERTS + 1]).astype(BF16)
        n1_ref[...] = n1
        raw = dot(n1, w[:, : 3 * width])
        qk_ref[...] = raw[:, : 2 * width]
        v_ref[...] = raw[:, 2 * width :].astype(BF16)
        cos, sin = cos_ref[...], sin_ref[...]
        for h in range(heads):
            span = slice(h * HD, (h + 1) * HD)
            turned_rows = []
            for which in range(2):
                values = raw[:, which * width + h * HD : which * width + (h + 1) * HD]
                scaled = values * rms_inverse(values) * head_gains[2 + which : 3 + which]
                low = (scaled * cos + half_turn(scaled) * sin).astype(BF16)
                rot_ref[:, which * width + h * HD : which * width + (h + 1) * HD] = low
                turned_rows.append(low)
            scores = dot_nt(turned_rows[0], turned_rows[1]) * (HD**-0.5)
            shifted = jnp.exp(scores - jnp.max(scores, axis=-1, keepdims=True))
            probs = shifted / jnp.sum(shifted, axis=-1, keepdims=True)
            prob_ref[h] = probs
            att_ref[:, span] = dot(probs.astype(BF16), v_ref[:, span]).astype(BF16)
        out[...] = dot_nt(att_ref[...], w[:, 3 * width : 4 * width]).astype(BF16)
        for d in range(nt):
            start = pl.multiple_of((t ^ d) * rows, 16)
            part_refs[d][...] = out[pl.ds(start, rows), :]

    results = pl.pallas_call(
        without(kernel, 4 + count, len(deps)),
        out_shape=[
            shape((length, D), BF16),
            shape((length, 2 * width), F32),
            shape((length, 2 * width), BF16),
            shape((length, width), BF16),
            shape((heads, length, length), F32),
            shape((length, width), BF16),
            shape((D, SIDE), BF16),
            shape((8, D), F32),
            shape((8, HD), F32),
        ]
        + [shape((rows, D), BF16)] * nt,
        in_specs=[SMEM, VMEM, VMEM, VMEM] + [HBM] * (count + len(deps)),
        out_specs=[VMEM] * (9 + nt),
        scratch_shapes=[
            pltpu.VMEM((D, columns), BF16),
            pltpu.VMEM((length, D), BF16),
            pltpu.SemaphoreType.DMA((len(pieces),)),
        ],
        compiler_params=params(),
        cost_estimate=cost(5),
        name="attend_forward",
    )(pos, tokens, cosine, sine, *arrays, *deps)
    return results[:9], results[9:]


def attend_backward(pos, grad_rows, ffn_row, pieces, saved, tokens, cosine, sine, nf, nt, deps=()):
    _, qk, rot, values, probs, _, _, gains, head_gains = saved
    length = tokens.shape[0]
    block = D // nf
    rows = length // nt
    columns = pieces[0][2].shape[1]
    width = (columns - SIDE) // 4
    heads = width // HD
    more = gain_columns(rows)
    arrays = arrays_of(pieces)
    count = len(arrays)

    def kernel(pos_ref, x_ref, cos_ref, sin_ref, qk_ref, rot_ref, v_ref, prob_ref, gain_ref, head_gain_ref, ffn_ref, *refs):
        grad_refs, refs = refs[:nt], refs[nt:]
        piece_refs, refs = refs[:count], refs[count:]
        dqkv_ref = refs[0]
        part_refs, (w, out, db_ref, sems) = refs[1:3], refs[3:]
        f, t = pos_ref[0], pos_ref[1]

        def place(index, row, number):
            start = pl.multiple_of((f ^ index) * block + row, 16)
            return w.at[pl.ds(start, number), :]

        copies = start_fetch(pieces, piece_refs, place, sems)
        for d in range(nt):
            start = pl.multiple_of((t ^ d) * rows, 16)
            db_ref[pl.ds(start, rows), :] = grad_refs[d][:, :D]
        for copy in copies:
            copy.wait()
        cos, sin = cos_ref[...], sin_ref[...]
        head_gains = head_gain_ref[...]
        grad_att = dot(db_ref[...], w[:, 3 * width : 4 * width]).astype(BF16)
        gain_rows = [jnp.zeros((1, HD), F32), jnp.zeros((1, HD), F32)]
        for h in range(heads):
            span = slice(h * HD, (h + 1) * HD)
            query_low = rot_ref[:, span]
            key_low = rot_ref[:, width + h * HD : width + (h + 1) * HD]
            grad_out = grad_att[:, span]
            exact = prob_ref[h]
            grad_probs = dot_nt(grad_out, v_ref[:, span])
            row_terms = jnp.sum(exact * grad_probs, axis=-1, keepdims=True)
            grad_scores = (exact * (grad_probs - row_terms)).astype(BF16)
            dqkv_ref[:, 2 * width + h * HD : 2 * width + (h + 1) * HD] = dot_tn(
                exact.astype(BF16), grad_out
            ).astype(BF16)
            both = (dot(grad_scores, key_low), dot_tn(grad_scores, query_low))
            for which in range(2):
                span_w = slice(which * width + h * HD, which * width + (h + 1) * HD)
                grads = both[which] * (HD**-0.5)
                grads = grads * cos - half_turn(grads) * sin
                raw = qk_ref[:, span_w]
                inverse = rms_inverse(raw)
                gain_rows[which] = gain_rows[which] + jnp.sum(
                    grads * raw * inverse, axis=0, keepdims=True
                )
                dqkv_ref[:, span_w] = norm_backward(
                    raw, inverse, head_gains[2 + which : 3 + which], grads
                ).astype(BF16)
        grad_normed = dot_nt(dqkv_ref[...], w[:, : 3 * width])
        out[...] = grad_normed.astype(BF16)
        x = x_ref[...].astype(F32)
        row = jnp.sum(grad_normed * (x * rms_inverse(x)), axis=0, keepdims=True)
        lines = [row[:, k * SIDE : (k + 1) * SIDE] for row in (ffn_ref[0:1, :], row) for k in range(D // SIDE)]
        lines = lines + gain_rows
        gain_blocks = []
        for k in range(more // SIDE):
            own = lines[k * rows : (k + 1) * rows]
            blank = [jnp.zeros((rows - len(own), SIDE), F32)] if len(own) < rows else []
            gain_blocks.append(jnp.concatenate(own + blank, axis=0).astype(BF16))
        for d in range(nt):
            start = pl.multiple_of((t ^ d) * rows, 16)
            to = part_refs[d % 2]
            span = slice(d // 2 * rows, (d // 2 + 1) * rows)
            to[span, :D] = out[pl.ds(start, rows), :]
            for k, gain_block in enumerate(gain_blocks):
                to[span, D + k * SIDE : D + (k + 1) * SIDE] = gain_block

    results = pl.pallas_call(
        without(kernel, 11 + nt + count, len(deps)),
        out_shape=[
            shape((length, 3 * width), BF16),
        ]
        + [shape((nt // 2 * rows, D + more), BF16)] * 2,
        in_specs=[SMEM] + [VMEM] * (10 + nt) + [HBM] * (count + len(deps)),
        out_specs=[VMEM] * 3,
        scratch_shapes=[
            pltpu.VMEM((D, columns), BF16),
            pltpu.VMEM((length, D), BF16),
            pltpu.VMEM((length, D), BF16),
            pltpu.SemaphoreType.DMA((len(pieces),)),
        ],
        compiler_params=params(),
        cost_estimate=cost(0.1),
        name="attend_backward",
    )(
        pos, tokens, cosine, sine, qk, rot, values, probs, gains, head_gains, ffn_row,
        *grad_rows, *arrays, *deps,
    )
    return results


def projection_gradients(pos, normed, dqkv, nf, deps=()):
    length = normed.shape[0]
    block = D // nf
    width = dqkv.shape[1]

    def kernel(pos_ref, n1_ref, dqkv_ref, keep_ref, send_ref):
        for p in range(nf):
            start = pl.multiple_of((pos_ref[0] ^ p) * block, 128)
            to = (keep_ref if p % 2 == 0 else send_ref).at[p // 2]
            to[...] = dot_tn(n1_ref[:, pl.ds(start, block)], dqkv_ref[...]).astype(BF16)

    return pl.pallas_call(
        without(kernel, 3, len(deps)),
        out_shape=[shape((nf // 2, block, width), BF16)] * 2,
        in_specs=[SMEM, VMEM, VMEM] + [HBM] * len(deps),
        out_specs=[VMEM] * 2,
        compiler_params=params(),
        cost_estimate=cost(0.1),
        name="projection_gradients",
    )(pos, normed, dqkv, *deps)


def output_gradients(pos, attended, grad_parts, normed_parts, gain_parts, group, nf, nt, deps=()):
    length, width = attended.shape
    rows = length // nt
    block = D // nf
    columns = width + SIDE
    more = gain_columns(rows)
    count = D // SIDE

    def kernel(pos_ref, att_ref, *refs):
        grad_refs, normed_refs, part_refs = refs[:nt], refs[nt : 2 * nt], refs[2 * nt : 2 * nt + 2]
        keep_ref, send_ref, db, n2, gain_ref = refs[2 * nt + 2 :]
        f, t = pos_ref[0], pos_ref[1]
        for d in range(nt):
            start = pl.multiple_of((t ^ d) * rows, 16)
            db[pl.ds(start, rows), :] = grad_refs[d][...]
            n2[pl.ds(start, rows), :] = normed_refs[d][:, :D]
        total = part_refs[0][:, D:].astype(F32) + part_refs[1][:, D:].astype(F32)
        for line in range(2 * count + 2):
            column, at = line // rows * SIDE, line % rows
            to = line // count if line < 2 * count else line - 2 * count + 2
            lane = line % count * SIDE if line < 2 * count else 0
            gain_ref[to : to + 1, lane : lane + SIDE] = total[at : at + 1, column : column + SIDE]
        lane = lanes((block, SIDE))
        sub = lax.broadcasted_iota(jnp.int32, (block, SIDE), 0)
        for p in range(nf):
            owner = f ^ p
            start = pl.multiple_of(owner * block, 128)
            to = (keep_ref if p % 2 == 0 else send_ref).at[p // 2]
            to[:, :width] = dot_tn(db[:, pl.ds(start, block)], att_ref[...]).astype(BF16)
            side = dot_tn(n2[:, pl.ds(start, block)], db[:, D:])
            for which in range(2):
                row = gain_ref[which : which + 1, pl.ds(start, block)]
                column = jnp.transpose(jnp.broadcast_to(row, (SIDE, block)))
                side = jnp.where(lane == EXPERTS + which, column, side)
            mine = (lane == owner * group + sub) & (sub < group)
            for which in range(2, 4):
                spread = jnp.where(mine, gain_ref[which : which + 1, :HD], 0.0)
                column = jnp.sum(spread, axis=1, keepdims=True)
                side = jnp.where(lane == EXPERTS + which, column, side)
            to[:, width:] = side.astype(BF16)

    return pl.pallas_call(
        without(kernel, 4 + 2 * nt, len(deps)),
        out_shape=[shape((nf // 2, block, columns), BF16)] * 2,
        in_specs=[SMEM] + [VMEM] * (3 + 2 * nt) + [HBM] * len(deps),
        out_specs=[VMEM] * 2,
        scratch_shapes=[
            pltpu.VMEM((length, D + SIDE), BF16),
            pltpu.VMEM((length, D), BF16),
            pltpu.VMEM((8, D), F32),
        ],
        compiler_params=params(),
        cost_estimate=cost(0.1),
        name="output_gradients",
    )(pos, attended, *grad_parts, *normed_parts, *gain_parts, *deps)


def gain_columns(rows):
    return SIDE * -(-(2 * D // SIDE + 2) // rows)


def norm_and_route(pos, tokens, routes, parts, gains, side, nt, deps=()):
    rows = tokens.shape[0] // nt
    top = routes.shape[1]

    def kernel(pos_ref, x_ref, route_ref, gain_ref, side_ref, *refs):
        part_refs, (h_ref, next_ref, gate_ref) = refs[:nt], refs[nt:]
        h = x_ref[...].astype(F32)
        for ref in part_refs:
            h = h + ref[...].astype(F32)
        h_ref[...] = h
        n2 = (h * rms_inverse(h) * gain_ref[1:2]).astype(BF16)
        next_ref[:, :D] = n2
        logits = dot(n2, side_ref[...])
        lane = lanes((rows, SIDE))
        chosen = route_ref[:, 0:1] == lane
        for j in range(1, top):
            chosen = chosen | (route_ref[:, j : j + 1] == lane)
        highest = jnp.max(jnp.where(chosen, logits, -jnp.inf), axis=-1, keepdims=True)
        shifted = jnp.where(chosen, jnp.exp(jnp.where(chosen, logits - highest, 0.0)), 0.0)
        gates = shifted / jnp.sum(shifted, axis=-1, keepdims=True)
        gate_ref[...] = gates
        first = gates.astype(BF16).astype(F32)
        rest = (gates - first).astype(BF16).astype(F32)
        next_ref[:, D:] = (first + pltpu.roll(rest, EXPERTS, 1)).astype(BF16)

    whole = lambda i, pos: (0, 0)
    mine = lambda i, pos: (pos[1], 0)
    return pl.pallas_call(
        without(kernel, 5 + nt, len(deps)),
        out_shape=[shape((rows, D), F32), shape((rows, D + SIDE), BF16), shape((rows, SIDE), F32)],
        grid_spec=pltpu.PrefetchScalarGridSpec(
            num_scalar_prefetch=1,
            grid=(1,),
            in_specs=[
                pl.BlockSpec((rows, D), mine),
                pl.BlockSpec((rows, top), mine),
                pl.BlockSpec((8, D), whole),
                pl.BlockSpec((D, SIDE), whole),
            ]
            + [pl.BlockSpec((rows, D), whole)] * nt
            + [HBM] * len(deps),
            out_specs=[
                pl.BlockSpec((rows, D), whole),
                pl.BlockSpec((rows, D + SIDE), whole),
                pl.BlockSpec((rows, SIDE), whole),
            ],
        ),
        compiler_params=params(),
        cost_estimate=cost(100),
        name="norm_and_route",
    )(pos, tokens, routes, gains, side, *parts, *deps)


def norm_back(pos, cotangent, parts, h, gates, gains, side, nt, deps=()):
    rows = h.shape[0]

    def kernel(pos_ref, cot_ref, h_ref, gate_ref, gain_ref, side_ref, *refs):
        part_refs, (dh_ref, db_ref, row_ref) = refs[:nt], refs[nt:]
        total = part_refs[0][...].astype(F32)
        for ref in part_refs[1:]:
            total = total + ref[...].astype(F32)
        pair = total[:, D:]
        pair = pair + pltpu.roll(pair, EXPERTS, 1)
        gates = gate_ref[...]
        grads = gates * (pair - jnp.sum(gates * pair, axis=-1, keepdims=True))
        low = grads.astype(BF16)
        dn2 = total[:, :D] + dot_nt(low, side_ref[...])
        h = h_ref[...]
        inverse = rms_inverse(h)
        gain_row = jnp.sum(dn2 * h * inverse, axis=0, keepdims=True)
        row_ref[...] = jnp.broadcast_to(gain_row, (8, D))
        dh = cot_ref[...].astype(F32) + norm_backward(h, inverse, gain_ref[1:2], dn2)
        dh_ref[...] = dh
        db_ref[:, :D] = dh.astype(BF16)
        db_ref[:, D:] = low

    whole = lambda i, pos: (0, 0)
    mine = lambda i, pos: (pos[1], 0)
    return pl.pallas_call(
        without(kernel, 6 + nt, len(deps)),
        out_shape=[shape((rows, D), F32), shape((rows, D + SIDE), BF16), shape((8, D), F32)],
        grid_spec=pltpu.PrefetchScalarGridSpec(
            num_scalar_prefetch=1,
            grid=(1,),
            in_specs=[
                pl.BlockSpec((rows, D), mine),
                pl.BlockSpec((rows, D), whole),
                pl.BlockSpec((rows, SIDE), whole),
                pl.BlockSpec((8, D), whole),
                pl.BlockSpec((D, SIDE), whole),
            ]
            + [pl.BlockSpec((rows, D + SIDE), whole)] * nt
            + [HBM] * len(deps),
            out_specs=[
                pl.BlockSpec((rows, D), whole),
                pl.BlockSpec((rows, D + SIDE), whole),
                pl.BlockSpec((8, D), whole),
            ],
        ),
        compiler_params=params(),
        cost_estimate=cost(100),
        name="norm_back",
    )(pos, cotangent, h, gates, gains, side, *parts, *deps)


def input_gradient(pos, tokens, parts, dh, gains, deps=()):
    rows = dh.shape[0]

    def kernel(pos_ref, x_ref, dh_ref, gain_ref, *refs):
        part_refs, out_ref = refs[:2], refs[2]
        total = part_refs[0][...].astype(F32)
        for ref in part_refs[1:]:
            total = total + ref[...].astype(F32)
        x = x_ref[...].astype(F32)
        out_ref[...] = (
            dh_ref[...] + norm_backward(x, rms_inverse(x), gain_ref[0:1], total)
        ).astype(BF16)

    whole = lambda i, pos: (0, 0)
    return pl.pallas_call(
        without(kernel, 6, len(deps)),
        out_shape=shape((rows, D), BF16),
        grid_spec=pltpu.PrefetchScalarGridSpec(
            num_scalar_prefetch=1,
            grid=(1,),
            in_specs=[
                pl.BlockSpec((rows, D), lambda i, pos: (pos[1], 0)),
                pl.BlockSpec((rows, D), whole),
                pl.BlockSpec((8, D), whole),
            ]
            + [pl.BlockSpec((rows, D), whole)] * 2
            + [HBM] * len(deps),
            out_specs=pl.BlockSpec((rows, D), whole),
        ),
        compiler_params=params(),
        cost_estimate=cost(0.1),
        name="input_gradient",
    )(pos, tokens, dh, gains, *parts, *deps)


def fold(kept, received, rows, deps=()):
    total, columns = kept.shape

    def kernel(kept_ref, received_ref, even_ref, odd_ref):
        for k in range(total // rows):
            span = slice(k * rows, (k + 1) * rows)
            to = (even_ref, odd_ref)[k % 2]
            to[k // 2 * rows : (k // 2 + 1) * rows, :] = (
                kept_ref[span, :].astype(F32) + received_ref[span, :].astype(F32)
            ).astype(BF16)

    return pl.pallas_call(
        without(kernel, 2, len(deps)),
        out_shape=[shape((total // 2, columns), BF16)] * 2,
        in_specs=[VMEM] * 2 + [HBM] * len(deps),
        out_specs=[VMEM] * 2,
        compiler_params=params(),
        cost_estimate=cost(0.1),
        name="fold",
    )(kept, received, *deps)


def pick_rows(pos, array, nt, deps=()):
    total, features = array.shape
    rows = total // nt

    def kernel(pos_ref, array_ref, *out_refs):
        for d in range(nt):
            start = pl.multiple_of((pos_ref[1] ^ d) * rows, 16)
            out_refs[d][...] = array_ref[pl.ds(start, rows), :]

    return pl.pallas_call(
        without(kernel, 2, len(deps)),
        out_shape=[shape((rows, features), array.dtype)] * nt,
        in_specs=[SMEM, VMEM] + [HBM] * len(deps),
        out_specs=[VMEM] * nt,
        compiler_params=params(),
        cost_estimate=cost(0.1),
        name="pick_rows",
    )(pos, array, *deps)


def place_rows(pos, arrays, order, rows, deps=()):
    features = arrays[0].shape[1]
    blocks = [(n, k) for n, array in enumerate(arrays) for k in range(array.shape[0] // rows)]

    def kernel(pos_ref, *refs):
        for (n, k), d in zip(blocks, order):
            start = pl.multiple_of((pos_ref[1] ^ d) * rows, 16)
            refs[-1][pl.ds(start, rows), :] = refs[n][k * rows : (k + 1) * rows, :]

    return pl.pallas_call(
        without(kernel, 1 + len(arrays), len(deps)),
        out_shape=shape((rows * len(order), features), arrays[0].dtype),
        in_specs=[SMEM] + [VMEM] * len(arrays) + [HBM] * len(deps),
        out_specs=VMEM,
        compiler_params=params(),
        cost_estimate=cost(0.1),
        name="place_rows",
    )(pos, *arrays, *deps)


def spread_rows(slots, source, target, pair, number, cut):
    for begin in range(0, source.shape[2], cut):
        span = slice(begin, min(begin + cut, source.shape[2]))
        two = [dot_tn(slots[2 * pair + k], source[2 * pair + k, :, span]) for k in range(2)]
        for e in range(number):
            joined = jnp.concatenate([rows[e * CAP : (e + 1) * CAP] for rows in two], axis=0)
            target(e, span, joined)


def sum_rows(slots, results, target, pair, number, total, cut):
    at = slice(pair * 2 * CAP, (pair + 1) * 2 * CAP)
    for begin in range(0, total, cut):
        span = slice(begin, min(begin + cut, total))
        blocks = [results[e, at, span].astype(F32) for e in range(number)]
        for k in range(2):
            rows = jnp.concatenate([b[k * CAP : (k + 1) * CAP] for b in blocks], axis=0)
            target[2 * pair + k, :, span] = dot(slots[2 * pair + k], rows.astype(BF16)).astype(BF16)


def route_cotangent(pos, pieces, weights, nf, top, deps=()):
    number = weights.shape[0]
    length = sum(rows for index, _, _, _, rows in pieces if index == 0)
    slots = number * CAP
    arrays = arrays_of(pieces)
    count = len(arrays)

    def kernel(pos_ref, *refs):
        piece_refs, (slot_ref, rows_ref, cot, spread, sems) = refs[:count], refs[count:]
        e = pl.program_id(0)
        f = pos_ref[0]

        @pl.when(e == 0)
        def _():
            copies = start_fetch(
                pieces, piece_refs, lambda i, row, n: cot.at[i, pl.ds(row, n), :], sems, f
            )
            column = lanes((length, slots))
            expert = jnp.zeros((length, slots), jnp.int32)
            for k in range(1, number):
                expert = expert + (column >= k * CAP).astype(jnp.int32)
            rank = (column - expert * CAP + 1).astype(F32)
            expert = (expert + f * number).astype(F32)
            lower = (
                lax.broadcasted_iota(jnp.int32, (length, length), 0) >= lanes((length, length))
            ).astype(F32).astype(BF16)
            for copy in copies:
                copy.wait()
            for s in range(nf):
                named = cot[s, :, D:].astype(F32)
                hit = named[:, 0:1] == expert
                for j in range(1, top):
                    hit = hit | (named[:, j : j + 1] == expert)
                hit = jnp.where(hit, 1.0, 0.0)
                so_far = dot(lower, hit.astype(BF16))
                slot_ref[s] = jnp.where((so_far == rank) & (hit > 0.0), 1.0, 0.0).astype(BF16)
            for pair in range(nf // 2):
                at = slice(pair * 2 * CAP, (pair + 1) * 2 * CAP)

                def put(k, span, rows):
                    spread[k, at, span] = rows.astype(BF16)

                spread_rows(slot_ref, cot.at[:, :, :D], put, pair, number, 512)

        rows_ref[0] = spread[e]

    return pl.pallas_call(
        without(kernel, 1 + count, len(deps)),
        out_shape=[
            shape((nf, length, slots), BF16),
            shape((number, nf * CAP, D), BF16),
        ],
        grid_spec=pltpu.PrefetchScalarGridSpec(
            num_scalar_prefetch=1,
            grid=(number,),
            in_specs=[HBM] * (count + len(deps)),
            out_specs=[
                pl.BlockSpec((nf, length, slots), lambda e, pos: (0, 0, 0)),
                pl.BlockSpec((1, nf * CAP, D), lambda e, pos: (e, 0, 0)),
            ],
            scratch_shapes=[
                pltpu.VMEM((nf, length, D + SIDE), BF16),
                pltpu.VMEM((number, nf * CAP, D), BF16),
                pltpu.SemaphoreType.DMA((len(pieces),)),
            ],
        ),
        compiler_params=params(),
        cost_estimate=cost(0.1),
        name="route_cotangent",
    )(pos, *arrays, *deps)


def down_back(grad_rows, weights, deps=()):
    number, filled, _ = grad_rows.shape
    width = weights.shape[3]

    def kernel(rows_ref, w_ref, out_ref):
        out_ref[0] = dot(rows_ref[0], w_ref[0, 0])

    return pl.pallas_call(
        without(kernel, 2, len(deps)),
        out_shape=shape((number, filled, width), F32),
        grid=(number,),
        in_specs=[
            pl.BlockSpec((1, filled, D), lambda e: (e, 0, 0)),
            pl.BlockSpec((1, 1, D, width), lambda e: (e, 2, 0, 0)),
        ]
        + [HBM] * len(deps),
        out_specs=pl.BlockSpec((1, filled, width), lambda e: (e, 0, 0)),
        compiler_params=params(),
        cost_estimate=cost(0.1),
        name="down_back",
    )(grad_rows, weights, *deps)


def run_experts(pos, pieces, slot_table, down, weights, nf, cut):
    number, _, _, width = weights.shape
    length, slots = slot_table.shape[1:]
    filled = nf * CAP
    arrays = arrays_of(pieces)
    count = len(arrays)

    def kernel(pos_ref, slot_ref, down_ref, gate_w, up_w, *refs):
        piece_refs, refs = refs[:count], refs[count:]
        rows_ref, dg_ref, du_ref, hidden_ref = refs[:4]
        sums_refs = (refs[4:6], refs[6:8])
        wide, spread, gates, results, sems, out_sems = refs[8:]
        e = pl.program_id(0)
        f = pos_ref[0]

        @pl.when(e == 0)
        def _():
            copies = start_fetch(
                pieces, piece_refs, lambda i, row, n: wide.at[i, pl.ds(row, n), :], sems
            )
            for copy in copies:
                copy.wait()
            for pair in range(nf // 2):
                at = slice(pair * 2 * CAP, (pair + 1) * 2 * CAP)

                def put(k, span, rows):
                    if span.start < D:
                        spread[k, at, span] = rows.astype(BF16)
                    else:
                        lane = lanes((2 * CAP, SIDE))
                        own = f * number + k
                        gate = jnp.where((lane == own) | (lane == own + EXPERTS), rows, 0.0)
                        gates[k, at, :] = jnp.broadcast_to(
                            jnp.sum(gate, axis=-1, keepdims=True), (2 * CAP, SIDE)
                        )

                spread_rows(slot_ref, wide, put, pair, number, 512)

        rows = spread[e]
        rows_ref[0] = rows
        first, second = gate_w[0, 0], up_w[0, 0]
        gate_pre = dot(rows, first)
        up_pre = dot(rows, second)
        gate = gates[e][:, 0:1]
        sigma = jax.nn.sigmoid(gate_pre)
        swish = gate_pre * sigma
        hidden = (swish * up_pre).astype(BF16).astype(F32)
        hidden_ref[0] = (gate * hidden).astype(BF16)
        unscaled = down_ref[0]
        grad_hidden = gate * unscaled
        dg = (grad_hidden * up_pre * sigma * (1.0 + gate_pre * (1.0 - sigma))).astype(BF16)
        du = (grad_hidden * swish).astype(BF16)
        dg_ref[0] = dg
        du_ref[0] = du
        results[e, :, :D] = (dot_nt(dg, first) + dot_nt(du, second)).astype(BF16)
        pair_grad = jnp.sum(unscaled * hidden, axis=-1, keepdims=True)
        high = pair_grad.astype(BF16).astype(F32)
        lane = lanes((filled, SIDE))
        own = f * number + e
        results[e, :, D:] = jnp.where(
            lane == own, high, jnp.where(lane == own + EXPERTS, pair_grad - high, 0.0)
        ).astype(BF16)

        @pl.when(e == number - 1)
        def _():
            copies = []
            for pair in range(nf // 2):
                sum_rows(slot_ref, results, wide, pair, number, D + SIDE, 512)
                for k, to in enumerate(sums_refs):
                    index = 2 * pair + k
                    for g, span in enumerate((pl.ds(0, cut), pl.ds(cut, length - cut))):
                        copy = pltpu.make_async_copy(
                            wide.at[index, span, :], to[g].at[pair], out_sems.at[2 * index + g]
                        )
                        copy.start()
                        copies.append(copy)
            for copy in copies:
                copy.wait()

    return pl.pallas_call(
        kernel,
        out_shape=[
            shape((number, filled, D), BF16),
            shape((number, filled, width), BF16),
            shape((number, filled, width), BF16),
            shape((number, filled, width), BF16),
        ]
        + [shape((nf // 2, number, D + SIDE), BF16) for number in (cut, length - cut)] * 2,
        grid_spec=pltpu.PrefetchScalarGridSpec(
            num_scalar_prefetch=1,
            grid=(number,),
            in_specs=[
                pl.BlockSpec((nf, length, slots), lambda e, pos: (0, 0, 0)),
                pl.BlockSpec((1, filled, width), lambda e, pos: (e, 0, 0)),
                pl.BlockSpec((1, 1, D, width), lambda e, pos: (e, 0, 0, 0)),
                pl.BlockSpec((1, 1, D, width), lambda e, pos: (e, 1, 0, 0)),
            ]
            + [HBM] * count,
            out_specs=[
                pl.BlockSpec((1, filled, D), lambda e, pos: (e, 0, 0)),
                pl.BlockSpec((1, filled, width), lambda e, pos: (e, 0, 0)),
                pl.BlockSpec((1, filled, width), lambda e, pos: (e, 0, 0)),
                pl.BlockSpec((1, filled, width), lambda e, pos: (e, 0, 0)),
            ]
            + [HBM] * 4,
            scratch_shapes=[
                pltpu.VMEM((nf, length, D + SIDE), BF16),
                pltpu.VMEM((number, filled, D), BF16),
                pltpu.VMEM((number, filled, SIDE), F32),
                pltpu.VMEM((number, filled, D + SIDE), BF16),
                pltpu.SemaphoreType.DMA((len(pieces),)),
                pltpu.SemaphoreType.DMA((2 * nf,)),
            ],
        ),
        compiler_params=params(),
        cost_estimate=cost(5),
        name="run_experts",
    )(pos, slot_table, down, weights, weights, *arrays)


def expert_outputs(pos, slot_table, hidden, weights, nt, deps=()):
    number, filled, width = hidden.shape
    nf, length, slots = slot_table.shape

    rows = length // nt

    def kernel(pos_ref, slot_ref, hidden_ref, w_ref, out_ref, results, out, sems):
        e = pl.program_id(0)
        results[e] = dot_nt(hidden_ref[0], w_ref[0, 0]).astype(BF16)

        @pl.when(e == number - 1)
        def _():
            copies = []
            for pair in range(nf // 2):
                sum_rows(slot_ref, results, out, pair, number, D, 512)
                for index in (2 * pair, 2 * pair + 1):
                    for d in range(nt):
                        start = pl.multiple_of((pos_ref[1] ^ d) * rows, 16)
                        copy = pltpu.make_async_copy(
                            out.at[index, pl.ds(d * rows, rows), :],
                            out_ref.at[pos_ref[0] ^ index, pl.ds(start, rows), :],
                            sems.at[index * nt + d],
                        )
                        copy.start()
                        copies.append(copy)
            for copy in copies:
                copy.wait()

    return pl.pallas_call(
        without(kernel, 4, len(deps)),
        out_shape=shape((nf, length, D), BF16),
        grid_spec=pltpu.PrefetchScalarGridSpec(
            num_scalar_prefetch=1,
            grid=(number,),
            in_specs=[
                pl.BlockSpec((nf, length, slots), lambda e, pos: (0, 0, 0)),
                pl.BlockSpec((1, filled, width), lambda e, pos: (e, 0, 0)),
                pl.BlockSpec((1, 1, D, width), lambda e, pos: (e, 2, 0, 0)),
            ]
            + [HBM] * len(deps),
            out_specs=HBM,
            scratch_shapes=[
                pltpu.VMEM((number, filled, D), BF16),
                pltpu.VMEM((nf, length, D), BF16),
                pltpu.SemaphoreType.DMA((nf * nt,)),
            ],
        ),
        compiler_params=params(),
        cost_estimate=cost(0.1),
        name="expert_outputs",
    )(pos, slot_table, hidden, weights, *deps)


def expert_gradients(rows, grad_rows, dg, du, hidden, first, number, so_far=None, deps=()):
    everyone, filled, width = dg.shape

    def kernel(rows_ref, grad_ref, dg_ref, du_ref, hidden_ref, *refs):
        out_ref, done_ref = refs
        done_ref[...] = jnp.zeros_like(done_ref)
        rows = rows_ref[0]
        out_ref[0, 0] = dot_tn(rows, dg_ref[0])
        out_ref[0, 1] = dot_tn(rows, du_ref[0])
        out_ref[0, 2] = dot_tn(grad_ref[0], hidden_ref[0])

    tall = pl.BlockSpec((1, filled, D), lambda e: (first + e, 0, 0))
    thin = pl.BlockSpec((1, filled, width), lambda e: (first + e, 0, 0))
    before = [] if so_far is None else [so_far]
    return pl.pallas_call(
        without(kernel, 5, len(before) + len(deps)),
        out_shape=[shape((everyone, 3, D, width), F32), shape((8, SIDE), F32)],
        grid=(number,),
        in_specs=[tall, tall, thin, thin, thin] + [HBM] * (len(before) + len(deps)),
        out_specs=[
            pl.BlockSpec((1, 3, D, width), lambda e: (first + e, 0, 0, 0)),
            pl.BlockSpec((8, SIDE), lambda e: (0, 0)),
        ],
        input_output_aliases={5: 0} if before else {},
        compiler_params=params(),
        cost_estimate=cost(0.1),
        name="expert_gradients",
    )(rows, grad_rows, dg, du, hidden, *before, *deps)


def on_device(
    nf,
    nt,
    tokens,
    cotangent,
    routes,
    w_query,
    w_key,
    w_value,
    w_output,
    w_router,
    attn_gain,
    ffn_gain,
    query_gain,
    key_gain,
    expert_weights,
):
    length = tokens.shape[0]
    rows = length // nt
    block = D // nf
    group = query_gain.shape[0]
    top = routes.shape[1]
    f = lax.axis_index("fsdp").astype(jnp.int32)
    t = lax.axis_index("tensor").astype(jnp.int32)
    pos = jnp.stack([f, t])

    def placed(gain):
        return lax.dynamic_update_slice(jnp.zeros((block,), BF16), gain, (f * group,))[:, None]

    columns = [
        w_query,
        w_key,
        w_value,
        w_output,
        w_router,
        attn_gain[:, None],
        ffn_gain[:, None],
        placed(query_gain),
        placed(key_gain),
        jnp.zeros((block, SIDE - EXPERTS - 4), BF16),
    ]
    number = expert_weights.shape[0]
    cut = 2 * rows

    def around(block):
        return [block] + [swap(block, "tensor", nt, d) for d in range(1, nt)]

    def sent(parts):
        return [parts[0]] + [swap(parts[d], "tensor", nt, d) for d in range(1, nt)]

    if nf == 8:
        packed = [
            jnp.concatenate([part[half : half + block // 2] for part in columns], axis=1)
            for half in (0, block // 2)
        ]
        weights_near = [gather_near(part, nf) for part in packed]
    else:
        packed = jnp.concatenate(columns, axis=1)

    wide_cot = jnp.concatenate(
        [cotangent, routes.astype(BF16), jnp.zeros((length, SIDE - top), BF16)], axis=1
    )
    wide_cot = jnp.concatenate(
        [lax.dynamic_slice_in_dim(wide_cot, (t ^ d) * rows, rows, 0) for d in range(nt)], axis=0
    )
    position = jnp.arange(length, dtype=F32)[:, None]
    inverse = ROPE_BASE ** (-jnp.arange(HD // 2, dtype=F32) / (HD // 2))
    angles = position * inverse[None, :]
    cosine = jnp.concatenate([jnp.cos(angles)] * 2, axis=1)
    sine = jnp.concatenate([-jnp.sin(angles), jnp.sin(angles)], axis=1)

    if nf == 8:
        weights = gather_two(packed, weights_near, nf)
        wide_cot = join(
            [wide_cot],
            weights_near[0] + weights_near[1] + [w[2] for w in weights if w[0] == nf - 2],
        )
    else:
        weights = gather_rest(packed, gather_near(packed, nf), nf)
    all_cot = lax.all_gather(wide_cot, "fsdp", axis=0, tiled=True)
    cot = [(p, 0, all_cot, None, length) for p in range(nf)]
    saved, parts = attend_forward(pos, tokens, cosine, sine, weights, nf, nt)
    normed_one, _, _, _, _, attended, side, gains, _ = saved
    parts = sent(parts)
    h, normed_two, gates = norm_and_route(pos, tokens, routes, parts, gains, side, nt)

    normed_parts = around(normed_two)
    if nf == 8:
        blocks = [join(normed_parts[:2])]
        near = [gather_near(blocks[0], nf)]
        slot_table, cot_rows = route_cotangent(pos, cot, expert_weights, nf, top, deps=blocks)
        blocks.append(join(normed_parts[2:], deps=[slot_table]))
        near.append(gather_near(blocks[1], nf))
        down = down_back(cot_rows, expert_weights, deps=blocks[1:])
        sources = [near[0][1]] + list(relay(near[1][:1], [down]))
        n2_pieces = gather_two(blocks, near, nf, sources)
    else:
        slot_table, cot_rows = route_cotangent(pos, cot, expert_weights, nf, top)
        down = down_back(cot_rows, expert_weights)
        joined = join(normed_parts)
        n2_pieces = gather_rest(joined, gather_near(joined, nf), nf)
    n2_rows, dg, du, hidden, keep_near, keep_far, send_near, send_far = run_experts(
        pos, n2_pieces, slot_table, down, expert_weights, nf, cut
    )

    far, near = Reduce(keep_far, send_far, nf), Reduce(keep_near, send_near, nf)
    began = far.first() + near.first()
    outputs = expert_outputs(pos, slot_table, hidden, expert_weights, nt, deps=began)
    layer_sum = lax.psum_scatter(
        outputs.reshape(nf * length, D), "fsdp", scatter_dimension=0, tiled=True
    )
    went = far.second(deps=[outputs], micros=20)
    near.second(deps=went, micros=20)
    far_rows = list(far.rows(nt - 2))
    near_rows = list(near.rows(2, deps=far_rows[:1]))
    grad_parts = sent(near_rows + far_rows)
    each = number // 4

    def expert_part(k, deps=()):
        return expert_gradients(
            n2_rows, cot_rows, dg, du, hidden, k * each, each, grad_experts, deps
        )

    grad_experts = None
    grad_experts, done = expert_part(0, near_rows[:1])
    dh, db, ffn_row = norm_back(
        pos, cotangent, grad_parts, h, gates, gains, side, nt, deps=[done]
    )
    db_parts = around(db)
    grad_experts, done = expert_part(1, [db])
    dqkv, kept, sent_on = attend_backward(
        pos, db_parts, ffn_row, weights, saved, tokens, cosine, sine, nf, nt,
        deps=[done],
    )
    layer_parts = list(pick_rows(pos, layer_sum, nt, deps=[kept]))
    layer_rows = h
    for part in sent(layer_parts):
        layer_rows = layer_rows + part.astype(F32)
    layer_blocks = around(layer_rows.astype(BF16))
    for k in (2, 3):
        grad_experts, done = expert_part(k, [kept])
    step, deps = 1, [done]
    while step < nt // 2:
        kept, sent_on = fold(kept, swap(sent_on, "tensor", nt, step), rows, deps)
        step, deps = 2 * step, []
    keep, send = projection_gradients(pos, normed_one, dqkv, nf, deps=[kept])
    projections = Reduce(keep, send, nf)
    parts = [kept, swap(sent_on, "tensor", nt, step)]
    token_rows = input_gradient(pos, tokens, parts, dh, gains)
    pairs = projections.first(deps=[token_rows])
    blocks, order = [token_rows], [0]
    while step > 0:
        mine = blocks[0] if len(blocks) == 1 else join(blocks)
        blocks = [mine, swap(mine, "tensor", nt, step)]
        order, step = order + [d ^ step for d in order], step // 2
    grad_tokens = place_rows(pos, blocks, order, rows)
    layer_out = place_rows(pos, layer_blocks, range(nt), rows, deps=blocks[:1])
    keep, send = output_gradients(
        pos, attended, db_parts, normed_parts, parts, group, nf, nt, deps=pairs + layer_blocks[:1]
    )
    output = Reduce(keep, send, nf)
    projections.second()
    output.first()
    output.second()
    width = attended.shape[1]
    weight_grads, out_sum = projections.total(), output.total()
    return (
        layer_out,
        grad_tokens,
        weight_grads[:, :width],
        weight_grads[:, width : 2 * width],
        weight_grads[:, 2 * width :],
        out_sum[:, :width],
        out_sum[:, width : width + EXPERTS],
        out_sum[:, width + EXPERTS + 1],
        out_sum[:, width + EXPERTS],
        out_sum[:group, width + EXPERTS + 2],
        out_sum[:group, width + EXPERTS + 3],
        grad_experts,
    )


def solution(mesh):
    nf, nt = mesh.shape["fsdp"], mesh.shape["tensor"]
    rows, both, line = P("fsdp", None), P("fsdp", "tensor"), P("fsdp")
    experts = P("fsdp", None, None, "tensor")
    return jax.shard_map(
        functools.partial(on_device, nf, nt),
        mesh=mesh,
        in_specs=(rows, rows, rows, both, both, both, both, rows, line, line, line, line, experts),
        out_specs=(rows, rows, both, both, both, both, rows, line, line, line, line, experts),
        check_vma=False,
    )
```

time: 591 us -> 490 us (0.83)
  waiting for transfers between devices: 292 us -> 148 us
  Pallas kernels: 144 us -> 198 us
  other arithmetic: 27.5 us -> 10.9 us
  local copies, waits for them, and re-layouts: 27.6 us -> 34.8 us
    ppermute x72 -> x70, waiting for transfers between devices: 260 us -> 148 us  [swap(): return lax.ppermute(block, axis, [(i, i ^ step) for i in range(size)])]
    pallas_call x10 -> x33, Pallas kernels: 110 us -> 164 us  [the longest x4 34.3 us: expert_gradients(): pl.pallas_call(without(kernel, 5, len(before) + len(deps)), out_shape=[sh...]
    psum x1 -> x0, waiting for transfers between devices: 32.3 us -> none  [on_device(): small = lax.psum(weight_grads[:, 4 * width:], 'tensor')]
    another operation x11 -> x0, other arithmetic: 13.3 us -> none
    unnamed x112 -> x142, local copies, waits for them, and re-layouts: 12.5 us -> 24.3 us
    ppermute x72 -> x70, starting transfers between devices: 75.3 us -> 75.4 us  [swap(): return lax.ppermute(block, axis, [(i, i ^ step) for i in range(size)])]
  transfers between devices with their start and end apart: 74 -> 72, of which waited for: 29 -> 26; matrix products, arithmetic and copies ran while one was open for 4% -> 2% of each run, Pallas kernels for 19% -> 33%
where the time goes in v2:
time: 490 us; the launch traced here: 482 us
  Pallas kernels  198 us (40%)
  waiting for transfers between devices  148 us (30%)
  starting transfers between devices  75.5 us (15%)
  local copies, waits for them, and re-layouts  34.8 us (7%)
  between operations  15 us (3%)
  other arithmetic  10.9 us (2%)
    ppermute x70, waiting for transfers between devices, swap(): return lax.ppermute(block, axis, [(i, i ^ step) for i in range(size)])  148 us
    ppermute x70, starting transfers between devices, swap(): return lax.ppermute(block, axis, [(i, i ^ step) for i in range(size)])  75.4 us
    pallas_call x4, Pallas kernels, expert_gradients(): pl.pallas_call(without(kernel, 5, len(before) + len(deps)), out_shape=[sh...  34.3 us
    pallas_call x1, Pallas kernels, run_experts(): pl.pallas_call(kernel, out_shape=[shape((number, filled, D), BF16), shape...  34 us
    unnamed x142, local copies, waits for them, and re-layouts  24.3 us
    pallas_call x1, Pallas kernels, route_cotangent(): pl.pallas_call(without(kernel, 1 + count, len(deps)), out_shape=[shape((n...  16.7 us
    pallas_call x1, Pallas kernels, expert_outputs(): pl.pallas_call(without(kernel, 4, len(deps)), out_shape=shape((nf, length...  15.9 us
    pallas_call x1, Pallas kernels, attend_backward(): pl.pallas_call(without(kernel, 11 + nt + count, len(deps)), out_shape=[sh...  12.4 us
  transfers between devices with their start and end apart: 72, of which 26 were waited for; matrix products, arithmetic and copies ran while one was open for 2% of the time, Pallas kernels for 33%

profile of v2, /device:TPU:0, one launch (start us, length us, event | category | flops | bytes accessed | tf_op | source)
XLA Modules:
  0.0 482.1 jit_solution(10354374145212629712)
XLA Ops:
  22.5 8.1 %collective-permute-done.3.refs_8_.refs_2_.refs_19_ = bf16[128,2176]{1,0:T(8,128)(2,1)S(1)} collective-permute-done((bf16[128,2176]{1,0:T(8,128)(2,1)S(1)}, bf16[128,2176]{1,0:T(8,128)(2,1)S(1)}, u32[]{:S(2)}, u32[]{:S(2)}) %collective-permute-start.3) | collective-permute-done | bytes 557088 | tf_op jit(solution)/shard_map/ppermute | solution.py:72
  35.3 10.2 %collective-permute-done.1.refs_6_.refs_1_.refs_17_ = bf16[128,2176]{1,0:T(8,128)(2,1)} collective-permute-done((bf16[128,2176]{1,0:T(8,128)(2,1)S(1)}, bf16[128,2176]{1,0:T(8,128)(2,1)}, u32[]{:S(2)}, u32[]{:S(2)}) %collective-permute-start.1) | collective-permute-done | bytes 557088 | tf_op jit(solution)/shard_map/ppermute | solution.py:72
  45.5 10.4 %collective-permute-done.5.refs_10_.refs_5_.refs_21_ = bf16[128,2176]{1,0:T(8,128)(2,1)S(1)} collective-permute-done((bf16[128,2176]{1,0:T(8,128)(2,1)S(1)}, bf16[128,2176]{1,0:T(8,128)(2,1)S(1)}, u32[]{:S(2)}, u32[]{:S(2)}) %collective-permute-start.5) | collective-permute-done | bytes 557088 | tf_op jit(solution)/shard_map/ppermute | solution.py:72
  68.5 10.1 %attend_forward.1 = (bf16[256,2048]{1,0:T(8,128)(2,1)}, f32[256,1024]{1,0:T(8,128)}, bf16[256,1024]{1,0:T(8,128)(2,1)}, bf16[256,512]{1,0:T(8,128)(2,1)}, f32[4,...) custom-call(s32[2]{0:T(128)} %pad_add_fusion.refs_0_.pos_ref, ...), custom_call_target="tpu_custom_call" | custom-call | flops 5000000000 | bytes 15000000 | tf_op jit(solution)/shard_map/attend_forward/pallas_call | solution.py:418
  83.8 8.7 %collective-permute-done.14.refs_6_ = bf16[64,2048]{1,0:T(8,128)(2,1)S(1)} collective-permute-done((bf16[64,2048]{1,0:T(8,128)(2,1)}, bf16[64,2048]{1,0:T(8,128)(2,1)S(1)}, u32[]{:S(2)}, u32[]{:S(2)}) %collective-permute-start.14) | collective-permute-done | bytes 262176 | tf_op jit(solution)/shard_map/ppermute | solution.py:72
  92.5 9.4 %collective-permute-done.15.refs_7_ = bf16[64,2048]{1,0:T(8,128)(2,1)S(1)} collective-permute-done((bf16[64,2048]{1,0:T(8,128)(2,1)}, bf16[64,2048]{1,0:T(8,128)(2,1)S(1)}, u32[]{:S(2)}, u32[]{:S(2)}) %collective-permute-start.15) | collective-permute-done | bytes 262176 | tf_op jit(solution)/shard_map/ppermute | solution.py:72
  106.3 5.2 %collective-permute-start.17 = (bf16[64,2176]{1,0:T(8,128)(2,1)}, bf16[64,2176]{1,0:T(8,128)(2,1)S(1)}, u32[]{:S(2)}, u32[]{:S(2)}) collective-permute-start(bf16[64,2176]{1,0:T(8,128)(2,1)} %get-tuple-element.88.refs_0_.refs_6_), channel_id=1, source_target_pairs={{0,1},{1,0},{2,3},{3,2},{4,5},{5,4},{6,7},{7,6},{8,9},{9,8},{10,11... | collective-permute-start | bytes 835592 | tf_op jit(solution)/shard_map/ppermute | solution.py:72
  113.9 5.0 %collective-permute-done.17.refs_1_.refs_7_ = bf16[64,2176]{1,0:T(8,128)(2,1)S(1)} collective-permute-done((bf16[64,2176]{1,0:T(8,128)(2,1)}, bf16[64,2176]{1,0:T(8,128)(2,1)S(1)}, u32[]{:S(2)}, u32[]{:S(2)}) %collective-permute-start.17) | collective-permute-done | bytes 278560 | tf_op jit(solution)/shard_map/ppermute | solution.py:72
  123.3 16.7 %route_cotangent.1 = (bf16[8,256,320]{2,1,0:T(8,128)(2,1)}, bf16[8,320,2048]{2,1,0:T(8,128)(2,1)}) custom-call(s32[2]{0:T(128)} %pad_add_fusion.refs_0_.pos_ref, bf16[2048,2176]{1,0:T(8,128)(2,1)} %all-gather.2.cloned.1.call-done.refs_1_, bf16[128,2176]{1,0:T(8,128)(2,1)} %joins.6.refs_2_.refs_0_), custom_call_target="tpu_custom_call" | custom-call | flops 100000000 | bytes 300000 | tf_op jit(solution)/shard_map/route_cotangent/pallas_call | solution.py:897
  145.3 11.0 %down_back.1.refs_1_.down_ref = f32[8,320,256]{2,1,0:T(8,128)} custom-call(bf16[8,320,2048]{2,1,0:T(8,128)(2,1)} %get-tuple-element.90.refs_0_.refs_1_, bf16[8,3,2048,256]{3,2,1,0:T(8,128)(2,1)} %refs_3_.1, bf16[128,2176]{1,0:T(8,128)(2,1)} %joins.7.refs_2_.refs_8_), custom_call_target="tpu_custom_call" | custom-call | flops 100000000 | bytes 300000 | tf_op jit(solution)/shard_map/down_back/pallas_call | solution.py:930
  166.9 7.2 %collective-permute-done.30.refs_12_ = bf16[128,2176]{1,0:T(8,128)(2,1)} collective-permute-done((bf16[128,2176]{1,0:T(8,128)(2,1)S(1)}, bf16[128,2176]{1,0:T(8,128)(2,1)}, u32[]{:S(2)}, u32[]{:S(2)}) %collective-permute-start.30) | collective-permute-done | bytes 557088 | tf_op jit(solution)/shard_map/ppermute | solution.py:72
  174.2 8.9 %collective-permute-done.32.refs_14_ = bf16[128,2176]{1,0:T(8,128)(2,1)S(1)} collective-permute-done((bf16[128,2176]{1,0:T(8,128)(2,1)}, bf16[128,2176]{1,0:T(8,128)(2,1)S(1)}, u32[]{:S(2)}, u32[]{:S(2)}) %collective-permute-start.32) | collective-permute-done | bytes 557088 | tf_op jit(solution)/shard_map/ppermute | solution.py:72
  185.2 34.0 %run_experts.1 = (bf16[8,320,2048]{2,1,0:T(8,128)(2,1)}, bf16[8,320,256]{2,1,0:T(8,128)(2,1)}, bf16[8,320,256]{2,1,0:T(8,128)(2,1)}, bf16[8,320,256]{2,1,0:T(8,1...) custom-call(s32[2]{0:T(128)} %pad_add_fusion.refs_0_.pos_ref, ...), custom_call_target="tpu_custom_call" | custom-call | flops 5000000000 | bytes 15000000 | tf_op jit(solution)/shard_map/run_experts/pallas_call | solution.py:1025
  219.7 6.0 %collective-permute-done.34.refs_1_.refs_3_.refs_4_.refs_5_ = bf16[4,128,2176]{2,1,0:T(8,128)(2,1)} collective-permute-done((bf16[4,128,2176]{2,1,0:T(8,128)(2,1)}, bf16[4,128,2176]{2,1,0:T(8,128)(2,1)}, u32[]{:S(2)}, u32[]{:S(2)}) %collective-permute-start.34) | collective-permute-done | bytes 2228256 | tf_op jit(solution)/shard_map/ppermute | solution.py:72
  236.0 15.9 %expert_outputs.1.refs_6_ = bf16[8,256,2048]{2,1,0:T(8,128)(2,1)} custom-call(s32[2]{0:T(128)} %pad_add_fusion.refs_0_.pos_ref, bf16[8,256,320]{2,1,0:T(8,128)(2,1)} %get-tuple-element.89.refs_2_.slot_ref.refs_1_, bf16[8,320,256]{2,1,0:T(8,128)(2,1)} %get-tuple-element.91.refs_2_.refs_4_, bf16[8,3,2048,256]{3,2,1,0:T(8,128)(2,1)} %refs_3_.1, ...), custom_call_target="tpu_custom_call" | custom-call | flops 100000000 | bytes 300000 | tf_op jit(solution)/shard_map/expert_outputs/pallas_call | solution.py:1094
  276.5 8.4 %expert_gradients.4 = (f32[8,3,2048,256]{3,2,1,0:T(8,128)}, f32[8,128]{1,0:T(8,128)}) custom-call(bf16[8,320,2048]{2,1,0:T(8,128)(2,1)} %get-tuple-element.114.refs_0_, bf16[8,320,2048]{2,1,0:T(8,128)(2,1)} %get-tuple-element.90.refs_0_.refs_1_, bf16[8,320,256]{2,1,0:T(8,128)(2,1)} %get-tuple-element.115.refs_2_, ...), custom_call_target="tpu_custom_call" | custom-call | flops 100000000 | bytes 300000 | tf_op jit(solution)/shard_map/expert_gradients/pallas_call | solution.py:1133
  285.0 9.2 %collective-permute-done.45.refs_8_ = bf16[64,2176]{1,0:T(8,128)(2,1)S(1)} collective-permute-done((bf16[64,2176]{1,0:T(8,128)(2,1)}, bf16[64,2176]{1,0:T(8,128)(2,1)S(1)}, u32[]{:S(2)}, u32[]{:S(2)}) %collective-permute-start.45) | collective-permute-done | bytes 278560 | tf_op jit(solution)/shard_map/ppermute | solution.py:72
  295.0 3.9 norm_back.1
  303.3 8.8 %expert_gradients.5 = (f32[8,3,2048,256]{3,2,1,0:T(8,128)}, f32[8,128]{1,0:T(8,128)}) custom-call(bf16[8,320,2048]{2,1,0:T(8,128)(2,1)} %get-tuple-element.114.refs_0_, bf16[8,320,2048]{2,1,0:T(8,128)(2,1)} %get-tuple-element.90.refs_0_.refs_1_, bf16[8,320,256]{2,1,0:T(8,128)(2,1)} %get-tuple-element.115.refs_2_, ...), custom_call_target="tpu_custom_call", output_to_operand_aliasing={{0}: (5, {})} | custom-call | flops 100000000 | bytes 300000 | tf_op jit(solution)/shard_map/expert_gradients/pallas_call | solution.py:1133
  312.1 12.1 %collective-permute-done.48.refs_13_.refs_4_ = bf16[64,2176]{1,0:T(8,128)(2,1)S(1)} collective-permute-done((bf16[64,2176]{1,0:T(8,128)(2,1)}, bf16[64,2176]{1,0:T(8,128)(2,1)S(1)}, u32[]{:S(2)}, u32[]{:S(2)}) %collective-permute-start.48) | collective-permute-done | bytes 278560 | tf_op jit(solution)/shard_map/ppermute | solution.py:72
  325.0 12.4 %attend_backward.1 = (bf16[256,1536]{1,0:T(8,128)(2,1)}, bf16[128,2176]{1,0:T(8,128)(2,1)}, bf16[128,2176]{1,0:T(8,128)(2,1)}) custom-call(s32[2]{0:T(128)} %pad_add_fusion.refs_0_.pos_ref, bf16[256,2048]{1,0:T(8,128)(2,1)} %refs_1_.11, f32[256,128]{1,0:T(8,128)} %get-tuple-element.216.refs_2_, f32[256,128]{1,0:T(8,128)} %get-tuple-element.217.refs_3_, ...), custom_call_target="tpu_custom_call" | custom-call | flops 100000000 | bytes 300000 | tf_op jit(solution)/shard_map/attend_backward/pallas_call | solution.py:523
  337.5 8.5 %expert_gradients.6 = (f32[8,3,2048,256]{3,2,1,0:T(8,128)}, f32[8,128]{1,0:T(8,128)}) custom-call(bf16[8,320,2048]{2,1,0:T(8,128)(2,1)} %get-tuple-element.114.refs_0_, bf16[8,320,2048]{2,1,0:T(8,128)(2,1)} %get-tuple-element.90.refs_0_.refs_1_, bf16[8,320,256]{2,1,0:T(8,128)(2,1)} %get-tuple-element.115.refs_2_, ...), custom_call_target="tpu_custom_call", output_to_operand_aliasing={{0}: (5, {})} | custom-call | flops 100000000 | bytes 300000 | tf_op jit(solution)/shard_map/expert_gradients/pallas_call | solution.py:1133
  346.0 8.5 %expert_gradients.7 = (f32[8,3,2048,256]{3,2,1,0:T(8,128)}, f32[8,128]{1,0:T(8,128)}) custom-call(bf16[8,320,2048]{2,1,0:T(8,128)(2,1)} %get-tuple-element.114.refs_0_, bf16[8,320,2048]{2,1,0:T(8,128)(2,1)} %get-tuple-element.90.refs_0_.refs_1_, bf16[8,320,256]{2,1,0:T(8,128)(2,1)} %get-tuple-element.115.refs_2_, ...), custom_call_target="tpu_custom_call", output_to_operand_aliasing={{0}: (5, {})} | custom-call | flops 100000000 | bytes 300000 | tf_op jit(solution)/shard_map/expert_gradients/pallas_call | solution.py:1133
  357.4 5.7 %projection_gradients.1 = (bf16[4,256,1536]{2,1,0:T(8,128)(2,1)}, bf16[4,256,1536]{2,1,0:T(8,128)(2,1)}) custom-call(s32[2]{0:T(128)} %pad_add_fusion.refs_0_.pos_ref, bf16[256,2048]{1,0:T(8,128)(2,1)} %get-tuple-element.134.refs_1_, bf16[256,1536]{1,0:T(8,128)(2,1)} %get-tuple-element.135.refs_2_, bf16[64,2176]{1,0:T(8,128)(2,1)} %get-tuple-element.132.refs_4_.refs_3_.refs_10_), custom_call_target="tpu_custom_call" | custom-call | flops 100000000 | bytes 300000 | tf_op jit(solution)/shard_map/projection_gradients/pallas_call | solution.py:558
  372.6 7.2 %collective-permute-done.57.refs_5_.refs_11_ = bf16[64,2176]{1,0:T(8,128)(2,1)S(1)} collective-permute-done((bf16[64,2176]{1,0:T(8,128)(2,1)}, bf16[64,2176]{1,0:T(8,128)(2,1)S(1)}, u32[]{:S(2)}, u32[]{:S(2)}) %collective-permute-start.57) | collective-permute-done | bytes 278560 | tf_op jit(solution)/shard_map/ppermute | solution.py:72
  388.3 8.4 %collective-permute-done.51 = bf16[64,2048]{1,0:T(8,128)(2,1)} collective-permute-done((bf16[64,2048]{1,0:T(8,128)(2,1)}, bf16[64,2048]{1,0:T(8,128)(2,1)}, u32[]{:S(2)}, u32[]{:S(2)}) %collective-permute-start.51) | collective-permute-done | bytes 262176 | tf_op jit(solution)/shard_map/ppermute | solution.py:72
  398.7 5.1 %output_gradients.1 = (bf16[4,256,640]{2,1,0:T(8,128)(2,1)}, bf16[4,256,640]{2,1,0:T(8,128)(2,1)}) custom-call(s32[2]{0:T(128)} %pad_add_fusion.refs_0_.pos_ref, bf16[256,512]{1,0:T(8,128)(2,1)} %get-tuple-element.142.refs_1_, bf16[64,2176]{1,0:T(8,128)(2,1)} %get-tuple-element.119.refs_6_.refs_11_.refs_2_, bf16[64,2176]{1,0:T(8,128)(2,1)} %copy-done.25, ...), custom_call_target="tpu_custom_call" | custom-call | flops 100000000 | bytes 300000 | tf_op jit(solution)/shard_map/output_gradients/pallas_call | solution.py:610
  406.5 6.5 %collective-permute-start.58 = (bf16[64,2048]{1,0:T(8,128)(2,1)S(1)}, bf16[64,2048]{1,0:T(8,128)(2,1)}, u32[]{:S(2)}, u32[]{:S(2)}) collective-permute-start(bf16[64,2048]{1,0:T(8,128)(2,1)S(1)} %copy-done.6), channel_id=1, source_target_pairs={{0,2},{1,3},{2,0},{3,1},{4,6},{5,7},{6,4},{7,5},{8,10},{9,11},{10,... | collective-permute-start | bytes 786440 | tf_op jit(solution)/shard_map/ppermute | solution.py:72
  413.0 12.1 %collective-permute-done.58.refs_1_ = bf16[64,2048]{1,0:T(8,128)(2,1)} collective-permute-done((bf16[64,2048]{1,0:T(8,128)(2,1)S(1)}, bf16[64,2048]{1,0:T(8,128)(2,1)}, u32[]{:S(2)}, u32[]{:S(2)}) %collective-permute-start.58) | collective-permute-done | bytes 262176 | tf_op jit(solution)/shard_map/ppermute | solution.py:72
  444.5 4.5 collective-permute-done.66.refs_2_
  449.0 5.2 %collective-permute-start.54 = (bf16[64,2048]{1,0:T(8,128)(2,1)S(1)}, bf16[64,2048]{1,0:T(8,128)(2,1)S(1)}, u32[]{:S(2)}, u32[]{:S(2)}) collective-permute-start(bf16[64,2048]{1,0:T(8,128)(2,1)S(1)} %copy-done.5), channel_id=1, source_target_pairs={{0,2},{1,3},{2,0},{3,1},{4,6},{5,7},{6,4},{7,5},{8,10},{9,11},{10,... | collective-permute-start | bytes 786440 | tf_op jit(solution)/shard_map/ppermute | solution.py:72
  461.3 5.7 %collective-permute-done.54.refs_3_ = bf16[64,2048]{1,0:T(8,128)(2,1)S(1)} collective-permute-done((bf16[64,2048]{1,0:T(8,128)(2,1)S(1)}, bf16[64,2048]{1,0:T(8,128)(2,1)S(1)}, u32[]{:S(2)}, u32[]{:S(2)}) %collective-permute-start.54) | collective-permute-done | bytes 262176 | tf_op jit(solution)/shard_map/ppermute | solution.py:72
  (327 shorter events, 168.2 us)
Async XLA Ops:
  7.2 116.1 %all-gather.2.cloned.1.call-start = ((), (), s32[]{:S(2)}) async-start(), calls=%async_computation.1 | async-start | bytes 10027008 | tf_op jit(solution)/shard_map/all_gather | solution.py:1228
  19.4 26.1 %collective-permute-start.1 = (bf16[128,2176]{1,0:T(8,128)(2,1)S(1)}, bf16[128,2176]{1,0:T(8,128)(2,1)}, u32[]{:S(2)}, u32[]{:S(2)}) collective-permute-start(bf16[128,2176]{1,0:T(8,128)(2,1)S(1)} %concatenate.26.refs_4_.refs_15_), channel_id=1, source_target_pairs={{0,8},{4,12},{8,0},{12,4},{16,24},{20,28},{24,16},{28,20},{1,9},{5... | collective-permute-start | bytes 1671176 | tf_op jit(solution)/shard_map/ppermute | solution.py:72
  19.9 25.6 %collective-permute-start.10 = (bf16[128,2176]{1,0:T(8,128)(2,1)S(1)}, bf16[128,2176]{1,0:T(8,128)(2,1)}, u32[]{:S(2)}, u32[]{:S(2)}) collective-permute-start(bf16[128,2176]{1,0:T(8,128)(2,1)S(1)} %concatenate.27.refs_12_.refs_23_), channel_id=1, source_target_pairs={{0,16},{4,20},{8,24},{12,28},{16,0},{20,4},{24,8},{28,12},{1,17},{... | collective-permute-start | bytes 1671176 | tf_op jit(solution)/shard_map/ppermute | solution.py:72
  30.6 25.3 %collective-permute-start.5 = (bf16[128,2176]{1,0:T(8,128)(2,1)S(1)}, bf16[128,2176]{1,0:T(8,128)(2,1)S(1)}, u32[]{:S(2)}, u32[]{:S(2)}) collective-permute-start(bf16[128,2176]{1,0:T(8,128)(2,1)S(1)} %collective-permute-done.3.refs_8_.refs_2_.refs_19_), channel_id=1, source_target_pairs={{0,8},{4,12},{8,0},{12,4},{16,24},{20,28},{24,16},{28,20},{1,9},{5... | collective-permute-start | bytes 1671176 | tf_op jit(solution)/shard_map/ppermute | solution.py:72
  33.4 22.4 %collective-permute-start.12 = (bf16[128,2176]{1,0:T(8,128)(2,1)S(1)}, bf16[128,2176]{1,0:T(8,128)(2,1)}, u32[]{:S(2)}, u32[]{:S(2)}) collective-permute-start(bf16[128,2176]{1,0:T(8,128)(2,1)S(1)} %collective-permute-done.8.refs_14_.refs_3_.refs_25_), channel_id=1, source_target_pairs={{0,16},{4,20},{8,24},{12,28},{16,0},{20,4},{24,8},{28,12},{1,17},{... | collective-permute-start | bytes 1671176 | tf_op jit(solution)/shard_map/ppermute | solution.py:72
  59.0 306.9 %reduce-scatter.2.cloned.1.call-start = ((), (), s32[]{:S(2)}) async-start(), calls=%async_computation.2 | async-start | bytes 9437184 | tf_op jit(solution)/shard_map/reduce_scatter | solution.py:1257
  80.4 21.6 %collective-permute-start.15 = (bf16[64,2048]{1,0:T(8,128)(2,1)}, bf16[64,2048]{1,0:T(8,128)(2,1)S(1)}, u32[]{:S(2)}, u32[]{:S(2)}) collective-permute-start(bf16[64,2048]{1,0:T(8,128)(2,1)} %get-tuple-element.85), channel_id=1, source_target_pairs={{0,2},{1,3},{2,0},{3,1},{4,6},{5,7},{6,4},{7,5},{8,10},{9,11},{10,... | collective-permute-start | bytes 786440 | tf_op jit(solution)/shard_map/ppermute | solution.py:72
  82.9 19.0 %collective-permute-start.16 = (bf16[64,2048]{1,0:T(8,128)(2,1)}, bf16[64,2048]{1,0:T(8,128)(2,1)S(1)}, u32[]{:S(2)}, u32[]{:S(2)}) collective-permute-start(bf16[64,2048]{1,0:T(8,128)(2,1)} %get-tuple-element.86), channel_id=1, source_target_pairs={{0,3},{1,2},{2,1},{3,0},{4,7},{5,6},{6,5},{7,4},{8,11},{9,10},{10,... | collective-permute-start | bytes 786440 | tf_op jit(solution)/shard_map/ppermute | solution.py:72
  111.4 28.6 %collective-permute-start.19 = (bf16[64,2176]{1,0:T(8,128)(2,1)}, bf16[64,2176]{1,0:T(8,128)(2,1)S(1)}, u32[]{:S(2)}, u32[]{:S(2)}) collective-permute-start(bf16[64,2176]{1,0:T(8,128)(2,1)} %get-tuple-element.88.refs_0_.refs_6_), channel_id=1, source_target_pairs={{0,3},{1,2},{2,1},{3,0},{4,7},{5,6},{6,5},{7,4},{8,11},{9,10},{10,... | collective-permute-start | bytes 835592 | tf_op jit(solution)/shard_map/ppermute | solution.py:72
  113.9 26.2 %collective-permute-start.18 = (bf16[64,2176]{1,0:T(8,128)(2,1)}, bf16[64,2176]{1,0:T(8,128)(2,1)S(1)}, u32[]{:S(2)}, u32[]{:S(2)}) collective-permute-start(bf16[64,2176]{1,0:T(8,128)(2,1)} %get-tuple-element.88.refs_0_.refs_6_), channel_id=1, source_target_pairs={{0,2},{1,3},{2,0},{3,1},{4,6},{5,7},{6,4},{7,5},{8,10},{9,11},{10,... | collective-permute-start | bytes 835592 | tf_op jit(solution)/shard_map/ppermute | solution.py:72
  121.4 21.9 %collective-permute-start.23 = (bf16[128,2176]{1,0:T(8,128)(2,1)}, bf16[128,2176]{1,0:T(8,128)(2,1)S(1)}, u32[]{:S(2)}, u32[]{:S(2)}) collective-permute-start(bf16[128,2176]{1,0:T(8,128)(2,1)} %joins.6.refs_2_.refs_0_), channel_id=1, source_target_pairs={{0,16},{4,20},{8,24},{12,28},{16,0},{20,4},{24,8},{28,12},{1,17},{... | collective-permute-start | bytes 1671176 | tf_op jit(solution)/shard_map/ppermute | solution.py:72
  121.8 23.1 %collective-permute-start.21 = (bf16[128,2176]{1,0:T(8,128)(2,1)}, bf16[128,2176]{1,0:T(8,128)(2,1)S(1)}, u32[]{:S(2)}, u32[]{:S(2)}) collective-permute-start(bf16[128,2176]{1,0:T(8,128)(2,1)} %joins.6.refs_2_.refs_0_), channel_id=1, source_target_pairs={{0,8},{4,12},{8,0},{12,4},{16,24},{20,28},{24,16},{28,20},{1,9},{5... | collective-permute-start | bytes 1671176 | tf_op jit(solution)/shard_map/ppermute | solution.py:72
  143.3 23.1 %collective-permute-start.25 = (bf16[128,2176]{1,0:T(8,128)(2,1)S(1)}, bf16[128,2176]{1,0:T(8,128)(2,1)S(1)}, u32[]{:S(2)}, u32[]{:S(2)}) collective-permute-start(bf16[128,2176]{1,0:T(8,128)(2,1)S(1)} %collective-permute-done.23.refs_4_), channel_id=1, source_target_pairs={{0,8},{4,12},{8,0},{12,4},{16,24},{20,28},{24,16},{28,20},{1,9},{5... | collective-permute-start | bytes 1671176 | tf_op jit(solution)/shard_map/ppermute | solution.py:72
  144.8 21.5 %collective-permute-start.24 = (bf16[128,2176]{1,0:T(8,128)(2,1)S(1)}, bf16[128,2176]{1,0:T(8,128)(2,1)}, u32[]{:S(2)}, u32[]{:S(2)}) collective-permute-start(bf16[128,2176]{1,0:T(8,128)(2,1)S(1)} %collective-permute-done.23.refs_4_), channel_id=1, source_target_pairs={{0,4},{4,0},{8,12},{12,8},{16,20},{20,16},{24,28},{28,24},{1,5},{5... | collective-permute-start | bytes 1671176 | tf_op jit(solution)/shard_map/ppermute | solution.py:72
  145.0 21.9 %collective-permute-start.22 = (bf16[128,2176]{1,0:T(8,128)(2,1)S(1)}, bf16[128,2176]{1,0:T(8,128)(2,1)}, u32[]{:S(2)}, u32[]{:S(2)}) collective-permute-start(bf16[128,2176]{1,0:T(8,128)(2,1)S(1)} %collective-permute-done.21.refs_2_), channel_id=1, source_target_pairs={{0,4},{4,0},{8,12},{12,8},{16,20},{20,16},{24,28},{28,24},{1,5},{5... | collective-permute-start | bytes 1671176 | tf_op jit(solution)/shard_map/ppermute | solution.py:72
  162.0 21.0 %collective-permute-start.32 = (bf16[128,2176]{1,0:T(8,128)(2,1)}, bf16[128,2176]{1,0:T(8,128)(2,1)S(1)}, u32[]{:S(2)}, u32[]{:S(2)}) collective-permute-start(bf16[128,2176]{1,0:T(8,128)(2,1)} %joins.8), channel_id=1, source_target_pairs={{0,16},{4,20},{8,24},{12,28},{16,0},{20,4},{24,8},{28,12},{1,17},{... | collective-permute-start | bytes 1671176 | tf_op jit(solution)/shard_map/ppermute | solution.py:72
  228.2 23.8 %collective-permute-start.39 = (bf16[2,64,2176]{2,1,0:T(8,128)(2,1)}, bf16[2,64,2176]{2,1,0:T(8,128)(2,1)S(1)}, u32[]{:S(2)}, u32[]{:S(2)}) collective-permute-start(bf16[2,64,2176]{2,1,0:T(8,128)(2,1)} %get-tuple-element.105), channel_id=1, source_target_pairs={{0,16},{4,20},{8,24},{12,28},{16,0},{20,4},{24,8},{28,12},{1,17},{... | collective-permute-start | bytes 1671176 | tf_op jit(solution)/shard_map/ppermute | solution.py:72
  229.9 22.1 %collective-permute-start.38 = (bf16[2,64,2176]{2,1,0:T(8,128)(2,1)}, bf16[2,64,2176]{2,1,0:T(8,128)(2,1)S(1)}, u32[]{:S(2)}, u32[]{:S(2)}) collective-permute-start(bf16[2,64,2176]{2,1,0:T(8,128)(2,1)} %get-tuple-element.94.refs_4_), channel_id=1, source_target_pairs={{0,8},{4,12},{8,0},{12,4},{16,24},{20,28},{24,16},{28,20},{1,9},{5... | collective-permute-start | bytes 1671176 | tf_op jit(solution)/shard_map/ppermute | solution.py:72
  234.1 24.0 %collective-permute-start.37 = (bf16[2,64,2176]{2,1,0:T(8,128)(2,1)}, bf16[2,64,2176]{2,1,0:T(8,128)(2,1)S(1)}, u32[]{:S(2)}, u32[]{:S(2)}) collective-permute-start(bf16[2,64,2176]{2,1,0:T(8,128)(2,1)} %get-tuple-element.104), channel_id=1, source_target_pairs={{0,16},{4,20},{8,24},{12,28},{16,0},{20,4},{24,8},{28,12},{1,17},{... | collective-permute-start | bytes 1671176 | tf_op jit(solution)/shard_map/ppermute | solution.py:72
  234.5 23.6 %collective-permute-start.36 = (bf16[2,64,2176]{2,1,0:T(8,128)(2,1)}, bf16[2,64,2176]{2,1,0:T(8,128)(2,1)S(1)}, u32[]{:S(2)}, u32[]{:S(2)}) collective-permute-start(bf16[2,64,2176]{2,1,0:T(8,128)(2,1)} %get-tuple-element.97.refs_5_), channel_id=1, source_target_pairs={{0,8},{4,12},{8,0},{12,4},{16,24},{20,28},{24,16},{28,20},{1,9},{5... | collective-permute-start | bytes 1671176 | tf_op jit(solution)/shard_map/ppermute | solution.py:72
  271.2 23.0 %collective-permute-start.45 = (bf16[64,2176]{1,0:T(8,128)(2,1)}, bf16[64,2176]{1,0:T(8,128)(2,1)S(1)}, u32[]{:S(2)}, u32[]{:S(2)}) collective-permute-start(bf16[64,2176]{1,0:T(8,128)(2,1)} %get-tuple-element.110.refs_8_), channel_id=1, source_target_pairs={{0,2},{1,3},{2,0},{3,1},{4,6},{5,7},{6,4},{7,5},{8,10},{9,11},{10,... | collective-permute-start | bytes 835592 | tf_op jit(solution)/shard_map/ppermute | solution.py:72
  301.4 22.8 %collective-permute-start.48 = (bf16[64,2176]{1,0:T(8,128)(2,1)}, bf16[64,2176]{1,0:T(8,128)(2,1)S(1)}, u32[]{:S(2)}, u32[]{:S(2)}) collective-permute-start(bf16[64,2176]{1,0:T(8,128)(2,1)} %get-tuple-element.119.refs_6_.refs_11_.refs_2_), channel_id=1, source_target_pairs={{0,2},{1,3},{2,0},{3,1},{4,6},{5,7},{6,4},{7,5},{8,10},{9,11},{10,... | collective-permute-start | bytes 835592 | tf_op jit(solution)/shard_map/ppermute | solution.py:72
  301.4 22.8 %collective-permute-start.47 = (bf16[64,2176]{1,0:T(8,128)(2,1)}, bf16[64,2176]{1,0:T(8,128)(2,1)S(1)}, u32[]{:S(2)}, u32[]{:S(2)}) collective-permute-start(bf16[64,2176]{1,0:T(8,128)(2,1)} %get-tuple-element.119.refs_6_.refs_11_.refs_2_), channel_id=1, source_target_pairs={{0,1},{1,0},{2,3},{3,2},{4,5},{5,4},{6,7},{7,6},{8,9},{9,8},{10,11... | collective-permute-start | bytes 835592 | tf_op jit(solution)/shard_map/ppermute | solution.py:72
  363.2 20.3 %collective-permute-start.60 = (bf16[4,256,1536]{2,1,0:T(8,128)(2,1)}, bf16[4,256,1536]{2,1,0:T(8,128)(2,1)S(1)}, u32[]{:S(2)}, u32[]{:S(2)}) collective-permute-start(bf16[4,256,1536]{2,1,0:T(8,128)(2,1)} %get-tuple-element.137), channel_id=1, source_target_pairs={{0,4},{4,0},{8,12},{12,8},{16,20},{20,16},{24,28},{28,24},{1,5},{5... | collective-permute-start | bytes 9437192 | tf_op jit(solution)/shard_map/ppermute | solution.py:72
  368.2 20.1 %collective-permute-start.50 = (bf16[64,2048]{1,0:T(8,128)(2,1)}, bf16[64,2048]{1,0:T(8,128)(2,1)}, u32[]{:S(2)}, u32[]{:S(2)}) collective-permute-start(bf16[64,2048]{1,0:T(8,128)(2,1)} %get-tuple-element.124), channel_id=1, source_target_pairs={{0,1},{1,0},{2,3},{3,2},{4,5},{5,4},{6,7},{7,6},{8,9},{9,8},{10,11... | collective-permute-start | bytes 786440 | tf_op jit(solution)/shard_map/ppermute | solution.py:72
  368.2 28.5 %collective-permute-start.51 = (bf16[64,2048]{1,0:T(8,128)(2,1)}, bf16[64,2048]{1,0:T(8,128)(2,1)}, u32[]{:S(2)}, u32[]{:S(2)}) collective-permute-start(bf16[64,2048]{1,0:T(8,128)(2,1)} %get-tuple-element.125), channel_id=1, source_target_pairs={{0,2},{1,3},{2,0},{3,1},{4,6},{5,7},{6,4},{7,5},{8,10},{9,11},{10,... | collective-permute-start | bytes 786440 | tf_op jit(solution)/shard_map/ppermute | solution.py:72
  370.4 26.3 %collective-permute-start.52 = (bf16[64,2048]{1,0:T(8,128)(2,1)}, bf16[64,2048]{1,0:T(8,128)(2,1)}, u32[]{:S(2)}, u32[]{:S(2)}) collective-permute-start(bf16[64,2048]{1,0:T(8,128)(2,1)} %get-tuple-element.126), channel_id=1, source_target_pairs={{0,3},{1,2},{2,1},{3,0},{4,7},{5,6},{6,5},{7,4},{8,11},{9,10},{10,... | collective-permute-start | bytes 786440 | tf_op jit(solution)/shard_map/ppermute | solution.py:72
  403.8 28.8 %collective-permute-start.65 = (bf16[4,256,640]{2,1,0:T(8,128)(2,1)}, bf16[4,256,640]{2,1,0:T(8,128)(2,1)S(1)}, u32[]{:S(2)}, u32[]{:S(2)}) collective-permute-start(bf16[4,256,640]{2,1,0:T(8,128)(2,1)} %get-tuple-element.144), channel_id=1, source_target_pairs={{0,4},{4,0},{8,12},{12,8},{16,20},{20,16},{24,28},{28,24},{1,5},{5... | collective-permute-start | bytes 3932168 | tf_op jit(solution)/shard_map/ppermute | solution.py:72
  403.8 23.1 %collective-permute-start.62 = (bf16[2,128,1536]{2,1,0:T(8,128)(2,1)}, bf16[2,128,1536]{2,1,0:T(8,128)(2,1)S(1)}, u32[]{:S(2)}, u32[]{:S(2)}) collective-permute-start(bf16[2,128,1536]{2,1,0:T(8,128)(2,1)} %get-tuple-element.139), channel_id=1, source_target_pairs={{0,16},{4,20},{8,24},{12,28},{16,0},{20,4},{24,8},{28,12},{1,17},{... | collective-permute-start | bytes 2359304 | tf_op jit(solution)/shard_map/ppermute | solution.py:72
  405.6 21.4 %collective-permute-start.61 = (bf16[2,128,1536]{2,1,0:T(8,128)(2,1)S(1)}, bf16[2,128,1536]{2,1,0:T(8,128)(2,1)S(1)}, u32[]{:S(2)}, u32[]{:S(2)}) collective-permute-start(bf16[2,128,1536]{2,1,0:T(8,128)(2,1)S(1)} %copy-done.26), channel_id=1, source_target_pairs={{0,8},{4,12},{8,0},{12,4},{16,24},{20,28},{24,16},{28,20},{1,9},{5... | collective-permute-start | bytes 2359304 | tf_op jit(solution)/shard_map/ppermute | solution.py:72
  431.3 25.7 %collective-permute-start.63 = (bf16[128,1536]{1,0:T(8,128)(2,1)}, bf16[128,1536]{1,0:T(8,128)(2,1)S(1)}, u32[]{:S(2)}, u32[]{:S(2)}) collective-permute-start(bf16[128,1536]{1,0:T(8,128)(2,1)} %get-tuple-element.140), channel_id=1, source_target_pairs={{0,16},{4,20},{8,24},{12,28},{16,0},{20,4},{24,8},{28,12},{1,17},{... | collective-permute-start | bytes 1179656 | tf_op jit(solution)/shard_map/ppermute | solution.py:72
  431.5 25.8 %collective-permute-start.64 = (bf16[128,1536]{1,0:T(8,128)(2,1)}, bf16[128,1536]{1,0:T(8,128)(2,1)S(1)}, u32[]{:S(2)}, u32[]{:S(2)}) collective-permute-start(bf16[128,1536]{1,0:T(8,128)(2,1)} %get-tuple-element.141), channel_id=1, source_target_pairs={{0,8},{4,12},{8,0},{12,4},{16,24},{20,28},{24,16},{28,20},{1,9},{5... | collective-permute-start | bytes 1179656 | tf_op jit(solution)/shard_map/ppermute | solution.py:72
  (109 other events, 887.1 us)
Sparse Core Ops, SparseCore 0:
  59.1 56.8 all-gather.1
  276.7 73.0 reduce-scatter.1
